TPU v7x, 256 devices: a whole 4x4x8 slice. The times are simulated.
256 devices in a mesh: seq: 32 (over y, x, core), chan: 8 (over z).
Axes of the slice: x: 4, y: 4, z: 8, core: 2. Of those that a mesh axis runs over, the one named last changes fastest.
Arguments:
- outer_gate: bfloat16 [8192, 4096], P('seq', 'chan'), may hold values from -6 to 6
- inner_gate: bfloat16 [8192, 4096], P('seq', 'chan'), may hold values from -6 to 6
- signal: bfloat16 [8192, 4096], P('seq', 'chan'), may hold values from -6 to 6
- cotangent: bfloat16 [8192, 4096], P('seq', 'chan'), may hold values from -6 to 6
- filters: float32 [8192, 512], P('seq', 'chan'), may hold values from -1.1 to 1.1
Outputs:
- outer_grad: bfloat16 [8192, 4096], P('seq', 'chan')
- inner_grad: bfloat16 [8192, 4096], P('seq', 'chan')
- signal_grad: bfloat16 [8192, 4096], P('seq', 'chan')
- filter_grad: float32 [8192, 512], P('seq', 'chan')
All inputs are finite; a program needn't handle non-finite values.
Results may differ from a plain program's by a relative error of at most 0.0012.
Values sent between devices are 32-bit elements; how exact they have to be, the bound alone decides.
No kernel may reach another device: no remote copies, remote signals or barrier semaphores. Data moves between devices by JAX's collectives and lax.ppermute only.
A program may use at most 128 MiB of HBM per device.

v0:
```python
import math

import jax
import jax.numpy as jnp
import numpy as np
import ml_dtypes
from jax import lax
from jax.experimental import pallas as pl
from jax.experimental.pallas import tpu as pltpu
from jax.sharding import PartitionSpec as P

BF = jnp.bfloat16
F32 = jnp.float32

N = 8192
A = 64
B = 128
ROWS = 40
MEMBERS = 64
VMEM_LIMIT = 40 * 1024 * 1024


def two_parts(table):
    high = table.astype(ml_dtypes.bfloat16)
    low = (table - high.astype(np.float64)).astype(ml_dtypes.bfloat16)
    return high, low


def tables():
    order = np.array([2 * s + h for h in range(2) for s in range(32)])
    k1 = np.arange(A) - 0.25
    angle1 = 2 * np.pi / A * np.outer(k1, order)
    w1 = np.concatenate([np.cos(angle1), -np.sin(angle1)], axis=0)
    high, low = two_parts(w1)
    w1cat = np.concatenate([high, high, low], axis=1)
    v1 = np.concatenate([np.cos(angle1), -np.sin(angle1)], axis=0).T / N
    high, low = two_parts(v1)
    v1cat = np.concatenate([high, high, low], axis=1)
    angle2 = 2 * np.pi / B * np.outer(np.arange(B), np.arange(B))
    c, s = np.cos(angle2), np.sin(angle2)
    w2 = np.block([[c, -s], [s, c]])
    w2h, w2l = two_parts(w2)
    v2h, v2l = two_parts(w2.T)
    angle = 2 * np.pi / N * np.outer(k1, np.arange(B))
    twiddle = np.stack([np.cos(angle), np.sin(angle)]).astype(np.float32)
    return w1cat, w2h, w2l, twiddle, v2h, v2l, v1cat


def split(x):
    high = x.astype(BF)
    return high, (x - high.astype(F32)).astype(BF)


def dot(x, y):
    return jnp.dot(x, y, preferred_element_type=F32)


def first_stage(columns, w1, c, s):
    high, low = split(jnp.concatenate(columns, axis=1))
    out = dot(w1, jnp.concatenate([high, low, high], axis=0))
    pairs = []
    for i in range(len(columns)):
        re = out[:A, i * B : (i + 1) * B]
        im = out[A:, i * B : (i + 1) * B]
        pairs.append((re * c + im * s, im * c - re * s))
    return pairs


def second_stage(pairs, high_table, low_table):
    stacked = jnp.concatenate([jnp.concatenate(p, axis=1) for p in pairs], axis=0)
    high, low = split(stacked)
    return dot(high, high_table) + dot(low, high_table) + dot(high, low_table)


def last_stage(blocks, v1, c, s):
    re, im = [], []
    for block in blocks:
        qr, qi = block[:, :B], block[:, B:]
        re.append(qr * c - qi * s)
        im.append(qr * s + qi * c)
    both = jnp.concatenate([jnp.concatenate(re, axis=1), jnp.concatenate(im, axis=1)], axis=0)
    high, low = split(both)
    return dot(v1, jnp.concatenate([high, low, high], axis=0))


def forward(columns, w1, w2h, w2l, c, s):
    return second_stage(first_stage(columns, w1, c, s), w2h, w2l)


def prep_kernel(outer_ref, inner_ref, signal_ref, cot_ref, filt_ref, send_ref):
    def place(block, first_row, h, cb):
        turned = block.T
        for e in range(2):
            row = first_row + h * 8 + cb * 2 + e
            send_ref[pl.ds(row, MEMBERS, stride=ROWS), :] = turned[e * 64 : (e + 1) * 64]

    for h in range(2):
        rows = slice(h * B, (h + 1) * B)
        for cb in range(4):
            cols = slice(cb * 128, (cb + 1) * 128)
            place(inner_ref[rows, cols].astype(F32) * signal_ref[rows, cols].astype(F32), 0, h, cb)
            place(cot_ref[rows, cols].astype(F32) * outer_ref[rows, cols].astype(F32), 16, h, cb)
        send_ref[pl.ds(32 + h, MEMBERS, stride=ROWS), :] = filt_ref[rows, :].T
    for row in range(34, ROWS):
        send_ref[pl.ds(row, MEMBERS, stride=ROWS), :] = jnp.zeros((MEMBERS, B), F32)


def gather_rows(ref, q, row):
    return jnp.concatenate(
        [ref[pl.ds(q * 32 * ROWS + row + 8 * h, 32, stride=ROWS), :] for h in range(2)], axis=0
    )


def pick_kernel(recv_ref, out_ref):
    for q in range(2):
        for h in range(2):
            block = recv_ref[pl.ds(q * 32 * ROWS + 32 + h, 32, stride=ROWS), :]
            for p in range(4):
                out_ref[p, q, h * 32 : (h + 1) * 32, :] = block


def spectra_kernel(recv_ref, w1_ref, w2h_ref, w2l_ref, tw_ref, v2h_ref, v2l_ref, v1_ref,
                   u_ref, g_ref, fg_ref, prod_ref):
    c, s = tw_ref[0], tw_ref[1]

    def step(f, carry):
        columns = [gather_rows(recv_ref, q, f + base) for base in (0, 16) for q in range(2)]
        spec = forward(columns, w1_ref[...], w2h_ref[...], w2l_ref[...], c, s)
        u_ref[f] = spec[: 2 * A]
        g_ref[f] = spec[2 * A :]
        ur, ui = spec[: 2 * A, :B], spec[: 2 * A, B:]
        gr, gi = spec[2 * A :, :B], spec[2 * A :, B:]
        pr = gr * ur + gi * ui
        pi = gi * ur - gr * ui
        prod_ref[f] = jnp.concatenate([pr[:A] + pr[A:], pi[:A] + pi[A:]], axis=1)
        return carry

    lax.fori_loop(0, 8, step, 0)

    def back(j, carry):
        prod = prod_ref[pl.ds(j * 4, 4)].reshape(4 * A, 2 * B)
        high, low = split(prod)
        mid = dot(high, v2h_ref[...]) + dot(low, v2h_ref[...]) + dot(high, v2l_ref[...])
        out = last_stage([mid[i * A : (i + 1) * A] for i in range(4)], v1_ref[...], c, s)
        for i in range(4):
            fg_ref[j * 2 + i // 2, i % 2] = out[:, i * B : (i + 1) * B]
        return carry

    lax.fori_loop(0, 2, back, 0)


def conv_kernel(filt_ref, u_ref, g_ref, w1_ref, w2h_ref, w2l_ref, tw_ref, v2h_ref, v2l_ref, v1_ref,
                out_ref, spec_ref):
    c, s = tw_ref[0], tw_ref[1]

    def filters(j, carry):
        columns = [filt_ref[j * 2 + i // 2, i % 2] for i in range(4)]
        spec = forward(columns, w1_ref[...], w2h_ref[...], w2l_ref[...], c, s)
        spec_ref[pl.ds(j * 4, 4)] = spec.reshape(4, A, 2 * B)
        return carry

    lax.fori_loop(0, 2, filters, 0)

    def step(f, carry):
        hr, hi = spec_ref[f][:, :B], spec_ref[f][:, B:]
        prods = []
        for q in range(2):
            ur, ui = u_ref[f, q * A : (q + 1) * A, :B], u_ref[f, q * A : (q + 1) * A, B:]
            prods.append((hr * ur - hi * ui, hr * ui + hi * ur))
        for q in range(2):
            gr, gi = g_ref[f, q * A : (q + 1) * A, :B], g_ref[f, q * A : (q + 1) * A, B:]
            prods.append((gr * hr + gi * hi, gi * hr - gr * hi))
        mid = second_stage(prods, v2h_ref[...], v2l_ref[...])
        out = last_stage([mid[i * A : (i + 1) * A] for i in range(4)], v1_ref[...], c, s)
        for i in range(4):
            q, base = i % 2, (i // 2) * 16
            for h in range(2):
                out_ref[pl.ds(q * 32 * ROWS + base + 8 * h + f, 32, stride=ROWS), :] = (
                    out[h * 32 : (h + 1) * 32, i * B : (i + 1) * B]
                )
        return carry

    lax.fori_loop(0, 8, step, 0)
    for row in range(34, ROWS):
        out_ref[pl.ds(row, MEMBERS, stride=ROWS), :] = jnp.zeros((MEMBERS, B), F32)


def place_kernel(fg_ref, base_ref, out_ref):
    out_ref[...] = base_ref[...]
    total = (fg_ref[0] + fg_ref[1]) + (fg_ref[2] + fg_ref[3])
    for q in range(2):
        for h in range(2):
            out_ref[pl.ds(q * 32 * ROWS + 32 + h, 32, stride=ROWS), :] = total[q, h * 32 : (h + 1) * 32]


def post_kernel(recv_ref, inner_ref, signal_ref, cot_ref, og_ref, ig_ref, sg_ref, fg_ref):
    def fetch(first_row, h, cb):
        blocks = [
            recv_ref[pl.ds(first_row + h * 8 + cb * 2 + e, MEMBERS, stride=ROWS), :] for e in range(2)
        ]
        return jnp.concatenate(blocks, axis=0).T

    for h in range(2):
        rows = slice(h * B, (h + 1) * B)
        for cb in range(4):
            cols = slice(cb * 128, (cb + 1) * 128)
            og_ref[rows, cols] = (cot_ref[rows, cols].astype(F32) * fetch(0, h, cb)).astype(BF)
            back = fetch(16, h, cb)
            ig_ref[rows, cols] = (back * signal_ref[rows, cols].astype(F32)).astype(BF)
            sg_ref[rows, cols] = (back * inner_ref[rows, cols].astype(F32)).astype(BF)
        block = recv_ref[pl.ds(32 + h, MEMBERS, stride=ROWS), :]
        fg_ref[rows, :] = block.T * (1.0 / math.sqrt(N))


def call(kernel, out_shapes, name, scratch=(), cost=(0, 0)):
    return pl.pallas_call(
        kernel,
        out_shape=out_shapes,
        scratch_shapes=list(scratch),
        name=name,
        compiler_params=pltpu.CompilerParams(vmem_limit_bytes=VMEM_LIMIT),
        cost_estimate=pl.CostEstimate(flops=cost[0], bytes_accessed=cost[1], transcendentals=0),
    )


def shape(*dims, dtype=F32):
    return jax.ShapeDtypeStruct(dims, dtype)


GROUPS = [[s * 8 + 2 * p + q for q in range(2) for s in range(32)] for p in range(4)]
QUADS = [[0, 2, 4, 6], [1, 3, 5, 7]]


def exchange(x):
    x = x.reshape(MEMBERS, ROWS, B)
    x = lax.all_to_all(x, ("seq", "chan"), 0, 0, axis_index_groups=GROUPS, tiled=True)
    return x.reshape(MEMBERS * ROWS, B)


def quad_exchange(x):
    return lax.all_to_all(x, "chan", 0, 0, axis_index_groups=QUADS, tiled=True)


def body(outer_gate, inner_gate, signal, cotangent, filters):
    consts = [jnp.asarray(t) for t in tables()]
    w1, w2h, w2l, tw, v2h, v2l, v1 = consts
    buffer = shape(MEMBERS * ROWS, B)
    send = call(prep_kernel, buffer, "prep")(outer_gate, inner_gate, signal, cotangent, filters)
    recv = exchange(send)
    picked = call(pick_kernel, shape(4, 2, A, B), "pick")(recv)
    gathered = quad_exchange(picked)
    u, g, fg = call(
        spectra_kernel,
        (shape(8, 2 * A, 2 * B), shape(8, 2 * A, 2 * B), shape(4, 2, A, B)),
        "spectra",
        [pltpu.VMEM((8, A, 2 * B), F32)],
        (2_000_000_000, 4_000_000),
    )(recv, w1, w2h, w2l, tw, v2h, v2l, v1)
    fg_parts = quad_exchange(fg)
    out = call(
        conv_kernel, buffer, "conv", [pltpu.VMEM((8, A, 2 * B), F32)], (2_000_000_000, 4_000_000)
    )(gathered, u, g, w1, w2h, w2l, tw, v2h, v2l, v1)
    back_send = call(place_kernel, buffer, "place")(fg_parts, out)
    landed = exchange(back_send)
    return call(
        post_kernel,
        (shape(256, 512, dtype=BF), shape(256, 512, dtype=BF), shape(256, 512, dtype=BF), shape(256, 64)),
        "post",
    )(landed, inner_gate, signal, cotangent)


def solution(mesh):
    spec = P("seq", "chan")
    return jax.shard_map(
        body, mesh=mesh, in_specs=(spec,) * 5, out_specs=(spec,) * 4, check_vma=False
    )
```

profile of v0, /device:TPU:1, one launch (start us, length us, event | category | flops | bytes accessed | tf_op | source)
XLA Modules:
  0.0 96.2 jit_solution(8397714100060818210)
XLA Ops:
  0.6 0.9 copy.16.filt_ref
  1.6 0.0 copy-start
  1.6 0.9 copy-done
  2.5 0.9 copy-done.2
  3.5 0.9 copy-done.4
  4.4 0.9 copy-done.6
  5.4 0.4 prep.1
  5.8 29.6 %all_to_all.20 = f32[64,40,128]{2,1,0:T(8,128)S(1)} all-to-all(f32[64,40,128]{2,1,0:T(8,128)S(1)} %bitcast.8), channel_id=1, replica_groups={{0,8,16,24,32,40,48,56,64,72,80,88,96,104,112,120,128,136,144,152,160,1..., dimensions={0} | all-to-all | bytes 2621440 | tf_op jit(solution)/shard_map/all_to_all | solution.py:236
  35.4 0.0 copy-start.11
  35.4 0.0 copy-start.12
  35.5 0.0 copy-start.13
  35.5 0.7 pick.1
  36.2 7.3 %all-to-all-start.2 = ((f32[4,2,64,128]{3,2,1,0:T(8,128)}), f32[4,2,64,128]{3,2,1,0:T(8,128)S(1)}, u32[]{:S(2)}, u32[]{:S(2)}) async-start(f32[4,2,64,128]{3,2,1,0:T(8,128)} %pick.1), calls=%async_computation.2 | async-start | bytes 524288 | tf_op jit(solution)/shard_map/all_to_all | solution.py:241
  43.5 0.0 copy-done.7
  43.5 0.0 copy-done.8
  43.5 5.2 %spectra.1 = (f32[8,128,256]{2,1,0:T(8,128)S(1)}, f32[8,128,256]{2,1,0:T(8,128)S(1)}, f32[4,2,64,128]{3,2,1,0:T(8,128)}) custom-call(f32[2560,128]{1,0:T(8,128)S(1)} %bitcast.5, bf16[128,192]{1,0:T(8,128)(2,1)S(1)} %copy-done.12, bf16[256,256]{1,0:T(8,128)(2,1)S(1)} %copy-done.10, bf16[256,256]{1,0:T(8,128)(2,1)S(1)} %copy-done.9, ...), custom_call_target="tpu_custom_call" | custom-call | flops 2000000000 | bytes 4000000 | tf_op jit(solution)/shard_map/spectra/pallas_call | solution.py:252
  48.8 1.0 %copy-done.14 = f32[8,128,256]{2,1,0:T(8,128)} copy-done((f32[8,128,256]{2,1,0:T(8,128)}, f32[8,128,256]{2,1,0:T(8,128)S(1)}, u32[]{:S(2)}) %copy-start.14) | copy-done | bytes 1048600
  49.8 1.0 %copy-done.16 = f32[8,128,256]{2,1,0:T(8,128)} copy-done((f32[8,128,256]{2,1,0:T(8,128)}, f32[8,128,256]{2,1,0:T(8,128)S(1)}, u32[]{:S(2)}) %copy-start.16) | copy-done | bytes 1048600
  50.7 1.0 all-to-all-done.2.filt_ref
  51.7 5.7 %all-to-all-start.1 = ((f32[4,2,64,128]{3,2,1,0:T(8,128)}), f32[4,2,64,128]{3,2,1,0:T(8,128)S(1)}, u32[]{:S(2)}, u32[]{:S(2)}) async-start(f32[4,2,64,128]{3,2,1,0:T(8,128)} %get-tuple-element.7), calls=%async_computation.1 | async-start | bytes 524288 | tf_op jit(solution)/shard_map/all_to_all | solution.py:241
  57.4 1.2 %copy-done.15 = f32[8,128,256]{2,1,0:T(8,128)S(1)} copy-done((f32[8,128,256]{2,1,0:T(8,128)S(1)}, f32[8,128,256]{2,1,0:T(8,128)}, u32[]{:S(2)}) %copy-start.15) | copy-done | bytes 1048600
  58.6 1.2 %copy-done.17 = f32[8,128,256]{2,1,0:T(8,128)S(1)} copy-done((f32[8,128,256]{2,1,0:T(8,128)S(1)}, f32[8,128,256]{2,1,0:T(8,128)}, u32[]{:S(2)}) %copy-start.17) | copy-done | bytes 1048600
  59.8 5.2 %conv.1.base_ref = f32[2560,128]{1,0:T(8,128)S(1)} custom-call(f32[4,2,64,128]{3,2,1,0:T(8,128)S(1)} %all-to-all-done.2.filt_ref, f32[8,128,256]{2,1,0:T(8,128)S(1)} %copy-done.15, f32[8,128,256]{2,1,0:T(8,128)S(1)} %copy-done.17, bf16[128,192]{1,0:T(8,128)(2,1)S(1)} %copy-done.12, bf16[256,256]{1,0:T(8,128)(2,1)S(1)} %copy-done.10, ...), custom_call_target="tpu_custom_call" | custom-call | flops 2000000000 | bytes 4000000 | tf_op jit(solution)/shard_map/conv/pallas_call | solution.py:260
  65.0 0.7 all-to-all-done.1.fg_ref
  65.7 0.1 place.1
  65.8 0.0 copy-start.1
  65.8 0.0 copy-start.3
  65.9 0.0 copy-start.5
  65.9 28.4 %all_to_all.21 = f32[64,40,128]{2,1,0:T(8,128)S(1)} all-to-all(f32[64,40,128]{2,1,0:T(8,128)S(1)} %bitcast.7), channel_id=1, replica_groups={{0,8,16,24,32,40,48,56,64,72,80,88,96,104,112,120,128,136,144,152,160,1..., dimensions={0} | all-to-all | bytes 2621440 | tf_op jit(solution)/shard_map/all_to_all | solution.py:236
  94.3 0.0 copy-done.3
  94.3 1.2 %post.1 = (bf16[256,512]{1,0:T(8,128)(2,1)}, bf16[256,512]{1,0:T(8,128)(2,1)}, bf16[256,512]{1,0:T(8,128)(2,1)}, f32[256,64]{1,0:T(8,128)S(1)}) custom-call(f32[2560,128]{1,0:T(8,128)S(1)} %bitcast.6, bf16[256,512]{1,0:T(8,128)(2,1)S(1)} %copy-done.1, bf16[256,512]{1,0:T(8,128)(2,1)S(1)} %copy-done.3, bf16[256,512]{1,0:T(8,128)(2,1)S(1)} %copy-done.5), custom_call_target="tpu_custom_call" | custom-call | tf_op jit(solution)/shard_map/post/pallas_call | solution.py:265
  95.5 0.7 copy.17
  (18 shorter events, 0.0 us)
Async XLA Ops:
  1.6 1.0 copy-start
  2.5 0.9 copy-start.2
  3.5 0.9 copy-start.4
  4.4 0.9 copy-start.6
  35.4 8.1 %copy-start.7 = (bf16[256,256]{1,0:T(8,128)(2,1)S(1)}, bf16[256,256]{1,0:T(8,128)(2,1)}, u32[]{:S(2)}) copy-start(bf16[256,256]{1,0:T(8,128)(2,1)} %constant.19.clone.v2l_ref) | copy-start | bytes 393220
  35.4 8.1 %copy-start.8 = (bf16[256,256]{1,0:T(8,128)(2,1)S(1)}, bf16[256,256]{1,0:T(8,128)(2,1)}, u32[]{:S(2)}) copy-start(bf16[256,256]{1,0:T(8,128)(2,1)} %constant.18.clone.v2h_ref) | copy-start | bytes 393220
  35.4 8.1 %copy-start.9 = (bf16[256,256]{1,0:T(8,128)(2,1)S(1)}, bf16[256,256]{1,0:T(8,128)(2,1)}, u32[]{:S(2)}) copy-start(bf16[256,256]{1,0:T(8,128)(2,1)} %constant.16.clone.w2l_ref) | copy-start | bytes 393220
  35.4 8.1 %copy-start.10 = (bf16[256,256]{1,0:T(8,128)(2,1)S(1)}, bf16[256,256]{1,0:T(8,128)(2,1)}, u32[]{:S(2)}) copy-start(bf16[256,256]{1,0:T(8,128)(2,1)} %constant.15.clone.w2h_ref) | copy-start | bytes 393220
  35.4 8.1 %copy-start.11 = (f32[2,64,128]{2,1,0:T(8,128)S(1)}, f32[2,64,128]{2,1,0:T(8,128)}, u32[]{:S(2)}) copy-start(f32[2,64,128]{2,1,0:T(8,128)} %constant.17.clone.tw_ref) | copy-start | bytes 196612
  35.4 8.1 %copy-start.12 = (bf16[128,192]{1,0:T(8,128)(2,1)S(1)}, bf16[128,192]{1,0:T(8,128)(2,1)}, u32[]{:S(2)}) copy-start(bf16[128,192]{1,0:T(8,128)(2,1)} %constant.14.clone.w1_ref) | copy-start | bytes 147460
  35.5 8.1 %copy-start.13 = (bf16[64,384]{1,0:T(8,128)(2,1)S(1)}, bf16[64,384]{1,0:T(8,128)(2,1)}, u32[]{:S(2)}) copy-start(bf16[64,384]{1,0:T(8,128)(2,1)} %constant.20.clone.v1_ref) | copy-start | bytes 147460
  36.2 15.5 %all-to-all-start.2 = ((f32[4,2,64,128]{3,2,1,0:T(8,128)}), f32[4,2,64,128]{3,2,1,0:T(8,128)S(1)}, u32[]{:S(2)}, u32[]{:S(2)}) async-start(f32[4,2,64,128]{3,2,1,0:T(8,128)} %pick.1), calls=%async_computation.2 | async-start | bytes 524288 | tf_op jit(solution)/shard_map/all_to_all | solution.py:241
  48.8 1.0 %copy-start.14 = (f32[8,128,256]{2,1,0:T(8,128)}, f32[8,128,256]{2,1,0:T(8,128)S(1)}, u32[]{:S(2)}) copy-start(f32[8,128,256]{2,1,0:T(8,128)S(1)} %get-tuple-element.8.u_ref) | copy-start | bytes 3145732
  49.8 1.0 %copy-start.16 = (f32[8,128,256]{2,1,0:T(8,128)}, f32[8,128,256]{2,1,0:T(8,128)S(1)}, u32[]{:S(2)}) copy-start(f32[8,128,256]{2,1,0:T(8,128)S(1)} %get-tuple-element.9.g_ref) | copy-start | bytes 3145732
  51.7 14.0 %all-to-all-start.1 = ((f32[4,2,64,128]{3,2,1,0:T(8,128)}), f32[4,2,64,128]{3,2,1,0:T(8,128)S(1)}, u32[]{:S(2)}, u32[]{:S(2)}) async-start(f32[4,2,64,128]{3,2,1,0:T(8,128)} %get-tuple-element.7), calls=%async_computation.1 | async-start | bytes 524288 | tf_op jit(solution)/shard_map/all_to_all | solution.py:241
  57.4 1.2 %copy-start.15 = (f32[8,128,256]{2,1,0:T(8,128)S(1)}, f32[8,128,256]{2,1,0:T(8,128)}, u32[]{:S(2)}) copy-start(f32[8,128,256]{2,1,0:T(8,128)} %copy-done.14) | copy-start | bytes 3145732
  58.6 1.2 %copy-start.17 = (f32[8,128,256]{2,1,0:T(8,128)S(1)}, f32[8,128,256]{2,1,0:T(8,128)}, u32[]{:S(2)}) copy-start(f32[8,128,256]{2,1,0:T(8,128)} %copy-done.16) | copy-start | bytes 3145732
  65.8 28.5 %copy-start.1 = (bf16[256,512]{1,0:T(8,128)(2,1)S(1)}, bf16[256,512]{1,0:T(8,128)(2,1)}, u32[]{:S(2)}) copy-start(bf16[256,512]{1,0:T(8,128)(2,1)} %inner_ref.3) | copy-start | bytes 786436
  65.8 28.4 %copy-start.3 = (bf16[256,512]{1,0:T(8,128)(2,1)S(1)}, bf16[256,512]{1,0:T(8,128)(2,1)}, u32[]{:S(2)}) copy-start(bf16[256,512]{1,0:T(8,128)(2,1)} %signal_ref.3) | copy-start | bytes 786436
  65.9 28.4 %copy-start.5 = (bf16[256,512]{1,0:T(8,128)(2,1)S(1)}, bf16[256,512]{1,0:T(8,128)(2,1)}, u32[]{:S(2)}) copy-start(bf16[256,512]{1,0:T(8,128)(2,1)} %cot_ref.3) | copy-start | bytes 786436
where the time goes:
time: 96.8 us; the launch traced here: 96.2 us
  blocking collectives  58.1 us (60%)
  starting transfers between devices  13 us (13%)
  Pallas kernels  12.9 us (13%)
  local copies, waits for them, and re-layouts  9.9 us (10%)
  waiting for transfers between devices  1.65 us (2%)
    all_to_all x2, blocking collectives, exchange(): lax.all_to_all(x, ('seq', 'chan'), 0, 0, axis_index_groups=GROUPS, tiled=...  58.1 us
    all_to_all x2, starting transfers between devices, quad_exchange(): return lax.all_to_all(x, 'chan', 0, 0, axis_index_groups=QUADS, tiled=True)  13 us
    unnamed x37, local copies, waits for them, and re-layouts  9.19 us
    pallas_call x1, Pallas kernels, body(): call(spectra_kernel, (shape(8, 2 * A, 2 * B), shape(8, 2 * A, 2 * B), sha...  5.24 us
    pallas_call x1, Pallas kernels, body(): call(conv_kernel, buffer, 'conv', [pltpu.VMEM((8, A, 2 * B), F32)], (2000...  5.2 us
  transfers between devices with their start and end apart: 2, of which 2 were waited for; matrix products, arithmetic and copies ran while one was open for 0% of the time, Pallas kernels for 11%

commit v1 on v0

--- a/solution.py
+++ b/solution.py
@@ -15,9 +15,11 @@
 N = 8192
 A = 64
 B = 128
+SHARDS = 32
+MEMBERS = 64
 ROWS = 40
-MEMBERS = 64
-VMEM_LIMIT = 40 * 1024 * 1024
+SCATTER = np.random.RandomState(0).permutation(SHARDS)
+VMEM_LIMIT = 16 * 1024 * 1024
 
 
 def two_parts(table):
@@ -27,7 +29,7 @@
 
 
 def tables():
-    order = np.array([2 * s + h for h in range(2) for s in range(32)])
+    order = np.array([2 * s + h for h in range(2) for s in SCATTER])
     k1 = np.arange(A) - 0.25
     angle1 = 2 * np.pi / A * np.outer(k1, order)
     w1 = np.concatenate([np.cos(angle1), -np.sin(angle1)], axis=0)
@@ -87,44 +89,76 @@
     return second_stage(first_stage(columns, w1, c, s), w2h, w2l)
 
 
-def prep_kernel(outer_ref, inner_ref, signal_ref, cot_ref, filt_ref, send_ref):
+def prep_kernel(outer_hbm, inner_hbm, signal_hbm, cot_hbm, filt_hbm, send_ref,
+                outer_ref, inner_ref, signal_ref, cot_ref, filt_ref, sems):
+    def load(i, from_ref, to_ref, rows):
+        copy = pltpu.make_async_copy(from_ref.at[rows], to_ref.at[rows], sems.at[i])
+        copy.start()
+        return copy
+
+    halves = [pl.ds(0, B), pl.ds(B, B)]
+    pairs = [(inner_hbm, inner_ref), (signal_hbm, signal_ref), (cot_hbm, cot_ref), (outer_hbm, outer_ref)]
+    copies = [load(i * 4 + j, *pair, rows) for i, rows in enumerate(halves) for j, pair in enumerate(pairs)]
+    last = load(8, filt_hbm, filt_ref, pl.ds(0, 64))
+
     def place(block, first_row, h, cb):
         turned = block.T
         for e in range(2):
             row = first_row + h * 8 + cb * 2 + e
             send_ref[pl.ds(row, MEMBERS, stride=ROWS), :] = turned[e * 64 : (e + 1) * 64]
 
+    for row in range(34, ROWS):
+        send_ref[pl.ds(row, MEMBERS, stride=ROWS), :] = jnp.zeros((MEMBERS, B), F32)
     for h in range(2):
         rows = slice(h * B, (h + 1) * B)
+        for copy in copies[h * 4 : h * 4 + 4]:
+            copy.wait()
         for cb in range(4):
             cols = slice(cb * 128, (cb + 1) * 128)
             place(inner_ref[rows, cols].astype(F32) * signal_ref[rows, cols].astype(F32), 0, h, cb)
             place(cot_ref[rows, cols].astype(F32) * outer_ref[rows, cols].astype(F32), 16, h, cb)
-        send_ref[pl.ds(32 + h, MEMBERS, stride=ROWS), :] = filt_ref[rows, :].T
-    for row in range(34, ROWS):
-        send_ref[pl.ds(row, MEMBERS, stride=ROWS), :] = jnp.zeros((MEMBERS, B), F32)
-
-
-def gather_rows(ref, q, row):
-    return jnp.concatenate(
-        [ref[pl.ds(q * 32 * ROWS + row + 8 * h, 32, stride=ROWS), :] for h in range(2)], axis=0
-    )
+    last.wait()
+    for h in range(2):
+        send_ref[pl.ds(32 + h, MEMBERS, stride=ROWS), :] = filt_ref[:, h * B : (h + 1) * B]
+
+
+def partners():
+    pair = lax.axis_index("chan") // 2
+    beside = pair + 1 - 2 * lax.rem(pair, 2)
+    return [pair, beside, lax.rem(pair + 2, 4), lax.rem(beside + 2, 4)]
 
 
 def pick_kernel(recv_ref, out_ref):
     for q in range(2):
-        for h in range(2):
-            block = recv_ref[pl.ds(q * 32 * ROWS + 32 + h, 32, stride=ROWS), :]
-            for p in range(4):
-                out_ref[p, q, h * 32 : (h + 1) * 32, :] = block
+        out_ref[q] = gather_rows(recv_ref, q, 32, 1)
+
+
+def filter_kernel(f0_ref, f1_ref, f2_ref, f3_ref, w1_ref, w2h_ref, w2l_ref, tw_ref, spec_ref):
+    c, s = tw_ref[0], tw_ref[1]
+    refs = (f0_ref, f1_ref, f2_ref, f3_ref)
+    owners = partners()
+    for k in range(0, 4, 2):
+        columns = [refs[k + j][q] for j in range(2) for q in range(2)]
+        spec = forward(columns, w1_ref[...], w2h_ref[...], w2l_ref[...], c, s)
+        for j in range(2):
+            for q in range(2):
+                part = (j * 2 + q) * A
+                spec_ref[owners[k + j] * 2 + q] = spec[part : part + A]
+
+
+def gather_rows(ref, q, row, step):
+    return jnp.concatenate(
+        [ref[pl.ds(q * 32 * ROWS + row + step * h, 32, stride=ROWS), :] for h in range(2)], axis=0
+    )
 
 
 def spectra_kernel(recv_ref, w1_ref, w2h_ref, w2l_ref, tw_ref, v2h_ref, v2l_ref, v1_ref,
-                   u_ref, g_ref, fg_ref, prod_ref):
+                   u_ref, g_ref, fg0_ref, fg1_ref, fg2_ref, fg3_ref, prod_ref):
+    fg_refs = (fg0_ref, fg1_ref, fg2_ref, fg3_ref)
     c, s = tw_ref[0], tw_ref[1]
 
     def step(f, carry):
-        columns = [gather_rows(recv_ref, q, f + base) for base in (0, 16) for q in range(2)]
+        columns = [gather_rows(recv_ref, q, f + base, 8) for base in (0, 16) for q in range(2)]
         spec = forward(columns, w1_ref[...], w2h_ref[...], w2l_ref[...], c, s)
         u_ref[f] = spec[: 2 * A]
         g_ref[f] = spec[2 * A :]
@@ -137,29 +171,20 @@
 
     lax.fori_loop(0, 8, step, 0)
 
-    def back(j, carry):
-        prod = prod_ref[pl.ds(j * 4, 4)].reshape(4 * A, 2 * B)
+    owners = partners()
+    for k in (2, 0):
+        prod = jnp.concatenate(
+            [prod_ref[owners[k + j] * 2 + q] for j in range(2) for q in range(2)], axis=0
+        )
         high, low = split(prod)
         mid = dot(high, v2h_ref[...]) + dot(low, v2h_ref[...]) + dot(high, v2l_ref[...])
         out = last_stage([mid[i * A : (i + 1) * A] for i in range(4)], v1_ref[...], c, s)
         for i in range(4):
-            fg_ref[j * 2 + i // 2, i % 2] = out[:, i * B : (i + 1) * B]
-        return carry
-
-    lax.fori_loop(0, 2, back, 0)
-
-
-def conv_kernel(filt_ref, u_ref, g_ref, w1_ref, w2h_ref, w2l_ref, tw_ref, v2h_ref, v2l_ref, v1_ref,
-                out_ref, spec_ref):
+            fg_refs[k + i // 2][i % 2] = out[:, i * B : (i + 1) * B]
+
+
+def conv_kernel(spec_ref, u_ref, g_ref, tw_ref, v2h_ref, v2l_ref, v1_ref, out_ref):
     c, s = tw_ref[0], tw_ref[1]
-
-    def filters(j, carry):
-        columns = [filt_ref[j * 2 + i // 2, i % 2] for i in range(4)]
-        spec = forward(columns, w1_ref[...], w2h_ref[...], w2l_ref[...], c, s)
-        spec_ref[pl.ds(j * 4, 4)] = spec.reshape(4, A, 2 * B)
-        return carry
-
-    lax.fori_loop(0, 2, filters, 0)
 
     def step(f, carry):
         hr, hi = spec_ref[f][:, :B], spec_ref[f][:, B:]
@@ -185,9 +210,8 @@
         out_ref[pl.ds(row, MEMBERS, stride=ROWS), :] = jnp.zeros((MEMBERS, B), F32)
 
 
-def place_kernel(fg_ref, base_ref, out_ref):
-    out_ref[...] = base_ref[...]
-    total = (fg_ref[0] + fg_ref[1]) + (fg_ref[2] + fg_ref[3])
+def place_kernel(fg0_ref, fg1_ref, fg2_ref, fg3_ref, base_ref, out_ref):
+    total = (fg0_ref[...] + fg1_ref[...]) + (fg2_ref[...] + fg3_ref[...])
     for q in range(2):
         for h in range(2):
             out_ref[pl.ds(q * 32 * ROWS + 32 + h, 32, stride=ROWS), :] = total[q, h * 32 : (h + 1) * 32]
@@ -209,15 +233,17 @@
             ig_ref[rows, cols] = (back * signal_ref[rows, cols].astype(F32)).astype(BF)
             sg_ref[rows, cols] = (back * inner_ref[rows, cols].astype(F32)).astype(BF)
         block = recv_ref[pl.ds(32 + h, MEMBERS, stride=ROWS), :]
-        fg_ref[rows, :] = block.T * (1.0 / math.sqrt(N))
-
-
-def call(kernel, out_shapes, name, scratch=(), cost=(0, 0)):
+        fg_ref[:, rows] = block * (1.0 / math.sqrt(N))
+
+
+def call(kernel, out_shapes, name, scratch=(), cost=(0, 0), aliases=None, ins=None):
     return pl.pallas_call(
         kernel,
         out_shape=out_shapes,
+        in_specs=pl.no_block_spec if ins is None else ins,
         scratch_shapes=list(scratch),
         name=name,
+        input_output_aliases=aliases or {},
         compiler_params=pltpu.CompilerParams(vmem_limit_bytes=VMEM_LIMIT),
         cost_estimate=pl.CostEstimate(flops=cost[0], bytes_accessed=cost[1], transcendentals=0),
     )
@@ -227,46 +253,57 @@
     return jax.ShapeDtypeStruct(dims, dtype)
 
 
-GROUPS = [[s * 8 + 2 * p + q for q in range(2) for s in range(32)] for p in range(4)]
-QUADS = [[0, 2, 4, 6], [1, 3, 5, 7]]
+PAIRS = [[s * 8 + 2 * p + q for q in range(2) for s in SCATTER.tolist()] for p in range(4)]
 
 
 def exchange(x):
     x = x.reshape(MEMBERS, ROWS, B)
-    x = lax.all_to_all(x, ("seq", "chan"), 0, 0, axis_index_groups=GROUPS, tiled=True)
+    x = lax.all_to_all(x, ("seq", "chan"), 0, 0, axis_index_groups=PAIRS, tiled=True)
     return x.reshape(MEMBERS * ROWS, B)
 
 
-def quad_exchange(x):
-    return lax.all_to_all(x, "chan", 0, 0, axis_index_groups=QUADS, tiled=True)
+def swap(x, distance):
+    return lax.ppermute(x, "chan", [(z, z ^ distance) for z in range(8)])
 
 
 def body(outer_gate, inner_gate, signal, cotangent, filters):
-    consts = [jnp.asarray(t) for t in tables()]
-    w1, w2h, w2l, tw, v2h, v2l, v1 = consts
-    buffer = shape(MEMBERS * ROWS, B)
-    send = call(prep_kernel, buffer, "prep")(outer_gate, inner_gate, signal, cotangent, filters)
+    w1, w2h, w2l, tw, v2h, v2l, v1 = [jnp.asarray(t) for t in tables()]
+    buffer, spectra = shape(MEMBERS * ROWS, B), shape(8, A, 2 * B)
+    two = shape(2, A, B)
+    gate = pltpu.VMEM((256, 512), BF)
+    send = call(
+        prep_kernel, buffer, "prep",
+        [gate, gate, gate, gate, pltpu.VMEM((64, 256), F32), pltpu.SemaphoreType.DMA((9,))],
+        ins=[pl.BlockSpec(memory_space=pltpu.HBM)] * 5,
+    )(*[
+        pltpu.with_memory_space_constraint(x, pltpu.HBM)
+        for x in (outer_gate, inner_gate, signal, cotangent, filters.T)
+    ])
     recv = exchange(send)
-    picked = call(pick_kernel, shape(4, 2, A, B), "pick")(recv)
-    gathered = quad_exchange(picked)
-    u, g, fg = call(
+    own = call(pick_kernel, two, "pick")(recv)
+    f2, f1, f3 = [swap(own, d) for d in (4, 2, 6)]
+    u, g, fg0, fg1, fg2, fg3 = call(
         spectra_kernel,
-        (shape(8, 2 * A, 2 * B), shape(8, 2 * A, 2 * B), shape(4, 2, A, B)),
+        (shape(8, 2 * A, 2 * B), shape(8, 2 * A, 2 * B), two, two, two, two),
         "spectra",
         [pltpu.VMEM((8, A, 2 * B), F32)],
         (2_000_000_000, 4_000_000),
     )(recv, w1, w2h, w2l, tw, v2h, v2l, v1)
-    fg_parts = quad_exchange(fg)
-    out = call(
-        conv_kernel, buffer, "conv", [pltpu.VMEM((8, A, 2 * B), F32)], (2_000_000_000, 4_000_000)
-    )(gathered, u, g, w1, w2h, w2l, tw, v2h, v2l, v1)
-    back_send = call(place_kernel, buffer, "place")(fg_parts, out)
+    fg2, fg1, fg3 = [swap(x, d) for x, d in ((fg2, 4), (fg1, 2), (fg3, 6))]
+    spec = call(filter_kernel, spectra, "filters", cost=(500_000_000, 1_000_000))(
+        own, f1, f2, f3, w1, w2h, w2l, tw
+    )
+    out = call(conv_kernel, buffer, "conv", cost=(2_000_000_000, 4_000_000))(
+        spec, u, g, tw, v2h, v2l, v1
+    )
+    back_send = call(place_kernel, buffer, "place", aliases={4: 0})(fg0, fg1, fg2, fg3, out)
     landed = exchange(back_send)
-    return call(
+    *grads, fg = call(
         post_kernel,
-        (shape(256, 512, dtype=BF), shape(256, 512, dtype=BF), shape(256, 512, dtype=BF), shape(256, 64)),
+        (shape(256, 512, dtype=BF), shape(256, 512, dtype=BF), shape(256, 512, dtype=BF), shape(64, 256)),
         "post",
     )(landed, inner_gate, signal, cotangent)
+    return (*grads, fg.T)
 
 
 def solution(mesh):

time: 96.8 us -> 83.6 us (0.86)
  local copies, waits for them, and re-layouts: 9.9 us -> 0.05 us
  blocking collectives: 58.1 us -> 56.4 us
    ppermute x0 -> x6, starting transfers between devices: none -> 13 us  [swap(): return lax.ppermute(x, 'chan', [(z, z ^ distance) for z in range(8)])]
    all_to_all x2 -> x0, starting transfers between devices: 13 us -> none  [quad_exchange(): return lax.all_to_all(x, 'chan', 0, 0, axis_index_groups=QUADS, tiled=True)]
    unnamed x37 -> x20, local copies, waits for them, and re-layouts: 9.19 us -> 0.05 us
    all_to_all x2, blocking collectives: 58.1 us -> 56.4 us  [exchange(): lax.all_to_all(x, ('seq', 'chan'), 0, 0, axis_index_groups=PAIRS, tiled=T...]
    all_to_all x2 -> x0, waiting for transfers between devices: 1.65 us -> none  [quad_exchange(): return lax.all_to_all(x, 'chan', 0, 0, axis_index_groups=QUADS, tiled=True)]
    pallas_call x5 -> x6, Pallas kernels: 11.7 us -> 11 us  [the longest x1 4.42 us: body(): call(spectra_kernel, (shape(8, 2 * A, 2 * B), shape(8, 2 * A, 2 * B), two...]
  transfers between devices with their start and end apart: 2 -> 6, of which waited for: 2 -> 1; matrix products, arithmetic and copies ran while one was open for 0% -> 0% of each run, Pallas kernels for 11% -> 11%
where the time goes in v1:
time: 83.6 us; the launch traced here: 83.4 us
  blocking collectives  56.4 us (67%)
  starting transfers between devices  13 us (16%)
  Pallas kernels  12.3 us (15%)
  waiting for transfers between devices  0.9 us (1%)
    all_to_all x2, blocking collectives, exchange(): lax.all_to_all(x, ('seq', 'chan'), 0, 0, axis_index_groups=PAIRS, tiled=T...  56.4 us
    ppermute x6, starting transfers between devices, swap(): return lax.ppermute(x, 'chan', [(z, z ^ distance) for z in range(8)])  13 us
    pallas_call x1, Pallas kernels, body(): call(spectra_kernel, (shape(8, 2 * A, 2 * B), shape(8, 2 * A, 2 * B), two...  4.42 us
    pallas_call x1, Pallas kernels, body(): call(conv_kernel, buffer, 'conv', cost=(2000000000, 4000000))  4.35 us
  transfers between devices with their start and end apart: 6, of which 1 were waited for; matrix products, arithmetic and copies ran while one was open for 0% of the time, Pallas kernels for 11%

profile of v1, /device:TPU:1, one launch (start us, length us, event | category | flops | bytes accessed | tf_op | source)
XLA Modules:
  0.0 83.4 jit_solution(8103865873461594632)
XLA Ops:
  0.6 1.6 %prep.1 = f32[2560,128]{1,0:T(8,128)S(1)} custom-call(bf16[256,512]{1,0:T(8,128)(2,1)} %outer_hbm.1, bf16[256,512]{1,0:T(8,128)(2,1)} %inner_ref.1, bf16[256,512]{1,0:T(8,128)(2,1)} %signal_ref.1, bf16[256,512]{1,0:T(8,128)(2,1)} %cot_ref.1, f32[64,256]{1,0:T(8,128)} %bitcast.11), custom_call_target="tpu_custom_call" | custom-call | tf_op jit(solution)/shard_map/prep/pallas_call | solution.py:274
  2.3 29.0 %all_to_all.10 = f32[64,40,128]{2,1,0:T(8,128)S(1)} all-to-all(f32[64,40,128]{2,1,0:T(8,128)S(1)} %bitcast.10), channel_id=1, replica_groups={{88,176,80,16,128,112,224,208,160,104,192,40,136,64,240,200,184,8,248,4..., dimensions={0} | all-to-all | bytes 2621440 | tf_op jit(solution)/shard_map/all_to_all | solution.py:261
  31.3 0.0 copy-start.7
  31.3 0.0 copy-start.8
  31.4 0.0 copy-start.9
  31.4 3.1 %collective-permute-start.3 = (f32[2,64,128]{2,1,0:T(8,128)S(1)}, f32[2,64,128]{2,1,0:T(8,128)S(1)}, u32[]{:S(2)}, u32[]{:S(2)}) collective-permute-start(f32[2,64,128]{2,1,0:T(8,128)S(1)} %pick.1.f0_ref), channel_id=1, source_target_pairs={{0,2},{1,3},{2,0},{3,1},{4,6},{5,7},{6,4},{7,5},{8,10},{9,11},{10,... | collective-permute-start | bytes 196616 | tf_op jit(solution)/shard_map/ppermute | solution.py:266
  34.5 4.2 %collective-permute-start.4 = (f32[2,64,128]{2,1,0:T(8,128)S(1)}, f32[2,64,128]{2,1,0:T(8,128)S(1)}, u32[]{:S(2)}, u32[]{:S(2)}) collective-permute-start(f32[2,64,128]{2,1,0:T(8,128)S(1)} %pick.1.f0_ref), channel_id=1, source_target_pairs={{0,4},{1,5},{2,6},{3,7},{4,0},{5,1},{6,2},{7,3},{8,12},{9,13},{10,... | collective-permute-start | bytes 196616 | tf_op jit(solution)/shard_map/ppermute | solution.py:266
  38.7 0.0 collective-permute-start.5
  38.7 0.0 copy-done.3
  38.7 0.0 copy-done.4
  38.7 0.0 copy-done.5
  38.7 0.0 copy-done.6
  38.7 0.0 copy-done.7
  38.7 0.0 copy-done.8
  38.7 4.4 %spectra.1 = (f32[8,128,256]{2,1,0:T(8,128)S(1)}, f32[8,128,256]{2,1,0:T(8,128)S(1)}, f32[2,64,128]{2,1,0:T(8,128)S(1)}, f32[2,64,128]{2,1,0:T(8,128)S(1)}, f32[...) custom-call(f32[2560,128]{1,0:T(8,128)S(1)} %bitcast.8, bf16[128,192]{1,0:T(8,128)(2,1)S(1)} %copy-done.7, ...), custom_call_target="tpu_custom_call" | custom-call | flops 2000000000 | bytes 4000000 | tf_op jit(solution)/shard_map/spectra/pallas_call | solution.py:285
  43.2 1.5 %collective-permute-start = (f32[2,64,128]{2,1,0:T(8,128)S(1)}, f32[2,64,128]{2,1,0:T(8,128)S(1)}, u32[]{:S(2)}, u32[]{:S(2)}) collective-permute-start(f32[2,64,128]{2,1,0:T(8,128)S(1)} %get-tuple-element.15), channel_id=1, source_target_pairs={{0,2},{1,3},{2,0},{3,1},{4,6},{5,7},{6,4},{7,5},{8,10},{9,11},{10,... | collective-permute-start | bytes 196616 | tf_op jit(solution)/shard_map/ppermute | solution.py:266
  44.7 4.2 %collective-permute-start.1 = (f32[2,64,128]{2,1,0:T(8,128)S(1)}, f32[2,64,128]{2,1,0:T(8,128)S(1)}, u32[]{:S(2)}, u32[]{:S(2)}) collective-permute-start(f32[2,64,128]{2,1,0:T(8,128)S(1)} %get-tuple-element.16), channel_id=1, source_target_pairs={{0,4},{1,5},{2,6},{3,7},{4,0},{5,1},{6,2},{7,3},{8,12},{9,13},{10,... | collective-permute-start | bytes 196616 | tf_op jit(solution)/shard_map/ppermute | solution.py:266
  48.9 0.0 collective-permute-done.3.f1_ref
  48.9 0.0 collective-permute-start.2
  48.9 0.0 collective-permute-done.4.f2_ref
  48.9 0.0 collective-permute-done.5.f3_ref
  48.9 0.6 filters.1.spec_ref
  49.5 4.3 %conv.1.base_ref = f32[2560,128]{1,0:T(8,128)S(1)} custom-call(f32[8,64,256]{2,1,0:T(8,128)S(1)} %filters.1.spec_ref, f32[8,128,256]{2,1,0:T(8,128)S(1)} %get-tuple-element.18.u_ref, f32[8,128,256]{2,1,0:T(8,128)S(1)} %get-tuple-element.19.g_ref, f32[2,64,128]{2,1,0:T(8,128)S(1)} %copy-done.8, bf16[256,256]{1,0:T(8,128)(2,1)S(1)} %copy-done.3, ...), custom_call_target="tpu_custom_call" | custom-call | flops 2000000000 | bytes 4000000 | tf_op jit(solution)/shard_map/conv/pallas_call | solution.py:296
  53.9 0.0 collective-permute-done.fg1_ref
  53.9 0.0 collective-permute-done.1.fg2_ref
  53.9 0.9 %collective-permute-done.2.fg3_ref = f32[2,64,128]{2,1,0:T(8,128)S(1)} collective-permute-done((f32[2,64,128]{2,1,0:T(8,128)S(1)}, f32[2,64,128]{2,1,0:T(8,128)S(1)}, u32[]{:S(2)}, u32[]{:S(2)}) %collective-permute-start.2) | collective-permute-done | bytes 65568 | tf_op jit(solution)/shard_map/ppermute | solution.py:266
  54.8 0.0 copy-start
  54.8 0.0 copy-start.1
  54.8 0.0 copy-start.2
  54.8 27.3 %all_to_all.11 = f32[64,40,128]{2,1,0:T(8,128)S(1)} all-to-all(f32[64,40,128]{2,1,0:T(8,128)S(1)} %bitcast.6), channel_id=1, replica_groups={{88,176,80,16,128,112,224,208,160,104,192,40,136,64,240,200,184,8,248,4..., dimensions={0} | all-to-all | bytes 2621440 | tf_op jit(solution)/shard_map/all_to_all | solution.py:261
  82.2 0.0 copy-done.1
  82.2 1.2 %post.1 = (bf16[256,512]{1,0:T(8,128)(2,1)}, bf16[256,512]{1,0:T(8,128)(2,1)}, bf16[256,512]{1,0:T(8,128)(2,1)}, f32[64,256]{1,0:T(8,128)}) custom-call(f32[2560,128]{1,0:T(8,128)S(1)} %bitcast.9, bf16[256,512]{1,0:T(8,128)(2,1)S(1)} %copy-done, bf16[256,512]{1,0:T(8,128)(2,1)S(1)} %copy-done.1, bf16[256,512]{1,0:T(8,128)(2,1)S(1)} %copy-done.2), custom_call_target="tpu_custom_call" | custom-call | tf_op jit(solution)/shard_map/post/pallas_call | solution.py:301
  (9 shorter events, 0.0 us)
Async XLA Ops:
  31.3 7.4 %copy-start.3 = (bf16[256,256]{1,0:T(8,128)(2,1)S(1)}, bf16[256,256]{1,0:T(8,128)(2,1)}, u32[]{:S(2)}) copy-start(bf16[256,256]{1,0:T(8,128)(2,1)} %constant.18.clone.v2h_ref) | copy-start | bytes 393220
  31.3 7.4 %copy-start.4 = (bf16[256,256]{1,0:T(8,128)(2,1)S(1)}, bf16[256,256]{1,0:T(8,128)(2,1)}, u32[]{:S(2)}) copy-start(bf16[256,256]{1,0:T(8,128)(2,1)} %constant.19.clone.v2l_ref) | copy-start | bytes 393220
  31.3 7.4 %copy-start.5 = (bf16[256,256]{1,0:T(8,128)(2,1)S(1)}, bf16[256,256]{1,0:T(8,128)(2,1)}, u32[]{:S(2)}) copy-start(bf16[256,256]{1,0:T(8,128)(2,1)} %constant.15.clone.w2h_ref) | copy-start | bytes 393220
  31.3 7.4 %copy-start.6 = (bf16[256,256]{1,0:T(8,128)(2,1)S(1)}, bf16[256,256]{1,0:T(8,128)(2,1)}, u32[]{:S(2)}) copy-start(bf16[256,256]{1,0:T(8,128)(2,1)} %constant.16.clone.w2l_ref) | copy-start | bytes 393220
  31.3 7.4 %copy-start.7 = (bf16[128,192]{1,0:T(8,128)(2,1)S(1)}, bf16[128,192]{1,0:T(8,128)(2,1)}, u32[]{:S(2)}) copy-start(bf16[128,192]{1,0:T(8,128)(2,1)} %constant.14.clone.w1_ref) | copy-start | bytes 147460
  31.3 7.4 %copy-start.8 = (f32[2,64,128]{2,1,0:T(8,128)S(1)}, f32[2,64,128]{2,1,0:T(8,128)}, u32[]{:S(2)}) copy-start(f32[2,64,128]{2,1,0:T(8,128)} %constant.17.clone.tw_ref) | copy-start | bytes 196612
  31.4 7.4 %copy-start.9 = (bf16[64,384]{1,0:T(8,128)(2,1)S(1)}, bf16[64,384]{1,0:T(8,128)(2,1)}, u32[]{:S(2)}) copy-start(bf16[64,384]{1,0:T(8,128)(2,1)} %constant.20.clone.v1_ref) | copy-start | bytes 147460
  31.4 17.5 %collective-permute-start.3 = (f32[2,64,128]{2,1,0:T(8,128)S(1)}, f32[2,64,128]{2,1,0:T(8,128)S(1)}, u32[]{:S(2)}, u32[]{:S(2)}) collective-permute-start(f32[2,64,128]{2,1,0:T(8,128)S(1)} %pick.1.f0_ref), channel_id=1, source_target_pairs={{0,2},{1,3},{2,0},{3,1},{4,6},{5,7},{6,4},{7,5},{8,10},{9,11},{10,... | collective-permute-start | bytes 196616 | tf_op jit(solution)/shard_map/ppermute | solution.py:266
  34.5 14.4 %collective-permute-start.4 = (f32[2,64,128]{2,1,0:T(8,128)S(1)}, f32[2,64,128]{2,1,0:T(8,128)S(1)}, u32[]{:S(2)}, u32[]{:S(2)}) collective-permute-start(f32[2,64,128]{2,1,0:T(8,128)S(1)} %pick.1.f0_ref), channel_id=1, source_target_pairs={{0,4},{1,5},{2,6},{3,7},{4,0},{5,1},{6,2},{7,3},{8,12},{9,13},{10,... | collective-permute-start | bytes 196616 | tf_op jit(solution)/shard_map/ppermute | solution.py:266
  38.7 10.2 %collective-permute-start.5 = (f32[2,64,128]{2,1,0:T(8,128)S(1)}, f32[2,64,128]{2,1,0:T(8,128)S(1)}, u32[]{:S(2)}, u32[]{:S(2)}) collective-permute-start(f32[2,64,128]{2,1,0:T(8,128)S(1)} %pick.1.f0_ref), channel_id=1, source_target_pairs={{0,6},{1,7},{2,4},{3,5},{4,2},{5,3},{6,0},{7,1},{8,14},{9,15},{10,... | collective-permute-start | bytes 196616 | tf_op jit(solution)/shard_map/ppermute | solution.py:266
  43.2 10.7 %collective-permute-start = (f32[2,64,128]{2,1,0:T(8,128)S(1)}, f32[2,64,128]{2,1,0:T(8,128)S(1)}, u32[]{:S(2)}, u32[]{:S(2)}) collective-permute-start(f32[2,64,128]{2,1,0:T(8,128)S(1)} %get-tuple-element.15), channel_id=1, source_target_pairs={{0,2},{1,3},{2,0},{3,1},{4,6},{5,7},{6,4},{7,5},{8,10},{9,11},{10,... | collective-permute-start | bytes 196616 | tf_op jit(solution)/shard_map/ppermute | solution.py:266
  44.7 9.2 %collective-permute-start.1 = (f32[2,64,128]{2,1,0:T(8,128)S(1)}, f32[2,64,128]{2,1,0:T(8,128)S(1)}, u32[]{:S(2)}, u32[]{:S(2)}) collective-permute-start(f32[2,64,128]{2,1,0:T(8,128)S(1)} %get-tuple-element.16), channel_id=1, source_target_pairs={{0,4},{1,5},{2,6},{3,7},{4,0},{5,1},{6,2},{7,3},{8,12},{9,13},{10,... | collective-permute-start | bytes 196616 | tf_op jit(solution)/shard_map/ppermute | solution.py:266
  48.9 5.9 %collective-permute-start.2 = (f32[2,64,128]{2,1,0:T(8,128)S(1)}, f32[2,64,128]{2,1,0:T(8,128)S(1)}, u32[]{:S(2)}, u32[]{:S(2)}) collective-permute-start(f32[2,64,128]{2,1,0:T(8,128)S(1)} %get-tuple-element.17), channel_id=1, source_target_pairs={{0,6},{1,7},{2,4},{3,5},{4,2},{5,3},{6,0},{7,1},{8,14},{9,15},{10,... | collective-permute-start | bytes 196616 | tf_op jit(solution)/shard_map/ppermute | solution.py:266
  54.8 27.4 %copy-start = (bf16[256,512]{1,0:T(8,128)(2,1)S(1)}, bf16[256,512]{1,0:T(8,128)(2,1)}, u32[]{:S(2)}) copy-start(bf16[256,512]{1,0:T(8,128)(2,1)} %inner_ref.1) | copy-start | bytes 786436
  54.8 27.4 %copy-start.1 = (bf16[256,512]{1,0:T(8,128)(2,1)S(1)}, bf16[256,512]{1,0:T(8,128)(2,1)}, u32[]{:S(2)}) copy-start(bf16[256,512]{1,0:T(8,128)(2,1)} %signal_ref.1) | copy-start | bytes 786436
  54.8 27.4 %copy-start.2 = (bf16[256,512]{1,0:T(8,128)(2,1)S(1)}, bf16[256,512]{1,0:T(8,128)(2,1)}, u32[]{:S(2)}) copy-start(bf16[256,512]{1,0:T(8,128)(2,1)} %cot_ref.1) | copy-start | bytes 786436

commit v2 on v1

--- a/solution.py
+++ b/solution.py
@@ -17,7 +17,7 @@
 B = 128
 SHARDS = 32
 MEMBERS = 64
-ROWS = 40
+ROWS = 34
 SCATTER = np.random.RandomState(0).permutation(SHARDS)
 VMEM_LIMIT = 16 * 1024 * 1024
 
@@ -82,7 +82,8 @@
         im.append(qr * s + qi * c)
     both = jnp.concatenate([jnp.concatenate(re, axis=1), jnp.concatenate(im, axis=1)], axis=0)
     high, low = split(both)
-    return dot(v1, jnp.concatenate([high, low, high], axis=0))
+    vh, vl = v1[:, : 2 * A], v1[:, 4 * A :]
+    return dot(v1[:, : 4 * A], jnp.concatenate([high, low], axis=0)) + dot(vl, high)
 
 
 def forward(columns, w1, w2h, w2l, c, s):
@@ -107,8 +108,6 @@
             row = first_row + h * 8 + cb * 2 + e
             send_ref[pl.ds(row, MEMBERS, stride=ROWS), :] = turned[e * 64 : (e + 1) * 64]
 
-    for row in range(34, ROWS):
-        send_ref[pl.ds(row, MEMBERS, stride=ROWS), :] = jnp.zeros((MEMBERS, B), F32)
     for h in range(2):
         rows = slice(h * B, (h + 1) * B)
         for copy in copies[h * 4 : h * 4 + 4]:
@@ -169,7 +168,7 @@
         prod_ref[f] = jnp.concatenate([pr[:A] + pr[A:], pi[:A] + pi[A:]], axis=1)
         return carry
 
-    lax.fori_loop(0, 8, step, 0)
+    lax.fori_loop(0, 8, step, 0, unroll=True)
 
     owners = partners()
     for k in (2, 0):
@@ -205,45 +204,61 @@
                 )
         return carry
 
-    lax.fori_loop(0, 8, step, 0)
-    for row in range(34, ROWS):
-        out_ref[pl.ds(row, MEMBERS, stride=ROWS), :] = jnp.zeros((MEMBERS, B), F32)
+    lax.fori_loop(0, 8, step, 0, unroll=True)
 
 
 def place_kernel(fg0_ref, fg1_ref, fg2_ref, fg3_ref, base_ref, out_ref):
+    out_ref[...] = base_ref[...]
     total = (fg0_ref[...] + fg1_ref[...]) + (fg2_ref[...] + fg3_ref[...])
     for q in range(2):
         for h in range(2):
             out_ref[pl.ds(q * 32 * ROWS + 32 + h, 32, stride=ROWS), :] = total[q, h * 32 : (h + 1) * 32]
 
 
-def post_kernel(recv_ref, inner_ref, signal_ref, cot_ref, og_ref, ig_ref, sg_ref, fg_ref):
+def post_kernel(recv_ref, inner_ref, signal_ref, cot_ref, og_hbm, ig_hbm, sg_hbm, fg_hbm,
+                og_ref, ig_ref, sg_ref, fg_ref, sems):
     def fetch(first_row, h, cb):
         blocks = [
             recv_ref[pl.ds(first_row + h * 8 + cb * 2 + e, MEMBERS, stride=ROWS), :] for e in range(2)
         ]
         return jnp.concatenate(blocks, axis=0).T
 
+    copies = []
+
+    def store(from_ref, to_ref, rows):
+        copy = pltpu.make_async_copy(from_ref.at[rows], to_ref.at[rows], sems.at[len(copies)])
+        copy.start()
+        copies.append(copy)
+
+    for h in range(2):
+        block = recv_ref[pl.ds(32 + h, MEMBERS, stride=ROWS), :]
+        fg_ref[:, h * B : (h + 1) * B] = block * (1.0 / math.sqrt(N))
+    store(fg_ref, fg_hbm, pl.ds(0, 64))
     for h in range(2):
         rows = slice(h * B, (h + 1) * B)
         for cb in range(4):
             cols = slice(cb * 128, (cb + 1) * 128)
             og_ref[rows, cols] = (cot_ref[rows, cols].astype(F32) * fetch(0, h, cb)).astype(BF)
+        store(og_ref, og_hbm, pl.ds(h * B, B))
+        for cb in range(4):
+            cols = slice(cb * 128, (cb + 1) * 128)
             back = fetch(16, h, cb)
             ig_ref[rows, cols] = (back * signal_ref[rows, cols].astype(F32)).astype(BF)
             sg_ref[rows, cols] = (back * inner_ref[rows, cols].astype(F32)).astype(BF)
-        block = recv_ref[pl.ds(32 + h, MEMBERS, stride=ROWS), :]
-        fg_ref[:, rows] = block * (1.0 / math.sqrt(N))
-
-
-def call(kernel, out_shapes, name, scratch=(), cost=(0, 0), aliases=None, ins=None):
+        store(ig_ref, ig_hbm, pl.ds(h * B, B))
+        store(sg_ref, sg_hbm, pl.ds(h * B, B))
+    for copy in copies:
+        copy.wait()
+
+
+def call(kernel, out_shapes, name, scratch=(), cost=(0, 0), ins=None, outs=None):
     return pl.pallas_call(
         kernel,
         out_shape=out_shapes,
         in_specs=pl.no_block_spec if ins is None else ins,
         scratch_shapes=list(scratch),
         name=name,
-        input_output_aliases=aliases or {},
+        out_specs=pl.no_block_spec if outs is None else outs,
         compiler_params=pltpu.CompilerParams(vmem_limit_bytes=VMEM_LIMIT),
         cost_estimate=pl.CostEstimate(flops=cost[0], bytes_accessed=cost[1], transcendentals=0),
     )
@@ -257,7 +272,7 @@
 
 
 def exchange(x):
-    x = x.reshape(MEMBERS, ROWS, B)
+    x = x.reshape(MEMBERS, ROWS * B)
     x = lax.all_to_all(x, ("seq", "chan"), 0, 0, axis_index_groups=PAIRS, tiled=True)
     return x.reshape(MEMBERS * ROWS, B)
 
@@ -296,12 +311,14 @@
     out = call(conv_kernel, buffer, "conv", cost=(2_000_000_000, 4_000_000))(
         spec, u, g, tw, v2h, v2l, v1
     )
-    back_send = call(place_kernel, buffer, "place", aliases={4: 0})(fg0, fg1, fg2, fg3, out)
+    back_send = call(place_kernel, buffer, "place")(fg0, fg1, fg2, fg3, out)
     landed = exchange(back_send)
     *grads, fg = call(
         post_kernel,
         (shape(256, 512, dtype=BF), shape(256, 512, dtype=BF), shape(256, 512, dtype=BF), shape(64, 256)),
         "post",
+        [gate, gate, gate, pltpu.VMEM((64, 256), F32), pltpu.SemaphoreType.DMA((7,))],
+        outs=[pl.BlockSpec(memory_space=pltpu.HBM)] * 4,
     )(landed, inner_gate, signal, cotangent)
     return (*grads, fg.T)
 

time: 83.6 us -> 77.1 us (0.922)
  blocking collectives: 56.4 us -> 51.6 us
  Pallas kernels: 12.3 us -> 9.03 us
  waiting for transfers between devices: 0.9 us -> 2.33 us
    all_to_all x2, blocking collectives: 56.4 us -> 51.6 us  [exchange(): lax.all_to_all(x, ('seq', 'chan'), 0, 0, axis_index_groups=PAIRS, tiled=T...]
    pallas_call x1, Pallas kernels: 4.42 us -> 2.65 us  [body(): call(spectra_kernel, (shape(8, 2 * A, 2 * B), shape(8, 2 * A, 2 * B), two...]
    ppermute x6, waiting for transfers between devices: 0.9 us -> 2.33 us  [swap(): return lax.ppermute(x, 'chan', [(z, z ^ distance) for z in range(8)])]
    pallas_call x1, Pallas kernels: 4.35 us -> 3.01 us  [body(): call(conv_kernel, buffer, 'conv', cost=(2000000000, 4000000))]
  transfers between devices with their start and end apart: 6 -> 6, of which waited for: 1 -> 2; matrix products, arithmetic and copies ran while one was open for 0% -> 0% of each run, Pallas kernels for 11% -> 8%
where the time goes in v2:
time: 77.1 us; the launch traced here: 76.9 us
  blocking collectives  51.6 us (67%)
  starting transfers between devices  13 us (17%)
  Pallas kernels  9.03 us (12%)
  waiting for transfers between devices  2.33 us (3%)
  between operations  0.79 us (1%)
    all_to_all x2, blocking collectives, exchange(): lax.all_to_all(x, ('seq', 'chan'), 0, 0, axis_index_groups=PAIRS, tiled=T...  51.6 us
    ppermute x6, starting transfers between devices, swap(): return lax.ppermute(x, 'chan', [(z, z ^ distance) for z in range(8)])  13 us
    pallas_call x1, Pallas kernels, body(): call(conv_kernel, buffer, 'conv', cost=(2000000000, 4000000))  3.01 us
    pallas_call x1, Pallas kernels, body(): call(spectra_kernel, (shape(8, 2 * A, 2 * B), shape(8, 2 * A, 2 * B), two...  2.65 us
    ppermute x6, waiting for transfers between devices, swap(): return lax.ppermute(x, 'chan', [(z, z ^ distance) for z in range(8)])  2.33 us
    pallas_call x1, Pallas kernels, body(): call(prep_kernel, buffer, 'prep', [gate, gate, gate, gate, pltpu.VMEM((64...  1.6 us
  transfers between devices with their start and end apart: 6, of which 2 were waited for; matrix products, arithmetic and copies ran while one was open for 0% of the time, Pallas kernels for 8%

profile of v2, /device:TPU:1, one launch (start us, length us, event | category | flops | bytes accessed | tf_op | source)
XLA Modules:
  0.0 76.9 jit_solution(8690768681031077988)
XLA Ops:
  0.6 1.6 %prep.1 = f32[2176,128]{1,0:T(8,128)S(1)} custom-call(bf16[256,512]{1,0:T(8,128)(2,1)} %outer_hbm.1, bf16[256,512]{1,0:T(8,128)(2,1)} %inner_ref.1, bf16[256,512]{1,0:T(8,128)(2,1)} %signal_ref.1, bf16[256,512]{1,0:T(8,128)(2,1)} %cot_ref.1, f32[64,256]{1,0:T(8,128)} %bitcast.11), custom_call_target="tpu_custom_call" | custom-call | tf_op jit(solution)/shard_map/prep/pallas_call | solution.py:289
  2.2 27.1 %all_to_all.18 = f32[64,1,4352]{2,1,0:T(1,128)S(1)} all-to-all(f32[64,1,4352]{2,1,0:T(1,128)S(1)} %bitcast.9), channel_id=1, replica_groups={{88,176,80,16,128,112,224,208,160,104,192,40,136,64,240,200,184,8,248,4..., dimensions={0} | all-to-all | bytes 2228224 | tf_op jit(solution)/shard_map/all_to_all | solution.py:276
  29.3 0.0 copy-start.7
  29.3 0.0 copy-start.8
  29.3 0.0 copy-start.9
  29.4 3.1 %collective-permute-start.3 = (f32[2,64,128]{2,1,0:T(8,128)S(1)}, f32[2,64,128]{2,1,0:T(8,128)S(1)}, u32[]{:S(2)}, u32[]{:S(2)}) collective-permute-start(f32[2,64,128]{2,1,0:T(8,128)S(1)} %pick.1.f0_ref), channel_id=1, source_target_pairs={{0,2},{1,3},{2,0},{3,1},{4,6},{5,7},{6,4},{7,5},{8,10},{9,11},{10,... | collective-permute-start | bytes 196616 | tf_op jit(solution)/shard_map/ppermute | solution.py:281
  32.4 4.2 %collective-permute-start.4 = (f32[2,64,128]{2,1,0:T(8,128)S(1)}, f32[2,64,128]{2,1,0:T(8,128)S(1)}, u32[]{:S(2)}, u32[]{:S(2)}) collective-permute-start(f32[2,64,128]{2,1,0:T(8,128)S(1)} %pick.1.f0_ref), channel_id=1, source_target_pairs={{0,4},{1,5},{2,6},{3,7},{4,0},{5,1},{6,2},{7,3},{8,12},{9,13},{10,... | collective-permute-start | bytes 196616 | tf_op jit(solution)/shard_map/ppermute | solution.py:281
  36.6 0.0 collective-permute-start.5
  36.7 0.0 copy-done.4
  36.7 0.0 copy-done.5
  36.7 0.0 copy-done.6
  36.7 0.0 copy-done.7
  36.7 0.0 copy-done.8
  36.7 0.0 copy-done.9
  36.7 2.6 %spectra.1 = (f32[8,128,256]{2,1,0:T(8,128)S(1)}, f32[8,128,256]{2,1,0:T(8,128)S(1)}, f32[2,64,128]{2,1,0:T(8,128)S(1)}, f32[2,64,128]{2,1,0:T(8,128)S(1)}, f32[...) custom-call(f32[2176,128]{1,0:T(8,128)S(1)} %bitcast.8, bf16[128,192]{1,0:T(8,128)(2,1)S(1)} %copy-done.7, ...), custom_call_target="tpu_custom_call" | custom-call | flops 2000000000 | bytes 4000000 | tf_op jit(solution)/shard_map/spectra/pallas_call | solution.py:300
  39.4 1.5 %collective-permute-start = (f32[2,64,128]{2,1,0:T(8,128)S(1)}, f32[2,64,128]{2,1,0:T(8,128)S(1)}, u32[]{:S(2)}, u32[]{:S(2)}) collective-permute-start(f32[2,64,128]{2,1,0:T(8,128)S(1)} %get-tuple-element.15), channel_id=1, source_target_pairs={{0,2},{1,3},{2,0},{3,1},{4,6},{5,7},{6,4},{7,5},{8,10},{9,11},{10,... | collective-permute-start | bytes 196616 | tf_op jit(solution)/shard_map/ppermute | solution.py:281
  40.9 4.2 %collective-permute-start.1 = (f32[2,64,128]{2,1,0:T(8,128)S(1)}, f32[2,64,128]{2,1,0:T(8,128)S(1)}, u32[]{:S(2)}, u32[]{:S(2)}) collective-permute-start(f32[2,64,128]{2,1,0:T(8,128)S(1)} %get-tuple-element.16), channel_id=1, source_target_pairs={{0,4},{1,5},{2,6},{3,7},{4,0},{5,1},{6,2},{7,3},{8,12},{9,13},{10,... | collective-permute-start | bytes 196616 | tf_op jit(solution)/shard_map/ppermute | solution.py:281
  45.1 0.0 collective-permute-done.3.f1_ref
  45.1 0.0 collective-permute-start.2
  45.1 0.0 collective-permute-done.4.f2_ref
  45.1 0.0 collective-permute-done.5.f3_ref
  45.1 0.6 filters.1.spec_ref
  45.7 3.0 %conv.1.base_ref = f32[2176,128]{1,0:T(8,128)S(1)} custom-call(f32[8,64,256]{2,1,0:T(8,128)S(1)} %filters.1.spec_ref, f32[8,128,256]{2,1,0:T(8,128)S(1)} %get-tuple-element.18.u_ref, f32[8,128,256]{2,1,0:T(8,128)S(1)} %get-tuple-element.19.g_ref, f32[2,64,128]{2,1,0:T(8,128)S(1)} %copy-done.8, bf16[256,256]{1,0:T(8,128)(2,1)S(1)} %copy-done.3, ...), custom_call_target="tpu_custom_call" | custom-call | flops 2000000000 | bytes 4000000 | tf_op jit(solution)/shard_map/conv/pallas_call | solution.py:311
  48.7 0.0 collective-permute-done.fg1_ref
  48.7 1.3 %collective-permute-done.1.fg2_ref = f32[2,64,128]{2,1,0:T(8,128)S(1)} collective-permute-done((f32[2,64,128]{2,1,0:T(8,128)S(1)}, f32[2,64,128]{2,1,0:T(8,128)S(1)}, u32[]{:S(2)}, u32[]{:S(2)}) %collective-permute-start.1) | collective-permute-done | bytes 65568 | tf_op jit(solution)/shard_map/ppermute | solution.py:281
  50.0 1.0 %collective-permute-done.2.fg3_ref = f32[2,64,128]{2,1,0:T(8,128)S(1)} collective-permute-done((f32[2,64,128]{2,1,0:T(8,128)S(1)}, f32[2,64,128]{2,1,0:T(8,128)S(1)}, u32[]{:S(2)}, u32[]{:S(2)}) %collective-permute-start.2) | collective-permute-done | bytes 65568 | tf_op jit(solution)/shard_map/ppermute | solution.py:281
  51.1 0.1 place.1
  51.1 0.0 copy-start
  51.2 0.0 copy-start.1
  51.2 0.0 copy-start.2
  51.2 24.6 %all_to_all.19 = f32[64,1,4352]{2,1,0:T(1,128)S(1)} all-to-all(f32[64,1,4352]{2,1,0:T(1,128)S(1)} %bitcast.6), channel_id=1, replica_groups={{88,176,80,16,128,112,224,208,160,104,192,40,136,64,240,200,184,8,248,4..., dimensions={0} | all-to-all | bytes 2228224 | tf_op jit(solution)/shard_map/all_to_all | solution.py:276
  75.8 1.1 %post.1 = (bf16[256,512]{1,0:T(8,128)(2,1)}, bf16[256,512]{1,0:T(8,128)(2,1)}, bf16[256,512]{1,0:T(8,128)(2,1)}, f32[64,256]{1,0:T(8,128)}) custom-call(f32[2176,128]{1,0:T(8,128)S(1)} %bitcast.10, bf16[256,512]{1,0:T(8,128)(2,1)S(1)} %copy-done, bf16[256,512]{1,0:T(8,128)(2,1)S(1)} %copy-done.1, bf16[256,512]{1,0:T(8,128)(2,1)S(1)} %copy-done.2), custom_call_target="tpu_custom_call" | custom-call | tf_op jit(solution)/shard_map/post/pallas_call | solution.py:316
  (9 shorter events, 0.0 us)
Async XLA Ops:
  29.3 7.4 %copy-start.3 = (bf16[256,256]{1,0:T(8,128)(2,1)S(1)}, bf16[256,256]{1,0:T(8,128)(2,1)}, u32[]{:S(2)}) copy-start(bf16[256,256]{1,0:T(8,128)(2,1)} %constant.18.clone.v2h_ref) | copy-start | bytes 393220
  29.3 7.4 %copy-start.4 = (bf16[256,256]{1,0:T(8,128)(2,1)S(1)}, bf16[256,256]{1,0:T(8,128)(2,1)}, u32[]{:S(2)}) copy-start(bf16[256,256]{1,0:T(8,128)(2,1)} %constant.19.clone.v2l_ref) | copy-start | bytes 393220
  29.3 7.4 %copy-start.5 = (bf16[256,256]{1,0:T(8,128)(2,1)S(1)}, bf16[256,256]{1,0:T(8,128)(2,1)}, u32[]{:S(2)}) copy-start(bf16[256,256]{1,0:T(8,128)(2,1)} %constant.15.clone.w2h_ref) | copy-start | bytes 393220
  29.3 7.4 %copy-start.6 = (bf16[256,256]{1,0:T(8,128)(2,1)S(1)}, bf16[256,256]{1,0:T(8,128)(2,1)}, u32[]{:S(2)}) copy-start(bf16[256,256]{1,0:T(8,128)(2,1)} %constant.16.clone.w2l_ref) | copy-start | bytes 393220
  29.3 7.4 %copy-start.7 = (bf16[128,192]{1,0:T(8,128)(2,1)S(1)}, bf16[128,192]{1,0:T(8,128)(2,1)}, u32[]{:S(2)}) copy-start(bf16[128,192]{1,0:T(8,128)(2,1)} %constant.14.clone.w1_ref) | copy-start | bytes 147460
  29.3 7.4 %copy-start.8 = (f32[2,64,128]{2,1,0:T(8,128)S(1)}, f32[2,64,128]{2,1,0:T(8,128)}, u32[]{:S(2)}) copy-start(f32[2,64,128]{2,1,0:T(8,128)} %constant.17.clone.tw_ref) | copy-start | bytes 196612
  29.3 7.4 %copy-start.9 = (bf16[64,384]{1,0:T(8,128)(2,1)S(1)}, bf16[64,384]{1,0:T(8,128)(2,1)}, u32[]{:S(2)}) copy-start(bf16[64,384]{1,0:T(8,128)(2,1)} %constant.20.clone.v1_ref) | copy-start | bytes 147460
  29.4 15.7 %collective-permute-start.3 = (f32[2,64,128]{2,1,0:T(8,128)S(1)}, f32[2,64,128]{2,1,0:T(8,128)S(1)}, u32[]{:S(2)}, u32[]{:S(2)}) collective-permute-start(f32[2,64,128]{2,1,0:T(8,128)S(1)} %pick.1.f0_ref), channel_id=1, source_target_pairs={{0,2},{1,3},{2,0},{3,1},{4,6},{5,7},{6,4},{7,5},{8,10},{9,11},{10,... | collective-permute-start | bytes 196616 | tf_op jit(solution)/shard_map/ppermute | solution.py:281
  32.4 12.7 %collective-permute-start.4 = (f32[2,64,128]{2,1,0:T(8,128)S(1)}, f32[2,64,128]{2,1,0:T(8,128)S(1)}, u32[]{:S(2)}, u32[]{:S(2)}) collective-permute-start(f32[2,64,128]{2,1,0:T(8,128)S(1)} %pick.1.f0_ref), channel_id=1, source_target_pairs={{0,4},{1,5},{2,6},{3,7},{4,0},{5,1},{6,2},{7,3},{8,12},{9,13},{10,... | collective-permute-start | bytes 196616 | tf_op jit(solution)/shard_map/ppermute | solution.py:281
  36.6 8.5 %collective-permute-start.5 = (f32[2,64,128]{2,1,0:T(8,128)S(1)}, f32[2,64,128]{2,1,0:T(8,128)S(1)}, u32[]{:S(2)}, u32[]{:S(2)}) collective-permute-start(f32[2,64,128]{2,1,0:T(8,128)S(1)} %pick.1.f0_ref), channel_id=1, source_target_pairs={{0,6},{1,7},{2,4},{3,5},{4,2},{5,3},{6,0},{7,1},{8,14},{9,15},{10,... | collective-permute-start | bytes 196616 | tf_op jit(solution)/shard_map/ppermute | solution.py:281
  39.4 9.4 %collective-permute-start = (f32[2,64,128]{2,1,0:T(8,128)S(1)}, f32[2,64,128]{2,1,0:T(8,128)S(1)}, u32[]{:S(2)}, u32[]{:S(2)}) collective-permute-start(f32[2,64,128]{2,1,0:T(8,128)S(1)} %get-tuple-element.15), channel_id=1, source_target_pairs={{0,2},{1,3},{2,0},{3,1},{4,6},{5,7},{6,4},{7,5},{8,10},{9,11},{10,... | collective-permute-start | bytes 196616 | tf_op jit(solution)/shard_map/ppermute | solution.py:281
  40.9 9.2 %collective-permute-start.1 = (f32[2,64,128]{2,1,0:T(8,128)S(1)}, f32[2,64,128]{2,1,0:T(8,128)S(1)}, u32[]{:S(2)}, u32[]{:S(2)}) collective-permute-start(f32[2,64,128]{2,1,0:T(8,128)S(1)} %get-tuple-element.16), channel_id=1, source_target_pairs={{0,4},{1,5},{2,6},{3,7},{4,0},{5,1},{6,2},{7,3},{8,12},{9,13},{10,... | collective-permute-start | bytes 196616 | tf_op jit(solution)/shard_map/ppermute | solution.py:281
  45.1 6.0 %collective-permute-start.2 = (f32[2,64,128]{2,1,0:T(8,128)S(1)}, f32[2,64,128]{2,1,0:T(8,128)S(1)}, u32[]{:S(2)}, u32[]{:S(2)}) collective-permute-start(f32[2,64,128]{2,1,0:T(8,128)S(1)} %get-tuple-element.17), channel_id=1, source_target_pairs={{0,6},{1,7},{2,4},{3,5},{4,2},{5,3},{6,0},{7,1},{8,14},{9,15},{10,... | collective-permute-start | bytes 196616 | tf_op jit(solution)/shard_map/ppermute | solution.py:281
  51.1 24.6 %copy-start = (bf16[256,512]{1,0:T(8,128)(2,1)S(1)}, bf16[256,512]{1,0:T(8,128)(2,1)}, u32[]{:S(2)}) copy-start(bf16[256,512]{1,0:T(8,128)(2,1)} %inner_ref.1) | copy-start | bytes 786436
  51.2 24.6 %copy-start.1 = (bf16[256,512]{1,0:T(8,128)(2,1)S(1)}, bf16[256,512]{1,0:T(8,128)(2,1)}, u32[]{:S(2)}) copy-start(bf16[256,512]{1,0:T(8,128)(2,1)} %signal_ref.1) | copy-start | bytes 786436
  51.2 24.6 %copy-start.2 = (bf16[256,512]{1,0:T(8,128)(2,1)S(1)}, bf16[256,512]{1,0:T(8,128)(2,1)}, u32[]{:S(2)}) copy-start(bf16[256,512]{1,0:T(8,128)(2,1)} %cot_ref.1) | copy-start | bytes 786436

commit v3 on v2

v3 whole, which is shorter than its diff:
```python
import functools
import math

import jax
import jax.numpy as jnp
import numpy as np
import ml_dtypes
from jax import lax
from jax.experimental import pallas as pl
from jax.experimental.pallas import tpu as pltpu
from jax.sharding import PartitionSpec as P

BF = jnp.bfloat16
F32 = jnp.float32

N = 8192
A = 64
B = 128
SHARDS = 32
MEMBERS = 64
ROWS = 34
SCATTER = np.random.RandomState(0).permutation(SHARDS)
VMEM_LIMIT = 16 * 1024 * 1024


def two_parts(table):
    high = table.astype(ml_dtypes.bfloat16)
    low = (table - high.astype(np.float64)).astype(ml_dtypes.bfloat16)
    return high, low


def tables():
    order = np.array([2 * s + h for h in range(2) for s in SCATTER])
    k1 = np.arange(A) - 0.25
    angle1 = 2 * np.pi / A * np.outer(k1, order)
    w1 = np.concatenate([np.cos(angle1), -np.sin(angle1)], axis=0)
    high, low = two_parts(w1)
    w1cat = np.concatenate([high, high, low], axis=1)
    v1 = np.concatenate([np.cos(angle1), -np.sin(angle1)], axis=0).T / N
    high, low = two_parts(v1)
    v1cat = np.concatenate([high, high, low], axis=1)
    angle2 = 2 * np.pi / B * np.outer(np.arange(B), np.arange(B))
    c, s = np.cos(angle2), np.sin(angle2)
    w2 = np.block([[c, -s], [s, c]])
    w2h, w2l = two_parts(w2)
    angle = 2 * np.pi / N * np.outer(k1, np.arange(B))
    twiddle = np.stack([np.cos(angle), np.sin(angle)]).astype(np.float32)
    return w1cat, w2h, w2l, twiddle, v1cat


def split(x):
    high = x.astype(BF)
    return high, (x - high.astype(F32)).astype(BF)


def dot(x, y):
    return jnp.dot(x, y, preferred_element_type=F32)


def first_stage(columns, w1, c, s):
    high, low = split(jnp.concatenate(columns, axis=1))
    out = dot(w1, jnp.concatenate([high, low, high], axis=0))
    pairs = []
    for i in range(len(columns)):
        re = out[:A, i * B : (i + 1) * B]
        im = out[A:, i * B : (i + 1) * B]
        pairs.append((re * c + im * s, im * c - re * s))
    return pairs


def second_stage(pairs, high_table, low_table):
    stacked = jnp.concatenate([jnp.concatenate(p, axis=1) for p in pairs], axis=0)
    high, low = split(stacked)
    return dot(high, high_table) + dot(low, high_table) + dot(high, low_table)


def last_stage(blocks, v1, c, s):
    re, im = [], []
    for block in blocks:
        qi, qr = block[:, :B], block[:, B:]
        re.append(qr * c - qi * s)
        im.append(qr * s + qi * c)
    both = jnp.concatenate([jnp.concatenate(re, axis=1), jnp.concatenate(im, axis=1)], axis=0)
    high, low = split(both)
    vh, vl = v1[:, : 2 * A], v1[:, 4 * A :]
    return dot(v1[:, : 4 * A], jnp.concatenate([high, low], axis=0)) + dot(vl, high)


def forward(columns, w1, w2h, w2l, c, s):
    return second_stage(first_stage(columns, w1, c, s), w2h, w2l)


def prep_kernel(outer_hbm, inner_hbm, signal_hbm, cot_hbm, filt_hbm, send_ref,
                outer_ref, inner_ref, signal_ref, cot_ref, filt_ref, sems):
    def load(i, from_ref, to_ref, rows):
        copy = pltpu.make_async_copy(from_ref.at[rows], to_ref.at[rows], sems.at[i])
        copy.start()
        return copy

    halves = [pl.ds(0, B), pl.ds(B, B)]
    arrays = [(inner_hbm, inner_ref), (signal_hbm, signal_ref), (cot_hbm, cot_ref), (outer_hbm, outer_ref)]
    copies = [load(i * 4 + j, *pair, rows) for i, rows in enumerate(halves) for j, pair in enumerate(arrays)]
    last = load(8, filt_hbm, filt_ref, pl.ds(0, 64))

    pairs = partners()

    def place(block, first_row, h, k):
        turned = block.T
        for e in range(2):
            row = first_row + h * 8 + k * 2 + e
            send_ref[pl.ds(row, MEMBERS, stride=ROWS), :] = turned[e * 64 : (e + 1) * 64]

    for h in range(2):
        rows = slice(h * B, (h + 1) * B)
        for copy in copies[h * 4 : h * 4 + 4]:
            copy.wait()
        for k in range(4):
            cols = pl.ds(pl.multiple_of(pairs[k] * B, B), B)
            place(inner_ref[rows, cols].astype(F32) * signal_ref[rows, cols].astype(F32), 0, h, k)
            place(cot_ref[rows, cols].astype(F32) * outer_ref[rows, cols].astype(F32), 16, h, k)
    last.wait()
    for h in range(2):
        send_ref[pl.ds(32 + h, MEMBERS, stride=ROWS), :] = filt_ref[:, h * B : (h + 1) * B]


def partners():
    pair = lax.axis_index("chan") // 2
    beside = pair + 1 - 2 * lax.rem(pair, 2)
    return [pair, beside, lax.rem(pair + 2, 4), lax.rem(beside + 2, 4)]


def gather_rows(ref, q, row, step):
    return jnp.concatenate(
        [ref[pl.ds(q * 32 * ROWS + row + step * h, 32, stride=ROWS), :] for h in range(2)], axis=0
    )


def pick_kernel(recv_ref, out_ref):
    for q in range(2):
        out_ref[q] = gather_rows(recv_ref, q, 32, 1)


def spectra_kernel(recv_ref, w1_ref, w2h_ref, w2l_ref, tw_ref, v1_ref, u_ref, g_ref, fg_ref,
                   prod_ref, *, first):
    c, s = tw_ref[0], tw_ref[1]
    for f in range(4):
        columns = [gather_rows(recv_ref, q, first + f + base, 8) for base in (0, 16) for q in range(2)]
        spec = forward(columns, w1_ref[...], w2h_ref[...], w2l_ref[...], c, s)
        u_ref[f] = spec[: 2 * A]
        g_ref[f] = spec[2 * A :]
        ur, ui = spec[: 2 * A, :B], spec[: 2 * A, B:]
        gr, gi = spec[2 * A :, :B], spec[2 * A :, B:]
        pr = gr * ur + gi * ui
        pi = gi * ur - gr * ui
        prod_ref[f] = jnp.concatenate([pi[:A] + pi[A:], pr[:A] + pr[A:]], axis=1)
    high, low = split(prod_ref[...].reshape(4 * A, 2 * B))
    mid = dot(high, w2h_ref[...]) + dot(low, w2h_ref[...]) + dot(high, w2l_ref[...])
    out = last_stage([mid[i * A : (i + 1) * A] for i in range(4)], v1_ref[...], c, s)
    for i in range(4):
        fg_ref[i] = out[:, i * B : (i + 1) * B]


def mix_kernel(near_ref, came_ref, keep_ref, give_ref):
    keep_ref[...] = near_ref[0:2] + came_ref[2:4]
    give_ref[...] = near_ref[2:4] + came_ref[0:2]


def conv_part(ks, filts, u_refs, g_refs, w1, w2h, w2l, tw_ref, v1, out_ref):
    c, s = tw_ref[0], tw_ref[1]
    spec = forward([filt[q] for filt in filts for q in range(2)], w1, w2h, w2l, c, s)
    for j, k in enumerate(ks):
        for e in range(2):
            f = 2 * k + e
            u_ref, g_ref, at = u_refs[k // 2], g_refs[k // 2], f % 4
            h_spec = spec[(2 * j + e) * A : (2 * j + e + 1) * A]
            hr, hi = h_spec[:, :B], h_spec[:, B:]
            prods = []
            for q in range(2):
                ur, ui = u_ref[at, q * A : (q + 1) * A, :B], u_ref[at, q * A : (q + 1) * A, B:]
                prods.append((hr * ui + hi * ur, hr * ur - hi * ui))
            for q in range(2):
                gr, gi = g_ref[at, q * A : (q + 1) * A, :B], g_ref[at, q * A : (q + 1) * A, B:]
                prods.append((gi * hr - gr * hi, gr * hr + gi * hi))
            mid = second_stage(prods, w2h, w2l)
            out = last_stage([mid[i * A : (i + 1) * A] for i in range(4)], v1, c, s)
            for i in range(4):
                q, base = i % 2, (i // 2) * 16
                for h in range(2):
                    out_ref[pl.ds(q * 32 * ROWS + base + 8 * h + f, 32, stride=ROWS), :] = (
                        out[h * 32 : (h + 1) * 32, i * B : (i + 1) * B]
                    )


def conv_even_kernel(own_ref, f3_ref, u0_ref, g0_ref, u1_ref, g1_ref, w1_ref, w2h_ref, w2l_ref, tw_ref, v1_ref,
                     out_ref):
    conv_part((0, 3), (own_ref, f3_ref), (u0_ref, u1_ref), (g0_ref, g1_ref), w1_ref[...], w2h_ref[...], w2l_ref[...], tw_ref,
              v1_ref[...], out_ref)


def conv_odd_kernel(far_ref, base_ref, u0_ref, g0_ref, u1_ref, g1_ref, w1_ref, w2h_ref, w2l_ref,
                    tw_ref, v1_ref, out_ref):
    out_ref[...] = base_ref[...]
    conv_part((1, 2), (far_ref.at[0], far_ref.at[1]), (u0_ref, u1_ref), (g0_ref, g1_ref), w1_ref[...], w2h_ref[...],
              w2l_ref[...], tw_ref, v1_ref[...], out_ref)


def place_kernel(keep_ref, came_ref, base_ref, out_ref):
    out_ref[...] = base_ref[...]
    for q in range(2):
        total = keep_ref[q] + came_ref[q]
        for h in range(2):
            out_ref[pl.ds(q * 32 * ROWS + 32 + h, 32, stride=ROWS), :] = total[h * 32 : (h + 1) * 32]


def post_kernel(recv_ref, inner_ref, signal_ref, cot_ref, og_hbm, ig_hbm, sg_hbm, fg_hbm,
                og_ref, ig_ref, sg_ref, fg_ref, sems):
    pairs = partners()

    def fetch(first_row, h, k):
        blocks = [
            recv_ref[pl.ds(first_row + h * 8 + k * 2 + e, MEMBERS, stride=ROWS), :] for e in range(2)
        ]
        return jnp.concatenate(blocks, axis=0).T

    copies = []

    def store(from_ref, to_ref, rows):
        copy = pltpu.make_async_copy(from_ref.at[rows], to_ref.at[rows], sems.at[len(copies)])
        copy.start()
        copies.append(copy)

    for h in range(2):
        block = recv_ref[pl.ds(32 + h, MEMBERS, stride=ROWS), :]
        fg_ref[:, h * B : (h + 1) * B] = block * (1.0 / math.sqrt(N))
    store(fg_ref, fg_hbm, pl.ds(0, 64))
    for h in range(2):
        rows = slice(h * B, (h + 1) * B)
        for k in range(4):
            cols = pl.ds(pl.multiple_of(pairs[k] * B, B), B)
            og_ref[rows, cols] = (cot_ref[rows, cols].astype(F32) * fetch(0, h, k)).astype(BF)
        store(og_ref, og_hbm, pl.ds(h * B, B))
        for k in range(4):
            cols = pl.ds(pl.multiple_of(pairs[k] * B, B), B)
            back = fetch(16, h, k)
            ig_ref[rows, cols] = (back * signal_ref[rows, cols].astype(F32)).astype(BF)
            sg_ref[rows, cols] = (back * inner_ref[rows, cols].astype(F32)).astype(BF)
        store(ig_ref, ig_hbm, pl.ds(h * B, B))
        store(sg_ref, sg_hbm, pl.ds(h * B, B))
    for copy in copies:
        copy.wait()


def call(kernel, out_shapes, name, scratch=(), cost=(0, 0), ins=None, outs=None):
    return pl.pallas_call(
        kernel,
        out_shape=out_shapes,
        in_specs=pl.no_block_spec if ins is None else ins,
        scratch_shapes=list(scratch),
        name=name,
        out_specs=pl.no_block_spec if outs is None else outs,
        compiler_params=pltpu.CompilerParams(vmem_limit_bytes=VMEM_LIMIT),
        cost_estimate=pl.CostEstimate(flops=cost[0], bytes_accessed=cost[1], transcendentals=0),
    )


def shape(*dims, dtype=F32):
    return jax.ShapeDtypeStruct(dims, dtype)


PAIRS = [[s * 8 + 2 * p + q for q in range(2) for s in SCATTER.tolist()] for p in range(4)]


def exchange(x):
    x = x.reshape(MEMBERS, ROWS * B)
    x = lax.all_to_all(x, ("seq", "chan"), 0, 0, axis_index_groups=PAIRS, tiled=True)
    return x.reshape(MEMBERS * ROWS, B)


def swap(x, distance):
    return lax.ppermute(x, "chan", [(z, z ^ distance) for z in range(8)])


def body(outer_gate, inner_gate, signal, cotangent, filters):
    w1, w2h, w2l, tw, v1 = [jnp.asarray(t) for t in tables()]
    buffer = shape(MEMBERS * ROWS, B)
    two = shape(2, A, B)
    gate = pltpu.VMEM((256, 512), BF)
    send = call(
        prep_kernel, buffer, "prep",
        [gate, gate, gate, gate, pltpu.VMEM((64, 256), F32), pltpu.SemaphoreType.DMA((9,))],
        ins=[pl.BlockSpec(memory_space=pltpu.HBM)] * 5,
    )(*[
        pltpu.with_memory_space_constraint(x, pltpu.HBM)
        for x in (outer_gate, inner_gate, signal, cotangent, filters.T)
    ])
    recv = exchange(send)
    own = call(pick_kernel, two, "pick")(recv)
    f3 = swap(own, 6)
    tables_in = (w1, w2h, w2l, tw, v1)

    def spectra(first):
        return call(
            functools.partial(spectra_kernel, first=first),
            (shape(4, 2 * A, 2 * B), shape(4, 2 * A, 2 * B), shape(4, A, B)),
            "spectra",
            [pltpu.VMEM((4, A, 2 * B), F32)],
            (1_000_000_000, 2_000_000),
        )(recv, *tables_in)

    u1, g1, away = spectra(4)
    came = swap(away, 6)
    u0, g0, near = spectra(0)
    f3, near = lax.optimization_barrier((f3, near))
    far = swap(jnp.stack([own, f3]), 2)
    even = call(conv_even_kernel, buffer, "even", cost=(1_000_000_000, 2_000_000))(
        own, f3, u0, g0, u1, g1, *tables_in
    )
    keep, give = call(mix_kernel, (two, two), "mix")(near, came)
    came = swap(give, 2)
    odd = call(conv_odd_kernel, buffer, "odd", cost=(1_000_000_000, 2_000_000))(
        far, even, u0, g0, u1, g1, *tables_in
    )
    back_send = call(place_kernel, buffer, "place")(keep, came, odd)
    landed = exchange(back_send)
    *grads, fg = call(
        post_kernel,
        (shape(256, 512, dtype=BF), shape(256, 512, dtype=BF), shape(256, 512, dtype=BF), shape(64, 256)),
        "post",
        [gate, gate, gate, pltpu.VMEM((64, 256), F32), pltpu.SemaphoreType.DMA((7,))],
        outs=[pl.BlockSpec(memory_space=pltpu.HBM)] * 4,
    )(landed, inner_gate, signal, cotangent)
    return (*grads, fg.T)


def solution(mesh):
    spec = P("seq", "chan")
    return jax.shard_map(
        body, mesh=mesh, in_specs=(spec,) * 5, out_specs=(spec,) * 4, check_vma=False
    )
```

time: 77.1 us -> 75.5 us (0.979)
  starting transfers between devices: 13 us -> 10.8 us
    ppermute x6 -> x4, starting transfers between devices: 13 us -> 10.8 us  [swap(): return lax.ppermute(x, 'chan', [(z, z ^ distance) for z in range(8)])]
    pallas_call x4 -> x6, Pallas kernels: 6.32 us -> 6.78 us  [the longest x2 2.76 us: spectra(): call(functools.partial(spectra_kernel, first=first), (shape(4, 2 * A, 2 *...]
    ppermute x6 -> x4, waiting for transfers between devices: 2.33 us -> 1.97 us  [swap(): return lax.ppermute(x, 'chan', [(z, z ^ distance) for z in range(8)])]
  transfers between devices with their start and end apart: 6 -> 4, of which waited for: 2 -> 2; matrix products, arithmetic and copies ran while one was open for 0% -> 0% of each run, Pallas kernels for 8% -> 9%
where the time goes in v3:
time: 75.5 us; the launch traced here: 75.3 us
  blocking collectives  52.2 us (69%)
  starting transfers between devices  10.8 us (14%)
  Pallas kernels  9.49 us (13%)
  waiting for transfers between devices  1.97 us (3%)
  between operations  0.76 us (1%)
    all_to_all x2, blocking collectives, exchange(): lax.all_to_all(x, ('seq', 'chan'), 0, 0, axis_index_groups=PAIRS, tiled=T...  52.2 us
    ppermute x4, starting transfers between devices, swap(): return lax.ppermute(x, 'chan', [(z, z ^ distance) for z in range(8)])  10.8 us
    pallas_call x2, Pallas kernels, spectra(): call(functools.partial(spectra_kernel, first=first), (shape(4, 2 * A, 2 *...  2.76 us
    ppermute x4, waiting for transfers between devices, swap(): return lax.ppermute(x, 'chan', [(z, z ^ distance) for z in range(8)])  1.97 us
    pallas_call x1, Pallas kernels, body(): call(conv_odd_kernel, buffer, 'odd', cost=(1000000000, 2000000))  1.96 us
    pallas_call x1, Pallas kernels, body(): call(conv_even_kernel, buffer, 'even', cost=(1000000000, 2000000))  1.96 us
    pallas_call x1, Pallas kernels, body(): call(prep_kernel, buffer, 'prep', [gate, gate, gate, gate, pltpu.VMEM((64...  1.6 us
  transfers between devices with their start and end apart: 4, of which 2 were waited for; matrix products, arithmetic and copies ran while one was open for 0% of the time, Pallas kernels for 9%

profile of v3, /device:TPU:1, one launch (start us, length us, event | category | flops | bytes accessed | tf_op | source)
XLA Modules:
  0.0 75.3 jit_solution(5143548338695108711)
XLA Ops:
  0.6 1.6 %prep.1 = f32[2176,128]{1,0:T(8,128)S(1)} custom-call(bf16[256,512]{1,0:T(8,128)(2,1)} %outer_hbm.1, bf16[256,512]{1,0:T(8,128)(2,1)} %inner_ref.1, bf16[256,512]{1,0:T(8,128)(2,1)} %signal_ref.1, bf16[256,512]{1,0:T(8,128)(2,1)} %cot_ref.1, f32[64,256]{1,0:T(8,128)} %bitcast.16), custom_call_target="tpu_custom_call" | custom-call | tf_op jit(solution)/shard_map/prep/pallas_call | solution.py:288
  2.2 27.1 %all_to_all.18 = f32[64,1,4352]{2,1,0:T(1,128)S(1)} all-to-all(f32[64,1,4352]{2,1,0:T(1,128)S(1)} %bitcast.12), channel_id=1, replica_groups={{88,176,80,16,128,112,224,208,160,104,192,40,136,64,240,200,184,8,248,4..., dimensions={0} | all-to-all | bytes 2228224 | tf_op jit(solution)/shard_map/all_to_all | solution.py:275
  29.3 0.0 copy-start.3
  29.3 0.0 copy-start.4
  29.3 0.0 copy-start.5
  29.3 0.0 copy-start.7
  29.3 5.2 %collective-permute-start = (f32[2,64,128]{2,1,0:T(8,128)S(1)}, f32[2,64,128]{2,1,0:T(8,128)S(1)}, u32[]{:S(2)}, u32[]{:S(2)}) collective-permute-start(f32[2,64,128]{2,1,0:T(8,128)S(1)} %pick.1.own_ref), channel_id=1, source_target_pairs={{0,6},{1,7},{2,4},{3,5},{4,2},{5,3},{6,0},{7,1},{8,14},{9,15},{10,... | collective-permute-start | bytes 196616 | tf_op jit(solution)/shard_map/ppermute | solution.py:280
  34.5 0.0 copy-done.3
  34.5 0.0 copy-done.4
  34.5 0.0 copy-done.5
  34.5 0.0 copy-done.6
  34.6 0.0 copy-done.7
  34.6 1.4 %spectra.3 = (f32[4,128,256]{2,1,0:T(8,128)S(1)}, f32[4,128,256]{2,1,0:T(8,128)S(1)}, f32[4,64,128]{2,1,0:T(8,128)S(1)}) custom-call(f32[2176,128]{1,0:T(8,128)S(1)} %bitcast.9, bf16[128,192]{1,0:T(8,128)(2,1)S(1)} %copy-done.6, bf16[256,256]{1,0:T(8,128)(2,1)S(1)} %copy-done.4, bf16[256,256]{1,0:T(8,128)(2,1)S(1)} %copy-done.3, ...), custom_call_target="tpu_custom_call" | custom-call | flops 1000000000 | bytes 2000000 | tf_op jit(solution)/shard_map/spectra/pallas_call | solution.py:302
  36.0 0.9 %collective-permute-start.1 = (f32[4,64,128]{2,1,0:T(8,128)S(1)}, f32[4,64,128]{2,1,0:T(8,128)S(1)}, u32[]{:S(2)}, u32[]{:S(2)}) collective-permute-start(f32[4,64,128]{2,1,0:T(8,128)S(1)} %get-tuple-element.20), channel_id=1, source_target_pairs={{0,6},{1,7},{2,4},{3,5},{4,2},{5,3},{6,0},{7,1},{8,14},{9,15},{10,... | collective-permute-start | bytes 393224 | tf_op jit(solution)/shard_map/ppermute | solution.py:280
  36.9 1.4 %spectra.2 = (f32[4,128,256]{2,1,0:T(8,128)S(1)}, f32[4,128,256]{2,1,0:T(8,128)S(1)}, f32[4,64,128]{2,1,0:T(8,128)S(1)}) custom-call(f32[2176,128]{1,0:T(8,128)S(1)} %bitcast.10, bf16[128,192]{1,0:T(8,128)(2,1)S(1)} %copy-done.6, bf16[256,256]{1,0:T(8,128)(2,1)S(1)} %copy-done.4, bf16[256,256]{1,0:T(8,128)(2,1)S(1)} %copy-done.3, ...), custom_call_target="tpu_custom_call" | custom-call | flops 1000000000 | bytes 2000000 | tf_op jit(solution)/shard_map/spectra/pallas_call | solution.py:302
  38.3 0.0 collective-permute-done.f3_ref
  38.3 1.3 %collective-permute-start.3 = (f32[2,2,64,128]{3,2,1,0:T(8,128)S(1)}, f32[2,2,64,128]{3,2,1,0:T(8,128)S(1)}, u32[]{:S(2)}, u32[]{:S(2)}) collective-permute-start(f32[2,2,64,128]{3,2,1,0:T(8,128)S(1)} %pad_maximum_fusion), channel_id=1, source_target_pairs={{0,2},{1,3},{2,0},{3,1},{4,6},{5,7},{6,4},{7,5},{8,10},{9,11},{10,... | collective-permute-start | bytes 393224 | tf_op jit(solution)/shard_map/ppermute | solution.py:280
  39.6 2.0 %even.1.base_ref = f32[2176,128]{1,0:T(8,128)S(1)} custom-call(f32[2,64,128]{2,1,0:T(8,128)S(1)} %pick.1.own_ref, f32[2,64,128]{2,1,0:T(8,128)S(1)} %collective-permute-done.f3_ref, f32[4,128,256]{2,1,0:T(8,128)S(1)} %get-tuple-element.24.u0_ref, f32[4,128,256]{2,1,0:T(8,128)S(1)} %get-tuple-element.25.g0_ref, f32[4,128,256]{2,1,0:T(8,128)S(1)} %get-tuple-element.26.u1_ref, ...), custom_call_target="tpu_custom_call" | custom-call | flops 1000000000 | bytes 2000000 | tf_op jit(solution)/shard_map/even/pallas_call | solution.py:315
  41.5 1.5 %collective-permute-done.1.came_ref = f32[4,64,128]{2,1,0:T(8,128)S(1)} collective-permute-done((f32[4,64,128]{2,1,0:T(8,128)S(1)}, f32[4,64,128]{2,1,0:T(8,128)S(1)}, u32[]{:S(2)}, u32[]{:S(2)}) %collective-permute-start.1) | collective-permute-done | bytes 131104 | tf_op jit(solution)/shard_map/ppermute | solution.py:280
  43.1 3.4 %collective-permute-start.2 = (f32[2,64,128]{2,1,0:T(8,128)S(1)}, f32[2,64,128]{2,1,0:T(8,128)S(1)}, u32[]{:S(2)}, u32[]{:S(2)}) collective-permute-start(f32[2,64,128]{2,1,0:T(8,128)S(1)} %get-tuple-element.22), channel_id=1, source_target_pairs={{0,2},{1,3},{2,0},{3,1},{4,6},{5,7},{6,4},{7,5},{8,10},{9,11},{10,... | collective-permute-start | bytes 196616 | tf_op jit(solution)/shard_map/ppermute | solution.py:280
  46.5 0.0 collective-permute-done.3.far_ref
  46.5 2.0 %odd.1.base_ref = f32[2176,128]{1,0:T(8,128)S(1)} custom-call(f32[2,2,64,128]{3,2,1,0:T(8,128)S(1)} %collective-permute-done.3.far_ref, f32[2176,128]{1,0:T(8,128)S(1)} %even.1.base_ref, f32[4,128,256]{2,1,0:T(8,128)S(1)} %get-tuple-element.24.u0_ref, f32[4,128,256]{2,1,0:T(8,128)S(1)} %get-tuple-element.25.g0_ref, ...), custom_call_target="tpu_custom_call" | custom-call | flops 1000000000 | bytes 2000000 | tf_op jit(solution)/shard_map/odd/pallas_call | solution.py:320
  48.5 0.4 collective-permute-done.2.came_ref
  48.9 0.1 place.1
  49.0 0.0 copy-start
  49.0 0.0 copy-start.1
  49.0 0.0 copy-start.2
  49.0 25.1 %all_to_all.19 = f32[64,1,4352]{2,1,0:T(1,128)S(1)} all-to-all(f32[64,1,4352]{2,1,0:T(1,128)S(1)} %bitcast.11), channel_id=1, replica_groups={{88,176,80,16,128,112,224,208,160,104,192,40,136,64,240,200,184,8,248,4..., dimensions={0} | all-to-all | bytes 2228224 | tf_op jit(solution)/shard_map/all_to_all | solution.py:275
  74.2 0.0 copy-done
  74.2 0.0 copy-done.1
  74.2 0.0 copy-done.2
  74.2 1.1 %post.1 = (bf16[256,512]{1,0:T(8,128)(2,1)}, bf16[256,512]{1,0:T(8,128)(2,1)}, bf16[256,512]{1,0:T(8,128)(2,1)}, f32[64,256]{1,0:T(8,128)}) custom-call(f32[2176,128]{1,0:T(8,128)S(1)} %bitcast.13, bf16[256,512]{1,0:T(8,128)(2,1)S(1)} %copy-done, bf16[256,512]{1,0:T(8,128)(2,1)S(1)} %copy-done.1, bf16[256,512]{1,0:T(8,128)(2,1)S(1)} %copy-done.2), custom_call_target="tpu_custom_call" | custom-call | tf_op jit(solution)/shard_map/post/pallas_call | solution.py:325
  (4 shorter events, 0.0 us)
Async XLA Ops:
  29.3 5.2 %copy-start.3 = (bf16[256,256]{1,0:T(8,128)(2,1)S(1)}, bf16[256,256]{1,0:T(8,128)(2,1)}, u32[]{:S(2)}) copy-start(bf16[256,256]{1,0:T(8,128)(2,1)} %constant.12.clone.w2l_ref) | copy-start | bytes 393220
  29.3 5.2 %copy-start.4 = (bf16[256,256]{1,0:T(8,128)(2,1)S(1)}, bf16[256,256]{1,0:T(8,128)(2,1)}, u32[]{:S(2)}) copy-start(bf16[256,256]{1,0:T(8,128)(2,1)} %constant.11.clone.w2h_ref) | copy-start | bytes 393220
  29.3 5.2 %copy-start.5 = (f32[2,64,128]{2,1,0:T(8,128)S(1)}, f32[2,64,128]{2,1,0:T(8,128)}, u32[]{:S(2)}) copy-start(f32[2,64,128]{2,1,0:T(8,128)} %constant.13.clone.tw_ref) | copy-start | bytes 196612
  29.3 5.2 %copy-start.6 = (bf16[128,192]{1,0:T(8,128)(2,1)S(1)}, bf16[128,192]{1,0:T(8,128)(2,1)}, u32[]{:S(2)}) copy-start(bf16[128,192]{1,0:T(8,128)(2,1)} %constant.10.clone.w1_ref) | copy-start | bytes 147460
  29.3 5.3 %copy-start.7 = (bf16[64,384]{1,0:T(8,128)(2,1)S(1)}, bf16[64,384]{1,0:T(8,128)(2,1)}, u32[]{:S(2)}) copy-start(bf16[64,384]{1,0:T(8,128)(2,1)} %constant.14.clone.v1_ref) | copy-start | bytes 147460
  29.3 8.9 %collective-permute-start = (f32[2,64,128]{2,1,0:T(8,128)S(1)}, f32[2,64,128]{2,1,0:T(8,128)S(1)}, u32[]{:S(2)}, u32[]{:S(2)}) collective-permute-start(f32[2,64,128]{2,1,0:T(8,128)S(1)} %pick.1.own_ref), channel_id=1, source_target_pairs={{0,6},{1,7},{2,4},{3,5},{4,2},{5,3},{6,0},{7,1},{8,14},{9,15},{10,... | collective-permute-start | bytes 196616 | tf_op jit(solution)/shard_map/ppermute | solution.py:280
  36.0 7.1 %collective-permute-start.1 = (f32[4,64,128]{2,1,0:T(8,128)S(1)}, f32[4,64,128]{2,1,0:T(8,128)S(1)}, u32[]{:S(2)}, u32[]{:S(2)}) collective-permute-start(f32[4,64,128]{2,1,0:T(8,128)S(1)} %get-tuple-element.20), channel_id=1, source_target_pairs={{0,6},{1,7},{2,4},{3,5},{4,2},{5,3},{6,0},{7,1},{8,14},{9,15},{10,... | collective-permute-start | bytes 393224 | tf_op jit(solution)/shard_map/ppermute | solution.py:280
  38.3 8.2 %collective-permute-start.3 = (f32[2,2,64,128]{3,2,1,0:T(8,128)S(1)}, f32[2,2,64,128]{3,2,1,0:T(8,128)S(1)}, u32[]{:S(2)}, u32[]{:S(2)}) collective-permute-start(f32[2,2,64,128]{3,2,1,0:T(8,128)S(1)} %pad_maximum_fusion), channel_id=1, source_target_pairs={{0,2},{1,3},{2,0},{3,1},{4,6},{5,7},{6,4},{7,5},{8,10},{9,11},{10,... | collective-permute-start | bytes 393224 | tf_op jit(solution)/shard_map/ppermute | solution.py:280
  43.1 5.8 %collective-permute-start.2 = (f32[2,64,128]{2,1,0:T(8,128)S(1)}, f32[2,64,128]{2,1,0:T(8,128)S(1)}, u32[]{:S(2)}, u32[]{:S(2)}) collective-permute-start(f32[2,64,128]{2,1,0:T(8,128)S(1)} %get-tuple-element.22), channel_id=1, source_target_pairs={{0,2},{1,3},{2,0},{3,1},{4,6},{5,7},{6,4},{7,5},{8,10},{9,11},{10,... | collective-permute-start | bytes 196616 | tf_op jit(solution)/shard_map/ppermute | solution.py:280
  49.0 25.2 %copy-start = (bf16[256,512]{1,0:T(8,128)(2,1)S(1)}, bf16[256,512]{1,0:T(8,128)(2,1)}, u32[]{:S(2)}) copy-start(bf16[256,512]{1,0:T(8,128)(2,1)} %inner_ref.1) | copy-start | bytes 786436
  49.0 25.2 %copy-start.1 = (bf16[256,512]{1,0:T(8,128)(2,1)S(1)}, bf16[256,512]{1,0:T(8,128)(2,1)}, u32[]{:S(2)}) copy-start(bf16[256,512]{1,0:T(8,128)(2,1)} %signal_ref.1) | copy-start | bytes 786436
  49.0 25.2 %copy-start.2 = (bf16[256,512]{1,0:T(8,128)(2,1)S(1)}, bf16[256,512]{1,0:T(8,128)(2,1)}, u32[]{:S(2)}) copy-start(bf16[256,512]{1,0:T(8,128)(2,1)} %cot_ref.1) | copy-start | bytes 786436

commit v4 on v3

--- a/solution.py
+++ b/solution.py
@@ -19,7 +19,7 @@
 SHARDS = 32
 MEMBERS = 64
 ROWS = 34
-SCATTER = np.random.RandomState(0).permutation(SHARDS)
+SCATTER = np.random.RandomState(3).permutation(SHARDS)
 VMEM_LIMIT = 16 * 1024 * 1024
 
 
@@ -141,9 +141,9 @@
 
 
 def spectra_kernel(recv_ref, w1_ref, w2h_ref, w2l_ref, tw_ref, v1_ref, u_ref, g_ref, fg_ref,
-                   prod_ref, *, first):
+                   prod_ref, *, first, count):
     c, s = tw_ref[0], tw_ref[1]
-    for f in range(4):
+    for f in range(count):
         columns = [gather_rows(recv_ref, q, first + f + base, 8) for base in (0, 16) for q in range(2)]
         spec = forward(columns, w1_ref[...], w2h_ref[...], w2l_ref[...], c, s)
         u_ref[f] = spec[: 2 * A]
@@ -153,61 +153,63 @@
         pr = gr * ur + gi * ui
         pi = gi * ur - gr * ui
         prod_ref[f] = jnp.concatenate([pi[:A] + pi[A:], pr[:A] + pr[A:]], axis=1)
-    high, low = split(prod_ref[...].reshape(4 * A, 2 * B))
+    high, low = split(prod_ref[...].reshape(count * A, 2 * B))
     mid = dot(high, w2h_ref[...]) + dot(low, w2h_ref[...]) + dot(high, w2l_ref[...])
-    out = last_stage([mid[i * A : (i + 1) * A] for i in range(4)], v1_ref[...], c, s)
-    for i in range(4):
+    out = last_stage([mid[i * A : (i + 1) * A] for i in range(count)], v1_ref[...], c, s)
+    for i in range(count):
         fg_ref[i] = out[:, i * B : (i + 1) * B]
 
 
-def mix_kernel(near_ref, came_ref, keep_ref, give_ref):
-    keep_ref[...] = near_ref[0:2] + came_ref[2:4]
-    give_ref[...] = near_ref[2:4] + came_ref[0:2]
+def mix_kernel(near_ref, came_ref, give_ref):
+    give_ref[...] = near_ref[2:4] + came_ref[...]
 
 
 def conv_part(ks, filts, u_refs, g_refs, w1, w2h, w2l, tw_ref, v1, out_ref):
     c, s = tw_ref[0], tw_ref[1]
     spec = forward([filt[q] for filt in filts for q in range(2)], w1, w2h, w2l, c, s)
+    prods, places = [], []
     for j, k in enumerate(ks):
         for e in range(2):
             f = 2 * k + e
-            u_ref, g_ref, at = u_refs[k // 2], g_refs[k // 2], f % 4
+            u_ref, g_ref, at = u_refs[k], g_refs[k], f % (2 if k > 1 else 4)
             h_spec = spec[(2 * j + e) * A : (2 * j + e + 1) * A]
             hr, hi = h_spec[:, :B], h_spec[:, B:]
-            prods = []
             for q in range(2):
                 ur, ui = u_ref[at, q * A : (q + 1) * A, :B], u_ref[at, q * A : (q + 1) * A, B:]
                 prods.append((hr * ui + hi * ur, hr * ur - hi * ui))
+                places.append((q, f))
             for q in range(2):
                 gr, gi = g_ref[at, q * A : (q + 1) * A, :B], g_ref[at, q * A : (q + 1) * A, B:]
                 prods.append((gi * hr - gr * hi, gr * hr + gi * hi))
-            mid = second_stage(prods, w2h, w2l)
-            out = last_stage([mid[i * A : (i + 1) * A] for i in range(4)], v1, c, s)
-            for i in range(4):
-                q, base = i % 2, (i // 2) * 16
-                for h in range(2):
-                    out_ref[pl.ds(q * 32 * ROWS + base + 8 * h + f, 32, stride=ROWS), :] = (
-                        out[h * 32 : (h + 1) * 32, i * B : (i + 1) * B]
-                    )
-
-
-def conv_even_kernel(own_ref, f3_ref, u0_ref, g0_ref, u1_ref, g1_ref, w1_ref, w2h_ref, w2l_ref, tw_ref, v1_ref,
+                places.append((q, 16 + f))
+    mid = second_stage(prods, w2h, w2l)
+    for n in range(0, 16, 4):
+        out = last_stage([mid[i * A : (i + 1) * A] for i in range(n, n + 4)], v1, c, s)
+        for i in range(4):
+            q, row = places[n + i]
+            for h in range(2):
+                out_ref[pl.ds(q * 32 * ROWS + row + 8 * h, 32, stride=ROWS), :] = (
+                    out[h * 32 : (h + 1) * 32, i * B : (i + 1) * B]
+                )
+
+
+def conv_even_kernel(own_ref, f3_ref, u0_ref, g0_ref, u2_ref, g2_ref, u3_ref, g3_ref, w1_ref, w2h_ref, w2l_ref, tw_ref, v1_ref,
                      out_ref):
-    conv_part((0, 3), (own_ref, f3_ref), (u0_ref, u1_ref), (g0_ref, g1_ref), w1_ref[...], w2h_ref[...], w2l_ref[...], tw_ref,
+    conv_part((0, 3), (own_ref, f3_ref), (u0_ref, u0_ref, u2_ref, u3_ref), (g0_ref, g0_ref, g2_ref, g3_ref), w1_ref[...], w2h_ref[...], w2l_ref[...], tw_ref,
               v1_ref[...], out_ref)
 
 
-def conv_odd_kernel(far_ref, base_ref, u0_ref, g0_ref, u1_ref, g1_ref, w1_ref, w2h_ref, w2l_ref,
+def conv_odd_kernel(far_ref, base_ref, u0_ref, g0_ref, u2_ref, g2_ref, u3_ref, g3_ref, w1_ref, w2h_ref, w2l_ref,
                     tw_ref, v1_ref, out_ref):
     out_ref[...] = base_ref[...]
-    conv_part((1, 2), (far_ref.at[0], far_ref.at[1]), (u0_ref, u1_ref), (g0_ref, g1_ref), w1_ref[...], w2h_ref[...],
+    conv_part((1, 2), (far_ref.at[0], far_ref.at[1]), (u0_ref, u0_ref, u2_ref, u3_ref), (g0_ref, g0_ref, g2_ref, g3_ref), w1_ref[...], w2h_ref[...],
               w2l_ref[...], tw_ref, v1_ref[...], out_ref)
 
 
-def place_kernel(keep_ref, came_ref, base_ref, out_ref):
+def place_kernel(near_ref, fg3_ref, came_ref, base_ref, out_ref):
     out_ref[...] = base_ref[...]
     for q in range(2):
-        total = keep_ref[q] + came_ref[q]
+        total = near_ref[q] + fg3_ref[q] + came_ref[q]
         for h in range(2):
             out_ref[pl.ds(q * 32 * ROWS + 32 + h, 32, stride=ROWS), :] = total[h * 32 : (h + 1) * 32]
 
@@ -250,7 +252,7 @@
         copy.wait()
 
 
-def call(kernel, out_shapes, name, scratch=(), cost=(0, 0), ins=None, outs=None):
+def call(kernel, out_shapes, name, scratch=(), cost=(1000, 1000), ins=None, outs=None):
     return pl.pallas_call(
         kernel,
         out_shape=out_shapes,
@@ -298,29 +300,32 @@
     f3 = swap(own, 6)
     tables_in = (w1, w2h, w2l, tw, v1)
 
-    def spectra(first):
+    def spectra(recv, first, count):
         return call(
-            functools.partial(spectra_kernel, first=first),
-            (shape(4, 2 * A, 2 * B), shape(4, 2 * A, 2 * B), shape(4, A, B)),
+            functools.partial(spectra_kernel, first=first, count=count),
+            (shape(count, 2 * A, 2 * B), shape(count, 2 * A, 2 * B), shape(count, A, B)),
             "spectra",
-            [pltpu.VMEM((4, A, 2 * B), F32)],
-            (1_000_000_000, 2_000_000),
+            [pltpu.VMEM((count, A, 2 * B), F32)],
+            (1000, 1000),
         )(recv, *tables_in)
 
-    u1, g1, away = spectra(4)
-    came = swap(away, 6)
-    u0, g0, near = spectra(0)
+    u2, g2, fg2 = spectra(recv, 4, 2)
+    relay = swap(fg2, 6)
+    recv, fg2 = lax.optimization_barrier((recv, fg2))
+    u3, g3, fg3 = spectra(recv, 6, 2)
+    fg3 = swap(fg3, 6)
+    recv, g3 = lax.optimization_barrier((recv, g3))
+    u0, g0, near = spectra(recv, 0, 4)
     f3, near = lax.optimization_barrier((f3, near))
     far = swap(jnp.stack([own, f3]), 2)
-    even = call(conv_even_kernel, buffer, "even", cost=(1_000_000_000, 2_000_000))(
-        own, f3, u0, g0, u1, g1, *tables_in
-    )
-    keep, give = call(mix_kernel, (two, two), "mix")(near, came)
-    came = swap(give, 2)
-    odd = call(conv_odd_kernel, buffer, "odd", cost=(1_000_000_000, 2_000_000))(
-        far, even, u0, g0, u1, g1, *tables_in
-    )
-    back_send = call(place_kernel, buffer, "place")(keep, came, odd)
+    even = call(conv_even_kernel, buffer, "even", cost=(1000, 1000))(
+        own, f3, u0, g0, u2, g2, u3, g3, *tables_in
+    )
+    came = swap(call(mix_kernel, two, "mix")(near, relay), 2)
+    odd = call(conv_odd_kernel, buffer, "odd", cost=(1000, 1000))(
+        far, even, u0, g0, u2, g2, u3, g3, *tables_in
+    )
+    back_send = call(place_kernel, buffer, "place")(near, fg3, came, odd)
     landed = exchange(back_send)
     *grads, fg = call(
         post_kernel,

time: 75.5 us -> 73.3 us (0.971)
  blocking collectives: 52.2 us -> 49.7 us
    all_to_all x2, blocking collectives: 52.2 us -> 49.7 us  [exchange(): lax.all_to_all(x, ('seq', 'chan'), 0, 0, axis_index_groups=PAIRS, tiled=T...]
    ppermute x4 -> x5, starting transfers between devices: 10.8 us -> 11.5 us  [swap(): return lax.ppermute(x, 'chan', [(z, z ^ distance) for z in range(8)])]
    ppermute x4 -> x5, waiting for transfers between devices: 1.97 us -> 1.74 us  [swap(): return lax.ppermute(x, 'chan', [(z, z ^ distance) for z in range(8)])]
    pallas_call x6 -> x7, Pallas kernels: 6.78 us -> 6.65 us  [the longest x3 3.19 us: spectra(): call(functools.partial(spectra_kernel, first=first, count=count), (shape(...]
  transfers between devices with their start and end apart: 4 -> 5, of which waited for: 2 -> 2; matrix products, arithmetic and copies ran while one was open for 0% -> 0% of each run, Pallas kernels for 9% -> 9%
where the time goes in v4:
time: 73.3 us; the launch traced here: 73.1 us
  blocking collectives  49.7 us (68%)
  starting transfers between devices  11.5 us (16%)
  Pallas kernels  9.37 us (13%)
  waiting for transfers between devices  1.74 us (2%)
  between operations  0.77 us (1%)
    all_to_all x2, blocking collectives, exchange(): lax.all_to_all(x, ('seq', 'chan'), 0, 0, axis_index_groups=PAIRS, tiled=T...  49.7 us
    ppermute x5, starting transfers between devices, swap(): return lax.ppermute(x, 'chan', [(z, z ^ distance) for z in range(8)])  11.5 us
    pallas_call x3, Pallas kernels, spectra(): call(functools.partial(spectra_kernel, first=first, count=count), (shape(...  3.19 us
    ppermute x5, waiting for transfers between devices, swap(): return lax.ppermute(x, 'chan', [(z, z ^ distance) for z in range(8)])  1.74 us
    pallas_call x1, Pallas kernels, body(): call(conv_odd_kernel, buffer, 'odd', cost=(1000, 1000))  1.7 us
    pallas_call x1, Pallas kernels, body(): call(conv_even_kernel, buffer, 'even', cost=(1000, 1000))  1.66 us
    pallas_call x1, Pallas kernels, body(): call(prep_kernel, buffer, 'prep', [gate, gate, gate, gate, pltpu.VMEM((64...  1.6 us
  transfers between devices with their start and end apart: 5, of which 2 were waited for; matrix products, arithmetic and copies ran while one was open for 0% of the time, Pallas kernels for 9%

profile of v4, /device:TPU:1, one launch (start us, length us, event | category | flops | bytes accessed | tf_op | source)
XLA Modules:
  0.0 73.1 jit_solution(1384472983355813818)
XLA Ops:
  0.6 1.6 %prep.1 = f32[2176,128]{1,0:T(8,128)S(1)} custom-call(bf16[256,512]{1,0:T(8,128)(2,1)} %outer_hbm.1, bf16[256,512]{1,0:T(8,128)(2,1)} %inner_ref.1, bf16[256,512]{1,0:T(8,128)(2,1)} %signal_ref.1, bf16[256,512]{1,0:T(8,128)(2,1)} %cot_ref.1, f32[64,256]{1,0:T(8,128)} %bitcast.17), custom_call_target="tpu_custom_call" | custom-call | flops 1000 | bytes 1000 | tf_op jit(solution)/shard_map/prep/pallas_call | solution.py:290
  2.2 25.6 %all_to_all.18 = f32[64,1,4352]{2,1,0:T(1,128)S(1)} all-to-all(f32[64,1,4352]{2,1,0:T(1,128)S(1)} %bitcast.13), channel_id=1, replica_groups={{160,136,40,112,224,216,32,120,16,144,128,8,184,208,56,104,96,232,48,17..., dimensions={0} | all-to-all | bytes 2228224 | tf_op jit(solution)/shard_map/all_to_all | solution.py:277
  27.8 0.0 copy-start.4
  27.9 5.2 %collective-permute-start = (f32[2,64,128]{2,1,0:T(8,128)S(1)}, f32[2,64,128]{2,1,0:T(8,128)S(1)}, u32[]{:S(2)}, u32[]{:S(2)}) collective-permute-start(f32[2,64,128]{2,1,0:T(8,128)S(1)} %pick.1.own_ref), channel_id=1, source_target_pairs={{0,6},{1,7},{2,4},{3,5},{4,2},{5,3},{6,0},{7,1},{8,14},{9,15},{10,... | collective-permute-start | bytes 196616 | tf_op jit(solution)/shard_map/ppermute | solution.py:282
  33.1 0.0 copy-done
  33.1 0.0 copy-done.1
  33.1 0.0 copy-done.2
  33.1 0.0 copy-done.3
  33.1 0.0 copy-done.4
  33.1 0.9 %spectra.3 = (f32[2,128,256]{2,1,0:T(8,128)S(1)}, f32[2,128,256]{2,1,0:T(8,128)S(1)}, f32[2,64,128]{2,1,0:T(8,128)S(1)}) custom-call(f32[2176,128]{1,0:T(8,128)S(1)} %bitcast.9, bf16[128,192]{1,0:T(8,128)(2,1)S(1)} %copy-done.3, bf16[256,256]{1,0:T(8,128)(2,1)S(1)} %copy-done.1, bf16[256,256]{1,0:T(8,128)(2,1)S(1)} %copy-done, f32[2,64,128]{2,1,0:T(8,128)S(1)} %copy-done.2, ...), custom_call_target="tpu_custom_call" | custom-call | flops 1000 | bytes 1000 | tf_op jit(solution)/shard_map/spectra/pallas_call | solution.py:304
  34.0 0.9 %collective-permute-start.2 = (f32[2,64,128]{2,1,0:T(8,128)S(1)}, f32[2,64,128]{2,1,0:T(8,128)S(1)}, u32[]{:S(2)}, u32[]{:S(2)}) collective-permute-start(f32[2,64,128]{2,1,0:T(8,128)S(1)} %get-tuple-element.22), channel_id=1, source_target_pairs={{0,6},{1,7},{2,4},{3,5},{4,2},{5,3},{6,0},{7,1},{8,14},{9,15},{10,... | collective-permute-start | bytes 196616 | tf_op jit(solution)/shard_map/ppermute | solution.py:282
  34.9 0.9 %spectra.4 = (f32[2,128,256]{2,1,0:T(8,128)S(1)}, f32[2,128,256]{2,1,0:T(8,128)S(1)}, f32[2,64,128]{2,1,0:T(8,128)S(1)}) custom-call(f32[2176,128]{1,0:T(8,128)S(1)} %bitcast.10, bf16[128,192]{1,0:T(8,128)(2,1)S(1)} %copy-done.3, bf16[256,256]{1,0:T(8,128)(2,1)S(1)} %copy-done.1, bf16[256,256]{1,0:T(8,128)(2,1)S(1)} %copy-done, f32[2,64,128]{2,1,0:T(8,128)S(1)} %copy-done.2, ...), custom_call_target="tpu_custom_call" | custom-call | flops 1000 | bytes 1000 | tf_op jit(solution)/shard_map/spectra/pallas_call | solution.py:304
  35.8 1.4 %spectra.5 = (f32[4,128,256]{2,1,0:T(8,128)S(1)}, f32[4,128,256]{2,1,0:T(8,128)S(1)}, f32[4,64,128]{2,1,0:T(8,128)S(1)}) custom-call(f32[2176,128]{1,0:T(8,128)S(1)} %bitcast.11, bf16[128,192]{1,0:T(8,128)(2,1)S(1)} %copy-done.3, bf16[256,256]{1,0:T(8,128)(2,1)S(1)} %copy-done.1, bf16[256,256]{1,0:T(8,128)(2,1)S(1)} %copy-done, f32[2,64,128]{2,1,0:T(8,128)S(1)} %copy-done.2, ...), custom_call_target="tpu_custom_call" | custom-call | flops 1000 | bytes 1000 | tf_op jit(solution)/shard_map/spectra/pallas_call | solution.py:304
  37.2 0.0 collective-permute-done.f3_ref
  37.3 1.3 %collective-permute-start.4 = (f32[2,2,64,128]{3,2,1,0:T(8,128)S(1)}, f32[2,2,64,128]{3,2,1,0:T(8,128)S(1)}, u32[]{:S(2)}, u32[]{:S(2)}) collective-permute-start(f32[2,2,64,128]{3,2,1,0:T(8,128)S(1)} %pad_maximum_fusion), channel_id=1, source_target_pairs={{0,2},{1,3},{2,0},{3,1},{4,6},{5,7},{6,4},{7,5},{8,10},{9,11},{10,... | collective-permute-start | bytes 393224 | tf_op jit(solution)/shard_map/ppermute | solution.py:282
  38.5 2.7 %collective-permute-start.1 = (f32[2,64,128]{2,1,0:T(8,128)S(1)}, f32[2,64,128]{2,1,0:T(8,128)S(1)}, u32[]{:S(2)}, u32[]{:S(2)}) collective-permute-start(f32[2,64,128]{2,1,0:T(8,128)S(1)} %get-tuple-element.28), channel_id=1, source_target_pairs={{0,6},{1,7},{2,4},{3,5},{4,2},{5,3},{6,0},{7,1},{8,14},{9,15},{10,... | collective-permute-start | bytes 196616 | tf_op jit(solution)/shard_map/ppermute | solution.py:282
  41.2 0.0 collective-permute-done.2.came_ref
  41.3 1.4 %collective-permute-start.3 = (f32[2,64,128]{2,1,0:T(8,128)S(1)}, f32[2,64,128]{2,1,0:T(8,128)S(1)}, u32[]{:S(2)}, u32[]{:S(2)}) collective-permute-start(f32[2,64,128]{2,1,0:T(8,128)S(1)} %mix.1), channel_id=1, source_target_pairs={{0,2},{1,3},{2,0},{3,1},{4,6},{5,7},{6,4},{7,5},{8,10},{9,11},{10,... | collective-permute-start | bytes 196616 | tf_op jit(solution)/shard_map/ppermute | solution.py:282
  42.6 1.7 %even.1.base_ref = f32[2176,128]{1,0:T(8,128)S(1)} custom-call(f32[2,64,128]{2,1,0:T(8,128)S(1)} %pick.1.own_ref, f32[2,64,128]{2,1,0:T(8,128)S(1)} %collective-permute-done.f3_ref, f32[4,128,256]{2,1,0:T(8,128)S(1)} %get-tuple-element.30.u0_ref, f32[4,128,256]{2,1,0:T(8,128)S(1)} %get-tuple-element.31.g0_ref, f32[2,128,256]{2,1,0:T(8,128)S(1)} %get-tuple-element.32.u2_ref, ...), custom_call_target="tpu_custom_call" | custom-call | flops 1000 | bytes 1000 | tf_op jit(solution)/shard_map/even/pallas_call | solution.py:321
  44.3 0.6 collective-permute-done.4.far_ref
  44.8 1.7 %odd.1.base_ref = f32[2176,128]{1,0:T(8,128)S(1)} custom-call(f32[2,2,64,128]{3,2,1,0:T(8,128)S(1)} %collective-permute-done.4.far_ref, f32[2176,128]{1,0:T(8,128)S(1)} %even.1.base_ref, f32[4,128,256]{2,1,0:T(8,128)S(1)} %get-tuple-element.30.u0_ref, f32[4,128,256]{2,1,0:T(8,128)S(1)} %get-tuple-element.31.g0_ref, ...), custom_call_target="tpu_custom_call" | custom-call | flops 1000 | bytes 1000 | tf_op jit(solution)/shard_map/odd/pallas_call | solution.py:325
  46.6 0.0 collective-permute-done.1.fg3_ref
  46.6 1.2 %collective-permute-done.3.came_ref = f32[2,64,128]{2,1,0:T(8,128)S(1)} collective-permute-done((f32[2,64,128]{2,1,0:T(8,128)S(1)}, f32[2,64,128]{2,1,0:T(8,128)S(1)}, u32[]{:S(2)}, u32[]{:S(2)}) %collective-permute-start.3) | collective-permute-done | bytes 65568 | tf_op jit(solution)/shard_map/ppermute | solution.py:282
  47.7 0.1 place.1
  47.8 0.0 copy-start.5
  47.8 0.0 copy-start.6
  47.9 0.0 copy-start.7
  47.9 24.2 %all_to_all.19 = f32[64,1,4352]{2,1,0:T(1,128)S(1)} all-to-all(f32[64,1,4352]{2,1,0:T(1,128)S(1)} %bitcast.12), channel_id=1, replica_groups={{160,136,40,112,224,216,32,120,16,144,128,8,184,208,56,104,96,232,48,17..., dimensions={0} | all-to-all | bytes 2228224 | tf_op jit(solution)/shard_map/all_to_all | solution.py:277
  72.0 0.0 copy-done.5
  72.0 0.0 copy-done.6
  72.0 0.0 copy-done.7
  72.0 1.1 %post.1 = (bf16[256,512]{1,0:T(8,128)(2,1)}, bf16[256,512]{1,0:T(8,128)(2,1)}, bf16[256,512]{1,0:T(8,128)(2,1)}, f32[64,256]{1,0:T(8,128)}) custom-call(f32[2176,128]{1,0:T(8,128)S(1)} %bitcast.14, bf16[256,512]{1,0:T(8,128)(2,1)S(1)} %copy-done.5, bf16[256,512]{1,0:T(8,128)(2,1)S(1)} %copy-done.6, bf16[256,512]{1,0:T(8,128)(2,1)S(1)} %copy-done.7), custom_call_target="tpu_custom_call" | custom-call | flops 1000 | bytes 1000 | tf_op jit(solution)/shard_map/post/pallas_call | solution.py:330
  (7 shorter events, 0.0 us)
Async XLA Ops:
  27.8 5.2 %copy-start = (bf16[256,256]{1,0:T(8,128)(2,1)S(1)}, bf16[256,256]{1,0:T(8,128)(2,1)}, u32[]{:S(2)}) copy-start(bf16[256,256]{1,0:T(8,128)(2,1)} %constant.12.clone.w2l_ref) | copy-start | bytes 393220
  27.8 5.2 %copy-start.1 = (bf16[256,256]{1,0:T(8,128)(2,1)S(1)}, bf16[256,256]{1,0:T(8,128)(2,1)}, u32[]{:S(2)}) copy-start(bf16[256,256]{1,0:T(8,128)(2,1)} %constant.11.clone.w2h_ref) | copy-start | bytes 393220
  27.8 5.2 %copy-start.2 = (f32[2,64,128]{2,1,0:T(8,128)S(1)}, f32[2,64,128]{2,1,0:T(8,128)}, u32[]{:S(2)}) copy-start(f32[2,64,128]{2,1,0:T(8,128)} %constant.13.clone.tw_ref) | copy-start | bytes 196612
  27.8 5.2 %copy-start.3 = (bf16[128,192]{1,0:T(8,128)(2,1)S(1)}, bf16[128,192]{1,0:T(8,128)(2,1)}, u32[]{:S(2)}) copy-start(bf16[128,192]{1,0:T(8,128)(2,1)} %constant.10.clone.w1_ref) | copy-start | bytes 147460
  27.8 5.3 %copy-start.4 = (bf16[64,384]{1,0:T(8,128)(2,1)S(1)}, bf16[64,384]{1,0:T(8,128)(2,1)}, u32[]{:S(2)}) copy-start(bf16[64,384]{1,0:T(8,128)(2,1)} %constant.14.clone.v1_ref) | copy-start | bytes 147460
  27.9 9.4 %collective-permute-start = (f32[2,64,128]{2,1,0:T(8,128)S(1)}, f32[2,64,128]{2,1,0:T(8,128)S(1)}, u32[]{:S(2)}, u32[]{:S(2)}) collective-permute-start(f32[2,64,128]{2,1,0:T(8,128)S(1)} %pick.1.own_ref), channel_id=1, source_target_pairs={{0,6},{1,7},{2,4},{3,5},{4,2},{5,3},{6,0},{7,1},{8,14},{9,15},{10,... | collective-permute-start | bytes 196616 | tf_op jit(solution)/shard_map/ppermute | solution.py:282
  34.0 7.3 %collective-permute-start.2 = (f32[2,64,128]{2,1,0:T(8,128)S(1)}, f32[2,64,128]{2,1,0:T(8,128)S(1)}, u32[]{:S(2)}, u32[]{:S(2)}) collective-permute-start(f32[2,64,128]{2,1,0:T(8,128)S(1)} %get-tuple-element.22), channel_id=1, source_target_pairs={{0,6},{1,7},{2,4},{3,5},{4,2},{5,3},{6,0},{7,1},{8,14},{9,15},{10,... | collective-permute-start | bytes 196616 | tf_op jit(solution)/shard_map/ppermute | solution.py:282
  37.3 7.6 %collective-permute-start.4 = (f32[2,2,64,128]{3,2,1,0:T(8,128)S(1)}, f32[2,2,64,128]{3,2,1,0:T(8,128)S(1)}, u32[]{:S(2)}, u32[]{:S(2)}) collective-permute-start(f32[2,2,64,128]{3,2,1,0:T(8,128)S(1)} %pad_maximum_fusion), channel_id=1, source_target_pairs={{0,2},{1,3},{2,0},{3,1},{4,6},{5,7},{6,4},{7,5},{8,10},{9,11},{10,... | collective-permute-start | bytes 393224 | tf_op jit(solution)/shard_map/ppermute | solution.py:282
  38.5 8.0 %collective-permute-start.1 = (f32[2,64,128]{2,1,0:T(8,128)S(1)}, f32[2,64,128]{2,1,0:T(8,128)S(1)}, u32[]{:S(2)}, u32[]{:S(2)}) collective-permute-start(f32[2,64,128]{2,1,0:T(8,128)S(1)} %get-tuple-element.28), channel_id=1, source_target_pairs={{0,6},{1,7},{2,4},{3,5},{4,2},{5,3},{6,0},{7,1},{8,14},{9,15},{10,... | collective-permute-start | bytes 196616 | tf_op jit(solution)/shard_map/ppermute | solution.py:282
  41.3 6.5 %collective-permute-start.3 = (f32[2,64,128]{2,1,0:T(8,128)S(1)}, f32[2,64,128]{2,1,0:T(8,128)S(1)}, u32[]{:S(2)}, u32[]{:S(2)}) collective-permute-start(f32[2,64,128]{2,1,0:T(8,128)S(1)} %mix.1), channel_id=1, source_target_pairs={{0,2},{1,3},{2,0},{3,1},{4,6},{5,7},{6,4},{7,5},{8,10},{9,11},{10,... | collective-permute-start | bytes 196616 | tf_op jit(solution)/shard_map/ppermute | solution.py:282
  47.8 24.2 %copy-start.5 = (bf16[256,512]{1,0:T(8,128)(2,1)S(1)}, bf16[256,512]{1,0:T(8,128)(2,1)}, u32[]{:S(2)}) copy-start(bf16[256,512]{1,0:T(8,128)(2,1)} %inner_ref.1) | copy-start | bytes 786436
  47.8 24.2 %copy-start.6 = (bf16[256,512]{1,0:T(8,128)(2,1)S(1)}, bf16[256,512]{1,0:T(8,128)(2,1)}, u32[]{:S(2)}) copy-start(bf16[256,512]{1,0:T(8,128)(2,1)} %signal_ref.1) | copy-start | bytes 786436
  47.9 24.2 %copy-start.7 = (bf16[256,512]{1,0:T(8,128)(2,1)S(1)}, bf16[256,512]{1,0:T(8,128)(2,1)}, u32[]{:S(2)}) copy-start(bf16[256,512]{1,0:T(8,128)(2,1)} %cot_ref.1) | copy-start | bytes 786436

commit v5 on v4

--- a/solution.py
+++ b/solution.py
@@ -135,16 +135,19 @@
     )
 
 
-def pick_kernel(recv_ref, out_ref):
+def pick_kernel(recv_ref, w1_ref, w2h_ref, w2l_ref, tw_ref, v1_ref, out_ref):
     for q in range(2):
         out_ref[q] = gather_rows(recv_ref, q, 32, 1)
 
 
-def spectra_kernel(recv_ref, w1_ref, w2h_ref, w2l_ref, tw_ref, v1_ref, u_ref, g_ref, fg_ref,
-                   prod_ref, *, first, count):
+def spectra_kernel(recv_ref, w1_ref, w2h_ref, w2l_ref, tw_ref, v1_ref, u_ref, g_ref, *rest,
+                   channels):
     c, s = tw_ref[0], tw_ref[1]
-    for f in range(count):
-        columns = [gather_rows(recv_ref, q, first + f + base, 8) for base in (0, 16) for q in range(2)]
+    count = len(channels)
+    *fg_refs, prod_ref = rest
+    fg_places = [(ref, i) for ref in fg_refs for i in range(ref.shape[0])]
+    for f, channel in enumerate(channels):
+        columns = [gather_rows(recv_ref, q, channel + base, 8) for base in (0, 16) for q in range(2)]
         spec = forward(columns, w1_ref[...], w2h_ref[...], w2l_ref[...], c, s)
         u_ref[f] = spec[: 2 * A]
         g_ref[f] = spec[2 * A :]
@@ -157,21 +160,22 @@
     mid = dot(high, w2h_ref[...]) + dot(low, w2h_ref[...]) + dot(high, w2l_ref[...])
     out = last_stage([mid[i * A : (i + 1) * A] for i in range(count)], v1_ref[...], c, s)
     for i in range(count):
-        fg_ref[i] = out[:, i * B : (i + 1) * B]
+        fg_ref, place = fg_places[i]
+        fg_ref[place] = out[:, i * B : (i + 1) * B]
 
 
 def mix_kernel(near_ref, came_ref, give_ref):
     give_ref[...] = near_ref[2:4] + came_ref[...]
 
 
-def conv_part(ks, filts, u_refs, g_refs, w1, w2h, w2l, tw_ref, v1, out_ref):
+def conv_part(ks, filts, u_ref, g_ref, starts, w1, w2h, w2l, tw_ref, v1, out_ref):
     c, s = tw_ref[0], tw_ref[1]
     spec = forward([filt[q] for filt in filts for q in range(2)], w1, w2h, w2l, c, s)
     prods, places = [], []
     for j, k in enumerate(ks):
         for e in range(2):
             f = 2 * k + e
-            u_ref, g_ref, at = u_refs[k], g_refs[k], f % (2 if k > 1 else 4)
+            at = starts[j] + e
             h_spec = spec[(2 * j + e) * A : (2 * j + e + 1) * A]
             hr, hi = h_spec[:, :B], h_spec[:, B:]
             for q in range(2):
@@ -183,7 +187,7 @@
                 prods.append((gi * hr - gr * hi, gr * hr + gi * hi))
                 places.append((q, 16 + f))
     mid = second_stage(prods, w2h, w2l)
-    for n in range(0, 16, 4):
+    for n in range(0, len(prods), 4):
         out = last_stage([mid[i * A : (i + 1) * A] for i in range(n, n + 4)], v1, c, s)
         for i in range(4):
             q, row = places[n + i]
@@ -193,23 +197,22 @@
                 )
 
 
-def conv_even_kernel(own_ref, f3_ref, u0_ref, g0_ref, u2_ref, g2_ref, u3_ref, g3_ref, w1_ref, w2h_ref, w2l_ref, tw_ref, v1_ref,
-                     out_ref):
-    conv_part((0, 3), (own_ref, f3_ref), (u0_ref, u0_ref, u2_ref, u3_ref), (g0_ref, g0_ref, g2_ref, g3_ref), w1_ref[...], w2h_ref[...], w2l_ref[...], tw_ref,
+def conv_three_kernel(own_ref, fb_ref, fa_ref, u_ref, g_ref, w1_ref, w2h_ref, w2l_ref, tw_ref, v1_ref,
+                      out_ref):
+    conv_part((0, 1, 3), (own_ref, fb_ref, fa_ref), u_ref, g_ref, (2, 4, 0), w1_ref[...], w2h_ref[...],
+              w2l_ref[...], tw_ref, v1_ref[...], out_ref)
+
+
+def conv_last_kernel(far_ref, base_ref, u_ref, g_ref, w1_ref, w2h_ref, w2l_ref, tw_ref, v1_ref, out_ref):
+    out_ref[...] = base_ref[...]
+    conv_part((2,), (far_ref,), u_ref, g_ref, (0,), w1_ref[...], w2h_ref[...], w2l_ref[...], tw_ref,
               v1_ref[...], out_ref)
 
 
-def conv_odd_kernel(far_ref, base_ref, u0_ref, g0_ref, u2_ref, g2_ref, u3_ref, g3_ref, w1_ref, w2h_ref, w2l_ref,
-                    tw_ref, v1_ref, out_ref):
-    out_ref[...] = base_ref[...]
-    conv_part((1, 2), (far_ref.at[0], far_ref.at[1]), (u0_ref, u0_ref, u2_ref, u3_ref), (g0_ref, g0_ref, g2_ref, g3_ref), w1_ref[...], w2h_ref[...],
-              w2l_ref[...], tw_ref, v1_ref[...], out_ref)
-
-
-def place_kernel(near_ref, fg3_ref, came_ref, base_ref, out_ref):
+def place_kernel(near_ref, direct_ref, came_ref, base_ref, out_ref):
     out_ref[...] = base_ref[...]
     for q in range(2):
-        total = near_ref[q] + fg3_ref[q] + came_ref[q]
+        total = near_ref[q] + direct_ref[q] + came_ref[q]
         for h in range(2):
             out_ref[pl.ds(q * 32 * ROWS + 32 + h, 32, stride=ROWS), :] = total[h * 32 : (h + 1) * 32]
 
@@ -296,36 +299,34 @@
         for x in (outer_gate, inner_gate, signal, cotangent, filters.T)
     ])
     recv = exchange(send)
-    own = call(pick_kernel, two, "pick")(recv)
-    f3 = swap(own, 6)
     tables_in = (w1, w2h, w2l, tw, v1)
-
-    def spectra(recv, first, count):
+    own = call(pick_kernel, two, "pick")(recv, *tables_in)
+    fa, fb = swap(own, 6), swap(own, 2)
+    def spectra(recv, ks, sizes):
+        channels = [2 * k + e for k in ks for e in range(2)]
+        count = len(channels)
         return call(
-            functools.partial(spectra_kernel, first=first, count=count),
-            (shape(count, 2 * A, 2 * B), shape(count, 2 * A, 2 * B), shape(count, A, B)),
+            functools.partial(spectra_kernel, channels=channels),
+            (shape(count, 2 * A, 2 * B), shape(count, 2 * A, 2 * B))
+            + tuple(shape(size, A, B) for size in sizes),
             "spectra",
             [pltpu.VMEM((count, A, 2 * B), F32)],
             (1000, 1000),
         )(recv, *tables_in)
 
-    u2, g2, fg2 = spectra(recv, 4, 2)
-    relay = swap(fg2, 6)
-    recv, fg2 = lax.optimization_barrier((recv, fg2))
-    u3, g3, fg3 = spectra(recv, 6, 2)
-    fg3 = swap(fg3, 6)
-    recv, g3 = lax.optimization_barrier((recv, g3))
-    u0, g0, near = spectra(recv, 0, 4)
-    f3, near = lax.optimization_barrier((f3, near))
-    far = swap(jnp.stack([own, f3]), 2)
-    even = call(conv_even_kernel, buffer, "even", cost=(1000, 1000))(
-        own, f3, u0, g0, u2, g2, u3, g3, *tables_in
+    ur, gr, relay = spectra(recv, (2,), (2,))
+    recv, relay = lax.optimization_barrier((recv, relay))
+    relay = swap(relay, 6)
+    un, gn, direct, near = spectra(recv, (3, 0, 1), (2, 4))
+    fb, near = lax.optimization_barrier((fb, near))
+    far = swap(fb, 6)
+    direct = swap(direct, 6)
+    three = call(conv_three_kernel, buffer, "three", cost=(1000, 1000))(
+        own, fb, fa, un, gn, *tables_in
     )
     came = swap(call(mix_kernel, two, "mix")(near, relay), 2)
-    odd = call(conv_odd_kernel, buffer, "odd", cost=(1000, 1000))(
-        far, even, u0, g0, u2, g2, u3, g3, *tables_in
-    )
-    back_send = call(place_kernel, buffer, "place")(near, fg3, came, odd)
+    last = call(conv_last_kernel, buffer, "last", cost=(1000, 1000))(far, three, ur, gr, *tables_in)
+    back_send = call(place_kernel, buffer, "place")(near, direct, came, last)
     landed = exchange(back_send)
     *grads, fg = call(
         post_kernel,

time: 73.3 us -> 73.1 us (level)
  blocking collectives: 49.7 us -> 51 us
  waiting for transfers between devices: 1.74 us -> 0.52 us
    all_to_all x2, blocking collectives: 49.7 us -> 51 us  [exchange(): lax.all_to_all(x, ('seq', 'chan'), 0, 0, axis_index_groups=PAIRS, tiled=T...]
    ppermute x5 -> x6, waiting for transfers between devices: 1.74 us -> 0.52 us  [swap(): return lax.ppermute(x, 'chan', [(z, z ^ distance) for z in range(8)])]
    pallas_call x7 -> x6, Pallas kernels: 6.65 us -> 6.29 us  [the longest x2 2.91 us: spectra(): call(functools.partial(spectra_kernel, channels=channels), (shape(count,...]
    ppermute x5 -> x6, starting transfers between devices: 11.5 us -> 11.5 us  [swap(): return lax.ppermute(x, 'chan', [(z, z ^ distance) for z in range(8)])]
  transfers between devices with their start and end apart: 5 -> 6, of which waited for: 2 -> 1; matrix products, arithmetic and copies ran while one was open for 0% -> 0% of each run, Pallas kernels for 9% -> 9%
where the time goes in v5:
time: 73.1 us; the launch traced here: 72.9 us
  blocking collectives  51 us (70%)
  starting transfers between devices  11.5 us (16%)
  Pallas kernels  9.01 us (12%)
  between operations  0.79 us (1%)
    all_to_all x2, blocking collectives, exchange(): lax.all_to_all(x, ('seq', 'chan'), 0, 0, axis_index_groups=PAIRS, tiled=T...  51 us
    ppermute x6, starting transfers between devices, swap(): return lax.ppermute(x, 'chan', [(z, z ^ distance) for z in range(8)])  11.5 us
    pallas_call x2, Pallas kernels, spectra(): call(functools.partial(spectra_kernel, channels=channels), (shape(count,...  2.91 us
    pallas_call x1, Pallas kernels, body(): call(conv_three_kernel, buffer, 'three', cost=(1000, 1000))  2.19 us
    pallas_call x1, Pallas kernels, body(): call(prep_kernel, buffer, 'prep', [gate, gate, gate, gate, pltpu.VMEM((64...  1.6 us
  transfers between devices with their start and end apart: 6, of which 1 were waited for; matrix products, arithmetic and copies ran while one was open for 0% of the time, Pallas kernels for 9%

profile of v5, /device:TPU:1, one launch (start us, length us, event | category | flops | bytes accessed | tf_op | source)
XLA Modules:
  0.0 72.9 jit_solution(16037706869333839692)
XLA Ops:
  0.6 1.6 %prep.1 = f32[2176,128]{1,0:T(8,128)S(1)} custom-call(bf16[256,512]{1,0:T(8,128)(2,1)} %outer_hbm.1, bf16[256,512]{1,0:T(8,128)(2,1)} %inner_ref.1, bf16[256,512]{1,0:T(8,128)(2,1)} %signal_ref.1, bf16[256,512]{1,0:T(8,128)(2,1)} %cot_ref.1, f32[64,256]{1,0:T(8,128)} %bitcast.12), custom_call_target="tpu_custom_call" | custom-call | flops 1000 | bytes 1000 | tf_op jit(solution)/shard_map/prep/pallas_call | solution.py:293
  2.2 0.0 copy-start
  2.2 0.0 copy-start.1
  2.3 0.0 copy-start.2
  2.3 0.0 copy-start.3
  2.3 0.0 copy-start.4
  2.3 25.7 %all_to_all.18 = f32[64,1,4352]{2,1,0:T(1,128)S(1)} all-to-all(f32[64,1,4352]{2,1,0:T(1,128)S(1)} %bitcast.10), channel_id=1, replica_groups={{160,136,40,112,224,216,32,120,16,144,128,8,184,208,56,104,96,232,48,17..., dimensions={0} | all-to-all | bytes 2228224 | tf_op jit(solution)/shard_map/all_to_all | solution.py:280
  28.0 0.0 copy-done
  28.0 0.0 copy-done.1
  28.1 3.1 %collective-permute-start = (f32[2,64,128]{2,1,0:T(8,128)S(1)}, f32[2,64,128]{2,1,0:T(8,128)S(1)}, u32[]{:S(2)}, u32[]{:S(2)}) collective-permute-start(f32[2,64,128]{2,1,0:T(8,128)S(1)} %pick.1.own_ref), channel_id=1, source_target_pairs={{0,2},{1,3},{2,0},{3,1},{4,6},{5,7},{6,4},{7,5},{8,10},{9,11},{10,... | collective-permute-start | bytes 196616 | tf_op jit(solution)/shard_map/ppermute | solution.py:285
  31.1 0.9 %spectra.2 = (f32[2,128,256]{2,1,0:T(8,128)S(1)}, f32[2,128,256]{2,1,0:T(8,128)S(1)}, f32[2,64,128]{2,1,0:T(8,128)S(1)}) custom-call(f32[2176,128]{1,0:T(8,128)S(1)} %bitcast.7, bf16[128,192]{1,0:T(8,128)(2,1)S(1)} %copy-done.3, bf16[256,256]{1,0:T(8,128)(2,1)S(1)} %copy-done.1, bf16[256,256]{1,0:T(8,128)(2,1)S(1)} %copy-done, f32[2,64,128]{2,1,0:T(8,128)S(1)} %copy-done.2, ...), custom_call_target="tpu_custom_call" | custom-call | flops 1000 | bytes 1000 | tf_op jit(solution)/shard_map/spectra/pallas_call | solution.py:308
  32.0 3.4 %collective-permute-start.2 = (f32[2,64,128]{2,1,0:T(8,128)S(1)}, f32[2,64,128]{2,1,0:T(8,128)S(1)}, u32[]{:S(2)}, u32[]{:S(2)}) collective-permute-start(f32[2,64,128]{2,1,0:T(8,128)S(1)} %get-tuple-element.24), channel_id=1, source_target_pairs={{0,6},{1,7},{2,4},{3,5},{4,2},{5,3},{6,0},{7,1},{8,14},{9,15},{10,... | collective-permute-start | bytes 196616 | tf_op jit(solution)/shard_map/ppermute | solution.py:285
  35.4 0.3 collective-permute-start.5
  35.7 2.0 %spectra.3 = (f32[6,128,256]{2,1,0:T(8,128)S(1)}, f32[6,128,256]{2,1,0:T(8,128)S(1)}, f32[2,64,128]{2,1,0:T(8,128)S(1)}, f32[4,64,128]{2,1,0:T(8,128)S(1)}) custom-call(f32[2176,128]{1,0:T(8,128)S(1)} %bitcast.8, bf16[128,192]{1,0:T(8,128)(2,1)S(1)} %copy-done.3, bf16[256,256]{1,0:T(8,128)(2,1)S(1)} %copy-done.1, bf16[256,256]{1,0:T(8,128)(2,1)S(1)} %copy-done, ...), custom_call_target="tpu_custom_call" | custom-call | flops 1000 | bytes 1000 | tf_op jit(solution)/shard_map/spectra/pallas_call | solution.py:308
  37.7 0.0 collective-permute-done.fb_ref
  37.7 3.4 %collective-permute-start.4 = (f32[2,64,128]{2,1,0:T(8,128)S(1)}, f32[2,64,128]{2,1,0:T(8,128)S(1)}, u32[]{:S(2)}, u32[]{:S(2)}) collective-permute-start(f32[2,64,128]{2,1,0:T(8,128)S(1)} %collective-permute-done.fb_ref), channel_id=1, source_target_pairs={{0,6},{1,7},{2,4},{3,5},{4,2},{5,3},{6,0},{7,1},{8,14},{9,15},{10,... | collective-permute-start | bytes 196616 | tf_op jit(solution)/shard_map/ppermute | solution.py:285
  41.1 0.3 collective-permute-start.1
  41.4 0.0 collective-permute-done.2.came_ref
  41.4 1.1 %collective-permute-start.3 = (f32[2,64,128]{2,1,0:T(8,128)S(1)}, f32[2,64,128]{2,1,0:T(8,128)S(1)}, u32[]{:S(2)}, u32[]{:S(2)}) collective-permute-start(f32[2,64,128]{2,1,0:T(8,128)S(1)} %mix.1), channel_id=1, source_target_pairs={{0,2},{1,3},{2,0},{3,1},{4,6},{5,7},{6,4},{7,5},{8,10},{9,11},{10,... | collective-permute-start | bytes 196616 | tf_op jit(solution)/shard_map/ppermute | solution.py:285
  42.5 0.0 collective-permute-done.5.fa_ref
  42.5 2.2 %three.1.base_ref = f32[2176,128]{1,0:T(8,128)S(1)} custom-call(f32[2,64,128]{2,1,0:T(8,128)S(1)} %pick.1.own_ref, f32[2,64,128]{2,1,0:T(8,128)S(1)} %collective-permute-done.fb_ref, f32[2,64,128]{2,1,0:T(8,128)S(1)} %collective-permute-done.5.fa_ref, f32[6,128,256]{2,1,0:T(8,128)S(1)} %get-tuple-element.26.u_ref, ...), custom_call_target="tpu_custom_call" | custom-call | flops 1000 | bytes 1000 | tf_op jit(solution)/shard_map/three/pallas_call | solution.py:324
  44.7 0.0 collective-permute-done.4.far_ref
  44.7 1.1 %last.1.base_ref = f32[2176,128]{1,0:T(8,128)S(1)} custom-call(f32[2,64,128]{2,1,0:T(8,128)S(1)} %collective-permute-done.4.far_ref, f32[2176,128]{1,0:T(8,128)S(1)} %three.1.base_ref, f32[2,128,256]{2,1,0:T(8,128)S(1)} %get-tuple-element.28.u_ref, f32[2,128,256]{2,1,0:T(8,128)S(1)} %get-tuple-element.29.g_ref, bf16[128,192]{1,0:T(8,128)(2,1)S(1)} %copy-done.3, ...), custom_call_target="tpu_custom_call" | custom-call | flops 1000 | bytes 1000 | tf_op jit(solution)/shard_map/last/pallas_call | solution.py:328
  45.8 0.5 collective-permute-done.1.direct_ref
  46.3 0.0 collective-permute-done.3.came_ref
  46.3 0.1 place.1
  46.4 0.0 copy-start.5
  46.4 0.0 copy-start.6
  46.5 0.0 copy-start.7
  46.5 25.3 %all_to_all.19 = f32[64,1,4352]{2,1,0:T(1,128)S(1)} all-to-all(f32[64,1,4352]{2,1,0:T(1,128)S(1)} %bitcast.9), channel_id=1, replica_groups={{160,136,40,112,224,216,32,120,16,144,128,8,184,208,56,104,96,232,48,17..., dimensions={0} | all-to-all | bytes 2228224 | tf_op jit(solution)/shard_map/all_to_all | solution.py:280
  71.8 0.0 copy-done.6
  71.8 1.1 %post.1 = (bf16[256,512]{1,0:T(8,128)(2,1)}, bf16[256,512]{1,0:T(8,128)(2,1)}, bf16[256,512]{1,0:T(8,128)(2,1)}, f32[64,256]{1,0:T(8,128)}) custom-call(f32[2176,128]{1,0:T(8,128)S(1)} %bitcast.11, bf16[256,512]{1,0:T(8,128)(2,1)S(1)} %copy-done.5, bf16[256,512]{1,0:T(8,128)(2,1)S(1)} %copy-done.6, bf16[256,512]{1,0:T(8,128)(2,1)S(1)} %copy-done.7), custom_call_target="tpu_custom_call" | custom-call | flops 1000 | bytes 1000 | tf_op jit(solution)/shard_map/post/pallas_call | solution.py:331
  (7 shorter events, 0.0 us)
Async XLA Ops:
  2.2 25.8 %copy-start = (bf16[256,256]{1,0:T(8,128)(2,1)S(1)}, bf16[256,256]{1,0:T(8,128)(2,1)}, u32[]{:S(2)}) copy-start(bf16[256,256]{1,0:T(8,128)(2,1)} %constant.12.clone.w2l_ref) | copy-start | bytes 393220
  2.2 25.8 %copy-start.1 = (bf16[256,256]{1,0:T(8,128)(2,1)S(1)}, bf16[256,256]{1,0:T(8,128)(2,1)}, u32[]{:S(2)}) copy-start(bf16[256,256]{1,0:T(8,128)(2,1)} %constant.11.clone.w2h_ref) | copy-start | bytes 393220
  2.3 25.8 %copy-start.2 = (f32[2,64,128]{2,1,0:T(8,128)S(1)}, f32[2,64,128]{2,1,0:T(8,128)}, u32[]{:S(2)}) copy-start(f32[2,64,128]{2,1,0:T(8,128)} %constant.13.clone.tw_ref) | copy-start | bytes 196612
  2.3 25.7 %copy-start.3 = (bf16[128,192]{1,0:T(8,128)(2,1)S(1)}, bf16[128,192]{1,0:T(8,128)(2,1)}, u32[]{:S(2)}) copy-start(bf16[128,192]{1,0:T(8,128)(2,1)} %constant.10.clone.w1_ref) | copy-start | bytes 147460
  2.3 25.7 %copy-start.4 = (bf16[64,384]{1,0:T(8,128)(2,1)S(1)}, bf16[64,384]{1,0:T(8,128)(2,1)}, u32[]{:S(2)}) copy-start(bf16[64,384]{1,0:T(8,128)(2,1)} %constant.14.clone.v1_ref) | copy-start | bytes 147460
  28.1 9.7 %collective-permute-start = (f32[2,64,128]{2,1,0:T(8,128)S(1)}, f32[2,64,128]{2,1,0:T(8,128)S(1)}, u32[]{:S(2)}, u32[]{:S(2)}) collective-permute-start(f32[2,64,128]{2,1,0:T(8,128)S(1)} %pick.1.own_ref), channel_id=1, source_target_pairs={{0,2},{1,3},{2,0},{3,1},{4,6},{5,7},{6,4},{7,5},{8,10},{9,11},{10,... | collective-permute-start | bytes 196616 | tf_op jit(solution)/shard_map/ppermute | solution.py:285
  32.0 9.4 %collective-permute-start.2 = (f32[2,64,128]{2,1,0:T(8,128)S(1)}, f32[2,64,128]{2,1,0:T(8,128)S(1)}, u32[]{:S(2)}, u32[]{:S(2)}) collective-permute-start(f32[2,64,128]{2,1,0:T(8,128)S(1)} %get-tuple-element.24), channel_id=1, source_target_pairs={{0,6},{1,7},{2,4},{3,5},{4,2},{5,3},{6,0},{7,1},{8,14},{9,15},{10,... | collective-permute-start | bytes 196616 | tf_op jit(solution)/shard_map/ppermute | solution.py:285
  35.4 7.1 %collective-permute-start.5 = (f32[2,64,128]{2,1,0:T(8,128)S(1)}, f32[2,64,128]{2,1,0:T(8,128)S(1)}, u32[]{:S(2)}, u32[]{:S(2)}) collective-permute-start(f32[2,64,128]{2,1,0:T(8,128)S(1)} %pick.1.own_ref), channel_id=1, source_target_pairs={{0,6},{1,7},{2,4},{3,5},{4,2},{5,3},{6,0},{7,1},{8,14},{9,15},{10,... | collective-permute-start | bytes 196616 | tf_op jit(solution)/shard_map/ppermute | solution.py:285
  37.7 7.0 %collective-permute-start.4 = (f32[2,64,128]{2,1,0:T(8,128)S(1)}, f32[2,64,128]{2,1,0:T(8,128)S(1)}, u32[]{:S(2)}, u32[]{:S(2)}) collective-permute-start(f32[2,64,128]{2,1,0:T(8,128)S(1)} %collective-permute-done.fb_ref), channel_id=1, source_target_pairs={{0,6},{1,7},{2,4},{3,5},{4,2},{5,3},{6,0},{7,1},{8,14},{9,15},{10,... | collective-permute-start | bytes 196616 | tf_op jit(solution)/shard_map/ppermute | solution.py:285
  41.1 5.2 %collective-permute-start.1 = (f32[2,64,128]{2,1,0:T(8,128)S(1)}, f32[2,64,128]{2,1,0:T(8,128)S(1)}, u32[]{:S(2)}, u32[]{:S(2)}) collective-permute-start(f32[2,64,128]{2,1,0:T(8,128)S(1)} %get-tuple-element.23), channel_id=1, source_target_pairs={{0,6},{1,7},{2,4},{3,5},{4,2},{5,3},{6,0},{7,1},{8,14},{9,15},{10,... | collective-permute-start | bytes 196616 | tf_op jit(solution)/shard_map/ppermute | solution.py:285
  41.4 4.9 %collective-permute-start.3 = (f32[2,64,128]{2,1,0:T(8,128)S(1)}, f32[2,64,128]{2,1,0:T(8,128)S(1)}, u32[]{:S(2)}, u32[]{:S(2)}) collective-permute-start(f32[2,64,128]{2,1,0:T(8,128)S(1)} %mix.1), channel_id=1, source_target_pairs={{0,2},{1,3},{2,0},{3,1},{4,6},{5,7},{6,4},{7,5},{8,10},{9,11},{10,... | collective-permute-start | bytes 196616 | tf_op jit(solution)/shard_map/ppermute | solution.py:285
  46.4 25.3 %copy-start.5 = (bf16[256,512]{1,0:T(8,128)(2,1)S(1)}, bf16[256,512]{1,0:T(8,128)(2,1)}, u32[]{:S(2)}) copy-start(bf16[256,512]{1,0:T(8,128)(2,1)} %inner_ref.1) | copy-start | bytes 786436
  46.4 25.3 %copy-start.6 = (bf16[256,512]{1,0:T(8,128)(2,1)S(1)}, bf16[256,512]{1,0:T(8,128)(2,1)}, u32[]{:S(2)}) copy-start(bf16[256,512]{1,0:T(8,128)(2,1)} %signal_ref.1) | copy-start | bytes 786436
  46.5 25.3 %copy-start.7 = (bf16[256,512]{1,0:T(8,128)(2,1)S(1)}, bf16[256,512]{1,0:T(8,128)(2,1)}, u32[]{:S(2)}) copy-start(bf16[256,512]{1,0:T(8,128)(2,1)} %cot_ref.1) | copy-start | bytes 786436

commit v6 on v5

--- a/solution.py
+++ b/solution.py
@@ -19,7 +19,7 @@
 SHARDS = 32
 MEMBERS = 64
 ROWS = 34
-SCATTER = np.random.RandomState(3).permutation(SHARDS)
+SCATTER = np.random.RandomState(10).permutation(SHARDS)
 VMEM_LIMIT = 16 * 1024 * 1024
 
 

time: 73.1 us -> 72.3 us (0.989)
  blocking collectives: 51 us -> 50.2 us
    all_to_all x2, blocking collectives: 51 us -> 50.2 us  [exchange(): lax.all_to_all(x, ('seq', 'chan'), 0, 0, axis_index_groups=PAIRS, tiled=T...]
where the time goes in v6:
time: 72.3 us; the launch traced here: 72.1 us
  blocking collectives  50.2 us (69%)
  starting transfers between devices  11.5 us (16%)
  Pallas kernels  9.01 us (12%)
  between operations  0.79 us (1%)
    all_to_all x2, blocking collectives, exchange(): lax.all_to_all(x, ('seq', 'chan'), 0, 0, axis_index_groups=PAIRS, tiled=T...  50.2 us
    ppermute x6, starting transfers between devices, swap(): return lax.ppermute(x, 'chan', [(z, z ^ distance) for z in range(8)])  11.5 us
    pallas_call x2, Pallas kernels, spectra(): call(functools.partial(spectra_kernel, channels=channels), (shape(count,...  2.91 us
    pallas_call x1, Pallas kernels, body(): call(conv_three_kernel, buffer, 'three', cost=(1000, 1000))  2.2 us
    pallas_call x1, Pallas kernels, body(): call(prep_kernel, buffer, 'prep', [gate, gate, gate, gate, pltpu.VMEM((64...  1.6 us
  transfers between devices with their start and end apart: 6, of which 1 were waited for; matrix products, arithmetic and copies ran while one was open for 0% of the time, Pallas kernels for 9%

profile of v6, /device:TPU:1, one launch (start us, length us, event | category | flops | bytes accessed | tf_op | source)
XLA Modules:
  0.0 72.1 jit_solution(3189810129540937570)
XLA Ops:
  0.6 1.6 %prep.1 = f32[2176,128]{1,0:T(8,128)S(1)} custom-call(bf16[256,512]{1,0:T(8,128)(2,1)} %outer_hbm.1, bf16[256,512]{1,0:T(8,128)(2,1)} %inner_ref.1, bf16[256,512]{1,0:T(8,128)(2,1)} %signal_ref.1, bf16[256,512]{1,0:T(8,128)(2,1)} %cot_ref.1, f32[64,256]{1,0:T(8,128)} %bitcast.12), custom_call_target="tpu_custom_call" | custom-call | flops 1000 | bytes 1000 | tf_op jit(solution)/shard_map/prep/pallas_call | solution.py:293
  2.2 0.0 copy-start
  2.2 0.0 copy-start.1
  2.3 0.0 copy-start.2
  2.3 0.0 copy-start.3
  2.3 0.0 copy-start.4
  2.3 25.3 %all_to_all.18 = f32[64,1,4352]{2,1,0:T(1,128)S(1)} all-to-all(f32[64,1,4352]{2,1,0:T(1,128)S(1)} %bitcast.10), channel_id=1, replica_groups={{160,56,40,16,24,168,104,224,96,8,152,112,144,48,88,184,192,240,176,80,..., dimensions={0} | all-to-all | bytes 2228224 | tf_op jit(solution)/shard_map/all_to_all | solution.py:280
  27.6 0.0 copy-done
  27.6 0.0 copy-done.1
  27.6 0.0 copy-done.2
  27.6 3.1 %collective-permute-start = (f32[2,64,128]{2,1,0:T(8,128)S(1)}, f32[2,64,128]{2,1,0:T(8,128)S(1)}, u32[]{:S(2)}, u32[]{:S(2)}) collective-permute-start(f32[2,64,128]{2,1,0:T(8,128)S(1)} %pick.1.own_ref), channel_id=1, source_target_pairs={{0,2},{1,3},{2,0},{3,1},{4,6},{5,7},{6,4},{7,5},{8,10},{9,11},{10,... | collective-permute-start | bytes 196616 | tf_op jit(solution)/shard_map/ppermute | solution.py:285
  30.7 0.9 %spectra.2 = (f32[2,128,256]{2,1,0:T(8,128)S(1)}, f32[2,128,256]{2,1,0:T(8,128)S(1)}, f32[2,64,128]{2,1,0:T(8,128)S(1)}) custom-call(f32[2176,128]{1,0:T(8,128)S(1)} %bitcast.7, bf16[128,192]{1,0:T(8,128)(2,1)S(1)} %copy-done.3, bf16[256,256]{1,0:T(8,128)(2,1)S(1)} %copy-done.1, bf16[256,256]{1,0:T(8,128)(2,1)S(1)} %copy-done, f32[2,64,128]{2,1,0:T(8,128)S(1)} %copy-done.2, ...), custom_call_target="tpu_custom_call" | custom-call | flops 1000 | bytes 1000 | tf_op jit(solution)/shard_map/spectra/pallas_call | solution.py:308
  31.6 3.4 %collective-permute-start.2 = (f32[2,64,128]{2,1,0:T(8,128)S(1)}, f32[2,64,128]{2,1,0:T(8,128)S(1)}, u32[]{:S(2)}, u32[]{:S(2)}) collective-permute-start(f32[2,64,128]{2,1,0:T(8,128)S(1)} %get-tuple-element.24), channel_id=1, source_target_pairs={{0,6},{1,7},{2,4},{3,5},{4,2},{5,3},{6,0},{7,1},{8,14},{9,15},{10,... | collective-permute-start | bytes 196616 | tf_op jit(solution)/shard_map/ppermute | solution.py:285
  35.0 0.3 collective-permute-start.5
  35.3 2.0 %spectra.3 = (f32[6,128,256]{2,1,0:T(8,128)S(1)}, f32[6,128,256]{2,1,0:T(8,128)S(1)}, f32[2,64,128]{2,1,0:T(8,128)S(1)}, f32[4,64,128]{2,1,0:T(8,128)S(1)}) custom-call(f32[2176,128]{1,0:T(8,128)S(1)} %bitcast.8, bf16[128,192]{1,0:T(8,128)(2,1)S(1)} %copy-done.3, bf16[256,256]{1,0:T(8,128)(2,1)S(1)} %copy-done.1, bf16[256,256]{1,0:T(8,128)(2,1)S(1)} %copy-done, ...), custom_call_target="tpu_custom_call" | custom-call | flops 1000 | bytes 1000 | tf_op jit(solution)/shard_map/spectra/pallas_call | solution.py:308
  37.3 0.0 collective-permute-done.fb_ref
  37.3 3.4 %collective-permute-start.4 = (f32[2,64,128]{2,1,0:T(8,128)S(1)}, f32[2,64,128]{2,1,0:T(8,128)S(1)}, u32[]{:S(2)}, u32[]{:S(2)}) collective-permute-start(f32[2,64,128]{2,1,0:T(8,128)S(1)} %collective-permute-done.fb_ref), channel_id=1, source_target_pairs={{0,6},{1,7},{2,4},{3,5},{4,2},{5,3},{6,0},{7,1},{8,14},{9,15},{10,... | collective-permute-start | bytes 196616 | tf_op jit(solution)/shard_map/ppermute | solution.py:285
  40.7 0.3 collective-permute-start.1
  41.0 0.0 collective-permute-done.2.came_ref
  41.0 1.1 %collective-permute-start.3 = (f32[2,64,128]{2,1,0:T(8,128)S(1)}, f32[2,64,128]{2,1,0:T(8,128)S(1)}, u32[]{:S(2)}, u32[]{:S(2)}) collective-permute-start(f32[2,64,128]{2,1,0:T(8,128)S(1)} %mix.1), channel_id=1, source_target_pairs={{0,2},{1,3},{2,0},{3,1},{4,6},{5,7},{6,4},{7,5},{8,10},{9,11},{10,... | collective-permute-start | bytes 196616 | tf_op jit(solution)/shard_map/ppermute | solution.py:285
  42.1 0.0 collective-permute-done.5.fa_ref
  42.1 2.2 %three.1.base_ref = f32[2176,128]{1,0:T(8,128)S(1)} custom-call(f32[2,64,128]{2,1,0:T(8,128)S(1)} %pick.1.own_ref, f32[2,64,128]{2,1,0:T(8,128)S(1)} %collective-permute-done.fb_ref, f32[2,64,128]{2,1,0:T(8,128)S(1)} %collective-permute-done.5.fa_ref, f32[6,128,256]{2,1,0:T(8,128)S(1)} %get-tuple-element.26.u_ref, ...), custom_call_target="tpu_custom_call" | custom-call | flops 1000 | bytes 1000 | tf_op jit(solution)/shard_map/three/pallas_call | solution.py:324
  44.3 0.0 collective-permute-done.4.far_ref
  44.3 1.1 %last.1.base_ref = f32[2176,128]{1,0:T(8,128)S(1)} custom-call(f32[2,64,128]{2,1,0:T(8,128)S(1)} %collective-permute-done.4.far_ref, f32[2176,128]{1,0:T(8,128)S(1)} %three.1.base_ref, f32[2,128,256]{2,1,0:T(8,128)S(1)} %get-tuple-element.28.u_ref, f32[2,128,256]{2,1,0:T(8,128)S(1)} %get-tuple-element.29.g_ref, bf16[128,192]{1,0:T(8,128)(2,1)S(1)} %copy-done.3, ...), custom_call_target="tpu_custom_call" | custom-call | flops 1000 | bytes 1000 | tf_op jit(solution)/shard_map/last/pallas_call | solution.py:328
  45.4 0.6 collective-permute-done.1.direct_ref
  46.0 0.0 collective-permute-done.3.came_ref
  46.0 0.1 place.1
  46.1 0.0 copy-start.5
  46.1 0.0 copy-start.6
  46.1 0.0 copy-start.7
  46.1 24.9 %all_to_all.19 = f32[64,1,4352]{2,1,0:T(1,128)S(1)} all-to-all(f32[64,1,4352]{2,1,0:T(1,128)S(1)} %bitcast.9), channel_id=1, replica_groups={{160,56,40,16,24,168,104,224,96,8,152,112,144,48,88,184,192,240,176,80,..., dimensions={0} | all-to-all | bytes 2228224 | tf_op jit(solution)/shard_map/all_to_all | solution.py:280
  71.0 1.1 %post.1 = (bf16[256,512]{1,0:T(8,128)(2,1)}, bf16[256,512]{1,0:T(8,128)(2,1)}, bf16[256,512]{1,0:T(8,128)(2,1)}, f32[64,256]{1,0:T(8,128)}) custom-call(f32[2176,128]{1,0:T(8,128)S(1)} %bitcast.11, bf16[256,512]{1,0:T(8,128)(2,1)S(1)} %copy-done.5, bf16[256,512]{1,0:T(8,128)(2,1)S(1)} %copy-done.6, bf16[256,512]{1,0:T(8,128)(2,1)S(1)} %copy-done.7), custom_call_target="tpu_custom_call" | custom-call | flops 1000 | bytes 1000 | tf_op jit(solution)/shard_map/post/pallas_call | solution.py:331
  (7 shorter events, 0.0 us)
Async XLA Ops:
  2.2 25.3 %copy-start = (bf16[256,256]{1,0:T(8,128)(2,1)S(1)}, bf16[256,256]{1,0:T(8,128)(2,1)}, u32[]{:S(2)}) copy-start(bf16[256,256]{1,0:T(8,128)(2,1)} %constant.12.clone.w2l_ref) | copy-start | bytes 393220
  2.2 25.3 %copy-start.1 = (bf16[256,256]{1,0:T(8,128)(2,1)S(1)}, bf16[256,256]{1,0:T(8,128)(2,1)}, u32[]{:S(2)}) copy-start(bf16[256,256]{1,0:T(8,128)(2,1)} %constant.11.clone.w2h_ref) | copy-start | bytes 393220
  2.3 25.3 %copy-start.2 = (f32[2,64,128]{2,1,0:T(8,128)S(1)}, f32[2,64,128]{2,1,0:T(8,128)}, u32[]{:S(2)}) copy-start(f32[2,64,128]{2,1,0:T(8,128)} %constant.13.clone.tw_ref) | copy-start | bytes 196612
  2.3 25.3 %copy-start.3 = (bf16[128,192]{1,0:T(8,128)(2,1)S(1)}, bf16[128,192]{1,0:T(8,128)(2,1)}, u32[]{:S(2)}) copy-start(bf16[128,192]{1,0:T(8,128)(2,1)} %constant.10.clone.w1_ref) | copy-start | bytes 147460
  2.3 25.3 %copy-start.4 = (bf16[64,384]{1,0:T(8,128)(2,1)S(1)}, bf16[64,384]{1,0:T(8,128)(2,1)}, u32[]{:S(2)}) copy-start(bf16[64,384]{1,0:T(8,128)(2,1)} %constant.14.clone.v1_ref) | copy-start | bytes 147460
  27.6 9.7 %collective-permute-start = (f32[2,64,128]{2,1,0:T(8,128)S(1)}, f32[2,64,128]{2,1,0:T(8,128)S(1)}, u32[]{:S(2)}, u32[]{:S(2)}) collective-permute-start(f32[2,64,128]{2,1,0:T(8,128)S(1)} %pick.1.own_ref), channel_id=1, source_target_pairs={{0,2},{1,3},{2,0},{3,1},{4,6},{5,7},{6,4},{7,5},{8,10},{9,11},{10,... | collective-permute-start | bytes 196616 | tf_op jit(solution)/shard_map/ppermute | solution.py:285
  31.6 9.4 %collective-permute-start.2 = (f32[2,64,128]{2,1,0:T(8,128)S(1)}, f32[2,64,128]{2,1,0:T(8,128)S(1)}, u32[]{:S(2)}, u32[]{:S(2)}) collective-permute-start(f32[2,64,128]{2,1,0:T(8,128)S(1)} %get-tuple-element.24), channel_id=1, source_target_pairs={{0,6},{1,7},{2,4},{3,5},{4,2},{5,3},{6,0},{7,1},{8,14},{9,15},{10,... | collective-permute-start | bytes 196616 | tf_op jit(solution)/shard_map/ppermute | solution.py:285
  35.0 7.1 %collective-permute-start.5 = (f32[2,64,128]{2,1,0:T(8,128)S(1)}, f32[2,64,128]{2,1,0:T(8,128)S(1)}, u32[]{:S(2)}, u32[]{:S(2)}) collective-permute-start(f32[2,64,128]{2,1,0:T(8,128)S(1)} %pick.1.own_ref), channel_id=1, source_target_pairs={{0,6},{1,7},{2,4},{3,5},{4,2},{5,3},{6,0},{7,1},{8,14},{9,15},{10,... | collective-permute-start | bytes 196616 | tf_op jit(solution)/shard_map/ppermute | solution.py:285
  37.3 7.0 %collective-permute-start.4 = (f32[2,64,128]{2,1,0:T(8,128)S(1)}, f32[2,64,128]{2,1,0:T(8,128)S(1)}, u32[]{:S(2)}, u32[]{:S(2)}) collective-permute-start(f32[2,64,128]{2,1,0:T(8,128)S(1)} %collective-permute-done.fb_ref), channel_id=1, source_target_pairs={{0,6},{1,7},{2,4},{3,5},{4,2},{5,3},{6,0},{7,1},{8,14},{9,15},{10,... | collective-permute-start | bytes 196616 | tf_op jit(solution)/shard_map/ppermute | solution.py:285
  40.7 5.3 %collective-permute-start.1 = (f32[2,64,128]{2,1,0:T(8,128)S(1)}, f32[2,64,128]{2,1,0:T(8,128)S(1)}, u32[]{:S(2)}, u32[]{:S(2)}) collective-permute-start(f32[2,64,128]{2,1,0:T(8,128)S(1)} %get-tuple-element.23), channel_id=1, source_target_pairs={{0,6},{1,7},{2,4},{3,5},{4,2},{5,3},{6,0},{7,1},{8,14},{9,15},{10,... | collective-permute-start | bytes 196616 | tf_op jit(solution)/shard_map/ppermute | solution.py:285
  41.0 5.0 %collective-permute-start.3 = (f32[2,64,128]{2,1,0:T(8,128)S(1)}, f32[2,64,128]{2,1,0:T(8,128)S(1)}, u32[]{:S(2)}, u32[]{:S(2)}) collective-permute-start(f32[2,64,128]{2,1,0:T(8,128)S(1)} %mix.1), channel_id=1, source_target_pairs={{0,2},{1,3},{2,0},{3,1},{4,6},{5,7},{6,4},{7,5},{8,10},{9,11},{10,... | collective-permute-start | bytes 196616 | tf_op jit(solution)/shard_map/ppermute | solution.py:285
  46.1 24.9 %copy-start.5 = (bf16[256,512]{1,0:T(8,128)(2,1)S(1)}, bf16[256,512]{1,0:T(8,128)(2,1)}, u32[]{:S(2)}) copy-start(bf16[256,512]{1,0:T(8,128)(2,1)} %inner_ref.1) | copy-start | bytes 786436
  46.1 24.9 %copy-start.6 = (bf16[256,512]{1,0:T(8,128)(2,1)S(1)}, bf16[256,512]{1,0:T(8,128)(2,1)}, u32[]{:S(2)}) copy-start(bf16[256,512]{1,0:T(8,128)(2,1)} %signal_ref.1) | copy-start | bytes 786436
  46.1 24.9 %copy-start.7 = (bf16[256,512]{1,0:T(8,128)(2,1)S(1)}, bf16[256,512]{1,0:T(8,128)(2,1)}, u32[]{:S(2)}) copy-start(bf16[256,512]{1,0:T(8,128)(2,1)} %cot_ref.1) | copy-start | bytes 786436

commit v7 on v6

--- a/solution.py
+++ b/solution.py
@@ -242,15 +242,17 @@
         rows = slice(h * B, (h + 1) * B)
         for k in range(4):
             cols = pl.ds(pl.multiple_of(pairs[k] * B, B), B)
-            og_ref[rows, cols] = (cot_ref[rows, cols].astype(F32) * fetch(0, h, k)).astype(BF)
-        store(og_ref, og_hbm, pl.ds(h * B, B))
-        for k in range(4):
-            cols = pl.ds(pl.multiple_of(pairs[k] * B, B), B)
             back = fetch(16, h, k)
             ig_ref[rows, cols] = (back * signal_ref[rows, cols].astype(F32)).astype(BF)
             sg_ref[rows, cols] = (back * inner_ref[rows, cols].astype(F32)).astype(BF)
         store(ig_ref, ig_hbm, pl.ds(h * B, B))
         store(sg_ref, sg_hbm, pl.ds(h * B, B))
+    for h in range(2):
+        rows = slice(h * B, (h + 1) * B)
+        for k in range(4):
+            cols = pl.ds(pl.multiple_of(pairs[k] * B, B), B)
+            og_ref[rows, cols] = (cot_ref[rows, cols].astype(F32) * fetch(0, h, k)).astype(BF)
+        store(og_ref, og_hbm, pl.ds(h * B, B))
     for copy in copies:
         copy.wait()
 

time: 72.3 us -> 72.3 us (level)
  no operation moved by 1% of the time
where the time goes in v7:
time: 72.3 us; the launch traced here: 72.1 us
  blocking collectives  50.2 us (69%)
  starting transfers between devices  11.5 us (16%)
  Pallas kernels  8.98 us (12%)
  between operations  0.79 us (1%)
    all_to_all x2, blocking collectives, exchange(): lax.all_to_all(x, ('seq', 'chan'), 0, 0, axis_index_groups=PAIRS, tiled=T...  50.2 us
    ppermute x6, starting transfers between devices, swap(): return lax.ppermute(x, 'chan', [(z, z ^ distance) for z in range(8)])  11.5 us
    pallas_call x2, Pallas kernels, spectra(): call(functools.partial(spectra_kernel, channels=channels), (shape(count,...  2.91 us
    pallas_call x1, Pallas kernels, body(): call(conv_three_kernel, buffer, 'three', cost=(1000, 1000))  2.2 us
    pallas_call x1, Pallas kernels, body(): call(prep_kernel, buffer, 'prep', [gate, gate, gate, gate, pltpu.VMEM((64...  1.6 us
  transfers between devices with their start and end apart: 6, of which 1 were waited for; matrix products, arithmetic and copies ran while one was open for 0% of the time, Pallas kernels for 9%

profile of v7, /device:TPU:1, one launch (start us, length us, event | category | flops | bytes accessed | tf_op | source)
XLA Modules:
  0.0 72.1 jit_solution(10144134698192945851)
XLA Ops:
  0.6 1.6 %prep.1 = f32[2176,128]{1,0:T(8,128)S(1)} custom-call(bf16[256,512]{1,0:T(8,128)(2,1)} %outer_hbm.1, bf16[256,512]{1,0:T(8,128)(2,1)} %inner_ref.1, bf16[256,512]{1,0:T(8,128)(2,1)} %signal_ref.1, bf16[256,512]{1,0:T(8,128)(2,1)} %cot_ref.1, f32[64,256]{1,0:T(8,128)} %bitcast.12), custom_call_target="tpu_custom_call" | custom-call | flops 1000 | bytes 1000 | tf_op jit(solution)/shard_map/prep/pallas_call | solution.py:295
  2.2 0.0 copy-start
  2.2 0.0 copy-start.1
  2.3 0.0 copy-start.2
  2.3 0.0 copy-start.3
  2.3 0.0 copy-start.4
  2.3 25.3 %all_to_all.18 = f32[64,1,4352]{2,1,0:T(1,128)S(1)} all-to-all(f32[64,1,4352]{2,1,0:T(1,128)S(1)} %bitcast.10), channel_id=1, replica_groups={{160,56,40,16,24,168,104,224,96,8,152,112,144,48,88,184,192,240,176,80,..., dimensions={0} | all-to-all | bytes 2228224 | tf_op jit(solution)/shard_map/all_to_all | solution.py:282
  27.6 0.0 copy-done.3
  27.6 0.0 copy-done.4
  27.6 3.1 %collective-permute-start = (f32[2,64,128]{2,1,0:T(8,128)S(1)}, f32[2,64,128]{2,1,0:T(8,128)S(1)}, u32[]{:S(2)}, u32[]{:S(2)}) collective-permute-start(f32[2,64,128]{2,1,0:T(8,128)S(1)} %pick.1.own_ref), channel_id=1, source_target_pairs={{0,2},{1,3},{2,0},{3,1},{4,6},{5,7},{6,4},{7,5},{8,10},{9,11},{10,... | collective-permute-start | bytes 196616 | tf_op jit(solution)/shard_map/ppermute | solution.py:287
  30.7 0.9 %spectra.2 = (f32[2,128,256]{2,1,0:T(8,128)S(1)}, f32[2,128,256]{2,1,0:T(8,128)S(1)}, f32[2,64,128]{2,1,0:T(8,128)S(1)}) custom-call(f32[2176,128]{1,0:T(8,128)S(1)} %bitcast.7, bf16[128,192]{1,0:T(8,128)(2,1)S(1)} %copy-done.3, bf16[256,256]{1,0:T(8,128)(2,1)S(1)} %copy-done.1, bf16[256,256]{1,0:T(8,128)(2,1)S(1)} %copy-done, f32[2,64,128]{2,1,0:T(8,128)S(1)} %copy-done.2, ...), custom_call_target="tpu_custom_call" | custom-call | flops 1000 | bytes 1000 | tf_op jit(solution)/shard_map/spectra/pallas_call | solution.py:310
  31.6 3.4 %collective-permute-start.2 = (f32[2,64,128]{2,1,0:T(8,128)S(1)}, f32[2,64,128]{2,1,0:T(8,128)S(1)}, u32[]{:S(2)}, u32[]{:S(2)}) collective-permute-start(f32[2,64,128]{2,1,0:T(8,128)S(1)} %get-tuple-element.24), channel_id=1, source_target_pairs={{0,6},{1,7},{2,4},{3,5},{4,2},{5,3},{6,0},{7,1},{8,14},{9,15},{10,... | collective-permute-start | bytes 196616 | tf_op jit(solution)/shard_map/ppermute | solution.py:287
  35.0 0.3 collective-permute-start.5
  35.3 2.0 %spectra.3 = (f32[6,128,256]{2,1,0:T(8,128)S(1)}, f32[6,128,256]{2,1,0:T(8,128)S(1)}, f32[2,64,128]{2,1,0:T(8,128)S(1)}, f32[4,64,128]{2,1,0:T(8,128)S(1)}) custom-call(f32[2176,128]{1,0:T(8,128)S(1)} %bitcast.8, bf16[128,192]{1,0:T(8,128)(2,1)S(1)} %copy-done.3, bf16[256,256]{1,0:T(8,128)(2,1)S(1)} %copy-done.1, bf16[256,256]{1,0:T(8,128)(2,1)S(1)} %copy-done, ...), custom_call_target="tpu_custom_call" | custom-call | flops 1000 | bytes 1000 | tf_op jit(solution)/shard_map/spectra/pallas_call | solution.py:310
  37.3 0.0 collective-permute-done.fb_ref
  37.3 3.4 %collective-permute-start.4 = (f32[2,64,128]{2,1,0:T(8,128)S(1)}, f32[2,64,128]{2,1,0:T(8,128)S(1)}, u32[]{:S(2)}, u32[]{:S(2)}) collective-permute-start(f32[2,64,128]{2,1,0:T(8,128)S(1)} %collective-permute-done.fb_ref), channel_id=1, source_target_pairs={{0,6},{1,7},{2,4},{3,5},{4,2},{5,3},{6,0},{7,1},{8,14},{9,15},{10,... | collective-permute-start | bytes 196616 | tf_op jit(solution)/shard_map/ppermute | solution.py:287
  40.7 0.3 collective-permute-start.1
  41.0 0.0 collective-permute-done.2.came_ref
  41.0 1.1 %collective-permute-start.3 = (f32[2,64,128]{2,1,0:T(8,128)S(1)}, f32[2,64,128]{2,1,0:T(8,128)S(1)}, u32[]{:S(2)}, u32[]{:S(2)}) collective-permute-start(f32[2,64,128]{2,1,0:T(8,128)S(1)} %mix.1), channel_id=1, source_target_pairs={{0,2},{1,3},{2,0},{3,1},{4,6},{5,7},{6,4},{7,5},{8,10},{9,11},{10,... | collective-permute-start | bytes 196616 | tf_op jit(solution)/shard_map/ppermute | solution.py:287
  42.1 0.0 collective-permute-done.5.fa_ref
  42.1 2.2 %three.1.base_ref = f32[2176,128]{1,0:T(8,128)S(1)} custom-call(f32[2,64,128]{2,1,0:T(8,128)S(1)} %pick.1.own_ref, f32[2,64,128]{2,1,0:T(8,128)S(1)} %collective-permute-done.fb_ref, f32[2,64,128]{2,1,0:T(8,128)S(1)} %collective-permute-done.5.fa_ref, f32[6,128,256]{2,1,0:T(8,128)S(1)} %get-tuple-element.26.u_ref, ...), custom_call_target="tpu_custom_call" | custom-call | flops 1000 | bytes 1000 | tf_op jit(solution)/shard_map/three/pallas_call | solution.py:326
  44.3 0.0 collective-permute-done.4.far_ref
  44.3 1.1 %last.1.base_ref = f32[2176,128]{1,0:T(8,128)S(1)} custom-call(f32[2,64,128]{2,1,0:T(8,128)S(1)} %collective-permute-done.4.far_ref, f32[2176,128]{1,0:T(8,128)S(1)} %three.1.base_ref, f32[2,128,256]{2,1,0:T(8,128)S(1)} %get-tuple-element.28.u_ref, f32[2,128,256]{2,1,0:T(8,128)S(1)} %get-tuple-element.29.g_ref, bf16[128,192]{1,0:T(8,128)(2,1)S(1)} %copy-done.3, ...), custom_call_target="tpu_custom_call" | custom-call | flops 1000 | bytes 1000 | tf_op jit(solution)/shard_map/last/pallas_call | solution.py:330
  45.4 0.6 collective-permute-done.1.direct_ref
  46.0 0.0 collective-permute-done.3.came_ref
  46.0 0.1 place.1
  46.1 0.0 copy-start.5
  46.1 0.0 copy-start.6
  46.1 0.0 copy-start.7
  46.1 24.9 %all_to_all.19 = f32[64,1,4352]{2,1,0:T(1,128)S(1)} all-to-all(f32[64,1,4352]{2,1,0:T(1,128)S(1)} %bitcast.9), channel_id=1, replica_groups={{160,56,40,16,24,168,104,224,96,8,152,112,144,48,88,184,192,240,176,80,..., dimensions={0} | all-to-all | bytes 2228224 | tf_op jit(solution)/shard_map/all_to_all | solution.py:282
  71.0 0.0 copy-done.5
  71.0 1.1 %post.1 = (bf16[256,512]{1,0:T(8,128)(2,1)}, bf16[256,512]{1,0:T(8,128)(2,1)}, bf16[256,512]{1,0:T(8,128)(2,1)}, f32[64,256]{1,0:T(8,128)}) custom-call(f32[2176,128]{1,0:T(8,128)S(1)} %bitcast.11, bf16[256,512]{1,0:T(8,128)(2,1)S(1)} %copy-done.5, bf16[256,512]{1,0:T(8,128)(2,1)S(1)} %copy-done.6, bf16[256,512]{1,0:T(8,128)(2,1)S(1)} %copy-done.7), custom_call_target="tpu_custom_call" | custom-call | flops 1000 | bytes 1000 | tf_op jit(solution)/shard_map/post/pallas_call | solution.py:333
  (7 shorter events, 0.0 us)
Async XLA Ops:
  2.2 25.3 %copy-start = (bf16[256,256]{1,0:T(8,128)(2,1)S(1)}, bf16[256,256]{1,0:T(8,128)(2,1)}, u32[]{:S(2)}) copy-start(bf16[256,256]{1,0:T(8,128)(2,1)} %constant.12.clone.w2l_ref) | copy-start | bytes 393220
  2.2 25.3 %copy-start.1 = (bf16[256,256]{1,0:T(8,128)(2,1)S(1)}, bf16[256,256]{1,0:T(8,128)(2,1)}, u32[]{:S(2)}) copy-start(bf16[256,256]{1,0:T(8,128)(2,1)} %constant.11.clone.w2h_ref) | copy-start | bytes 393220
  2.3 25.3 %copy-start.2 = (f32[2,64,128]{2,1,0:T(8,128)S(1)}, f32[2,64,128]{2,1,0:T(8,128)}, u32[]{:S(2)}) copy-start(f32[2,64,128]{2,1,0:T(8,128)} %constant.13.clone.tw_ref) | copy-start | bytes 196612
  2.3 25.3 %copy-start.3 = (bf16[128,192]{1,0:T(8,128)(2,1)S(1)}, bf16[128,192]{1,0:T(8,128)(2,1)}, u32[]{:S(2)}) copy-start(bf16[128,192]{1,0:T(8,128)(2,1)} %constant.10.clone.w1_ref) | copy-start | bytes 147460
  2.3 25.3 %copy-start.4 = (bf16[64,384]{1,0:T(8,128)(2,1)S(1)}, bf16[64,384]{1,0:T(8,128)(2,1)}, u32[]{:S(2)}) copy-start(bf16[64,384]{1,0:T(8,128)(2,1)} %constant.14.clone.v1_ref) | copy-start | bytes 147460
  27.6 9.7 %collective-permute-start = (f32[2,64,128]{2,1,0:T(8,128)S(1)}, f32[2,64,128]{2,1,0:T(8,128)S(1)}, u32[]{:S(2)}, u32[]{:S(2)}) collective-permute-start(f32[2,64,128]{2,1,0:T(8,128)S(1)} %pick.1.own_ref), channel_id=1, source_target_pairs={{0,2},{1,3},{2,0},{3,1},{4,6},{5,7},{6,4},{7,5},{8,10},{9,11},{10,... | collective-permute-start | bytes 196616 | tf_op jit(solution)/shard_map/ppermute | solution.py:287
  31.6 9.4 %collective-permute-start.2 = (f32[2,64,128]{2,1,0:T(8,128)S(1)}, f32[2,64,128]{2,1,0:T(8,128)S(1)}, u32[]{:S(2)}, u32[]{:S(2)}) collective-permute-start(f32[2,64,128]{2,1,0:T(8,128)S(1)} %get-tuple-element.24), channel_id=1, source_target_pairs={{0,6},{1,7},{2,4},{3,5},{4,2},{5,3},{6,0},{7,1},{8,14},{9,15},{10,... | collective-permute-start | bytes 196616 | tf_op jit(solution)/shard_map/ppermute | solution.py:287
  35.0 7.1 %collective-permute-start.5 = (f32[2,64,128]{2,1,0:T(8,128)S(1)}, f32[2,64,128]{2,1,0:T(8,128)S(1)}, u32[]{:S(2)}, u32[]{:S(2)}) collective-permute-start(f32[2,64,128]{2,1,0:T(8,128)S(1)} %pick.1.own_ref), channel_id=1, source_target_pairs={{0,6},{1,7},{2,4},{3,5},{4,2},{5,3},{6,0},{7,1},{8,14},{9,15},{10,... | collective-permute-start | bytes 196616 | tf_op jit(solution)/shard_map/ppermute | solution.py:287
  37.3 7.0 %collective-permute-start.4 = (f32[2,64,128]{2,1,0:T(8,128)S(1)}, f32[2,64,128]{2,1,0:T(8,128)S(1)}, u32[]{:S(2)}, u32[]{:S(2)}) collective-permute-start(f32[2,64,128]{2,1,0:T(8,128)S(1)} %collective-permute-done.fb_ref), channel_id=1, source_target_pairs={{0,6},{1,7},{2,4},{3,5},{4,2},{5,3},{6,0},{7,1},{8,14},{9,15},{10,... | collective-permute-start | bytes 196616 | tf_op jit(solution)/shard_map/ppermute | solution.py:287
  40.7 5.3 %collective-permute-start.1 = (f32[2,64,128]{2,1,0:T(8,128)S(1)}, f32[2,64,128]{2,1,0:T(8,128)S(1)}, u32[]{:S(2)}, u32[]{:S(2)}) collective-permute-start(f32[2,64,128]{2,1,0:T(8,128)S(1)} %get-tuple-element.23), channel_id=1, source_target_pairs={{0,6},{1,7},{2,4},{3,5},{4,2},{5,3},{6,0},{7,1},{8,14},{9,15},{10,... | collective-permute-start | bytes 196616 | tf_op jit(solution)/shard_map/ppermute | solution.py:287
  41.0 5.0 %collective-permute-start.3 = (f32[2,64,128]{2,1,0:T(8,128)S(1)}, f32[2,64,128]{2,1,0:T(8,128)S(1)}, u32[]{:S(2)}, u32[]{:S(2)}) collective-permute-start(f32[2,64,128]{2,1,0:T(8,128)S(1)} %mix.1), channel_id=1, source_target_pairs={{0,2},{1,3},{2,0},{3,1},{4,6},{5,7},{6,4},{7,5},{8,10},{9,11},{10,... | collective-permute-start | bytes 196616 | tf_op jit(solution)/shard_map/ppermute | solution.py:287
  46.1 24.9 %copy-start.5 = (bf16[256,512]{1,0:T(8,128)(2,1)S(1)}, bf16[256,512]{1,0:T(8,128)(2,1)}, u32[]{:S(2)}) copy-start(bf16[256,512]{1,0:T(8,128)(2,1)} %inner_ref.1) | copy-start | bytes 786436
  46.1 24.9 %copy-start.6 = (bf16[256,512]{1,0:T(8,128)(2,1)S(1)}, bf16[256,512]{1,0:T(8,128)(2,1)}, u32[]{:S(2)}) copy-start(bf16[256,512]{1,0:T(8,128)(2,1)} %signal_ref.1) | copy-start | bytes 786436
  46.1 24.9 %copy-start.7 = (bf16[256,512]{1,0:T(8,128)(2,1)S(1)}, bf16[256,512]{1,0:T(8,128)(2,1)}, u32[]{:S(2)}) copy-start(bf16[256,512]{1,0:T(8,128)(2,1)} %cot_ref.1) | copy-start | bytes 786436
